TPU v7x, 128 devices: a whole 4x4x4 slice. The times are simulated.
128 devices in a mesh: gx: 8 (over x, core), gy: 16 (over z, y).
Axes of the slice: x: 4, y: 4, z: 4, core: 2. Of those that a mesh axis runs over, the one named last changes fastest.
Arguments:
- fine_atmospheric_values: float32 [4, 1536, 1536], P(None, 'gx', 'gy'), may hold values from -6 to 6
- fine_skin_heat: float32 [1536, 1536], P('gx', 'gy'), may hold values from -6 to 6
- coarse_lowest_values: bfloat16 [4, 3072, 6144], P(None, 'gx', 'gy'), may hold values from -6 to 6
- holder_flat: int32 [1], replicated, may hold values from 0 to 127
- corner_offset: int32 [2], replicated, may hold values from 0 to 146
- exchange_patch_holder: int32 [18432, 1], P(('gx', 'gy')), may hold values from 0 to 127; in each aligned block of 144 rows (0 to 143, 144 to 287, ...) at most 3 rows name the same one
- holder_patch_position: int32 [18432], P(('gx', 'gy')), may hold values from 0 to 31
- coarse_interface_exchange: float32 [4, 524288], P(None, ('gx', 'gy')), may hold values from -6 to 6
- marine_stratum_values: float32 [4, 41, 524288], P(None, None, ('gx', 'gy')), may hold values from -6 to 6
- diffusion_solver_operator: float32 [41, 41], replicated, may hold values from -0.3 to 1
Outputs:
- nest_next: float32 [4, 1536, 1536], P(None, 'gx', 'gy')
- refreshed_marine_values: float32 [4, 41, 524288], P(None, None, ('gx', 'gy'))
- fine_refreshed_skin_heat: float32 [1536, 1536], P('gx', 'gy')
Inputs may be any that keep to these rules, and one draw needn't show every extreme that they name: `holder_flat`: index of the tile that holds the storm. `corner_offset`: the nest lies inside the owner tile. `exchange_patch_holder`: within the blocks of one device, no ocean owner is named more than 3 times.
All inputs are finite; a program needn't handle non-finite values.
Results may differ from a plain program's by a relative error of at most 0.0019.
Values may be sent and summed in bfloat16 or wider, within the bound.
No kernel may reach another device: no remote copies, remote signals or barrier semaphores. Data moves between devices by JAX's collectives and lax.ppermute only.
A program may use at most 64 MiB of HBM per device.

v0:
```python
import jax
import jax.numpy as jnp
from jax import lax
from jax.sharding import PartitionSpec as P

FIELDS = 4
EXCHANGE_PATCH = 128
MARINE_PATCHES = 32
STEPS = 4


diffuse_coef = 0.24
relax_coef = 0.3
drag_coefficient = 0.5


def spread(value, axis, root):
    mine = lax.axis_index(axis) == root
    return lax.psum(jnp.where(mine, value, jnp.zeros_like(value)), axis)


def extended(value, sides, width):
    for axis, dim in sides:
        devices, length = (lax.axis_size(axis), value.shape[dim])
        up = [(i, (i + 1) % devices) for i in range(devices - 1)]
        down = [(j, i) for i, j in up]
        last = lax.slice_in_dim(value, length - width, length, axis=dim)
        initial = lax.slice_in_dim(value, 0, width, axis=dim)
        before = lax.ppermute(last, axis, up)
        after = lax.ppermute(initial, axis, down)
        value = jnp.concatenate([before, value, after], axis=dim)
    return value


def hat_weights(cell_count, first_cell, anchor_cell, parent_cells):
    fine_cells = (jnp.arange(cell_count) + first_cell).astype(jnp.float32)
    centre = (fine_cells + 0.5) * (2.0 / 13.0) - 0.5 + anchor_cell.astype(jnp.float32)
    coarse = jnp.arange(parent_cells).astype(jnp.float32)
    return jnp.maximum(0.0, 1.0 - jnp.abs(centre[:, None] - coarse[None, :])).astype(jnp.bfloat16)


def interpolate(parent_part, corner_offset, first_x, count_x, first_y, count_y):
    weight_x = hat_weights(count_x, first_x, corner_offset[0], parent_part.shape[1])
    weight_y = hat_weights(count_y, first_y, corner_offset[1], parent_part.shape[2])
    partial_value = jnp.einsum(
        "fpq,jq->fpj", parent_part, weight_y, preferred_element_type=jnp.float32
    ).astype(jnp.bfloat16)
    return jnp.einsum("ip,fpj->fij", weight_x, partial_value, preferred_element_type=jnp.float32)


def on_device(
    fine_atmospheric_values,
    fine_skin_heat,
    coarse_lowest_values,
    holder_flat,
    corner_offset,
    exchange_patch_holder,
    holder_patch_position,
    coarse_interface_exchange,
    marine_stratum_values,
    diffusion_solver_operator,
):
    size_x = lax.axis_size("gx")
    size_y = lax.axis_size("gy")
    devices = size_x * size_y
    index_x = lax.axis_index("gx")
    index_y = lax.axis_index("gy")
    tile_column_index = fine_atmospheric_values.shape[1]
    tile_row_index = fine_atmospheric_values.shape[2]
    received = spread(coarse_lowest_values, ("gx", "gy"), holder_flat[0])
    start_x = index_x * tile_column_index
    start_y = index_y * tile_row_index
    forcing = interpolate(
        received, corner_offset, start_x, tile_column_index, start_y, tile_row_index
    )
    present_fine_values = fine_atmospheric_values
    for iteration in range(STEPS):
        padded = extended(present_fine_values, (("gx", 1), ("gy", 2)), 1)
        beside = (
            padded[:, 2:, 1:-1] + padded[:, :-2, 1:-1] + padded[:, 1:-1, 2:] + padded[:, 1:-1, :-2]
        )
        present_fine_values = (
            present_fine_values
            + diffuse_coef * (beside - 4.0 * present_fine_values)
            + relax_coef * (forcing - present_fine_values)
        )
    breeze_speed = jnp.sqrt(
        1.0
        + present_fine_values[0] * present_fine_values[0]
        + present_fine_values[1] * present_fine_values[1]
    )
    interface_exchange = jnp.stack(
        [
            drag_coefficient * breeze_speed * (present_fine_values[2] - fine_skin_heat),
            drag_coefficient * breeze_speed * (present_fine_values[3] - 0.5 * fine_skin_heat),
            drag_coefficient * breeze_speed * present_fine_values[0],
            drag_coefficient * breeze_speed * present_fine_values[1],
        ]
    )
    block_count = tile_column_index * tile_row_index // EXCHANGE_PATCH
    capacity = max(2, (2 * block_count + devices - 1) // devices)
    owner_list = exchange_patch_holder[:, 0]
    owners_hot = (owner_list[:, None] == jnp.arange(devices, dtype=jnp.int32)[None, :]).astype(
        jnp.int32
    )
    earlier = jnp.cumsum(owners_hot, axis=0) - owners_hot
    ranking = jnp.sum(earlier * owners_hot, axis=1)
    fine_grid_position = owner_list * capacity + ranking
    flux_rows = interface_exchange.reshape(FIELDS, block_count, EXCHANGE_PATCH)
    send_flux = (
        jnp.zeros((FIELDS, devices * capacity, EXCHANGE_PATCH), jnp.float32)
        .at[:, fine_grid_position]
        .set(flux_rows)
    )
    send_slot = (
        jnp.full((devices * capacity,), -1, jnp.int32)
        .at[fine_grid_position]
        .set(holder_patch_position)
    )
    got_flux, got_slot = (
        lax.all_to_all(
            send_flux.reshape(FIELDS, devices, capacity * EXCHANGE_PATCH),
            ("gx", "gy"),
            split_axis=1,
            concat_axis=1,
            tiled=True,
        ),
        lax.all_to_all(
            send_slot.reshape(1, devices, capacity),
            ("gx", "gy"),
            split_axis=1,
            concat_axis=1,
            tiled=True,
        ),
    )
    got_flux = got_flux.reshape(FIELDS, devices * capacity, EXCHANGE_PATCH)
    got_slot = got_slot.reshape(devices * capacity)
    patch_selector_hot = (
        got_slot[:, None] == jnp.arange(MARINE_PATCHES, dtype=jnp.int32)[None, :]
    ).astype(jnp.float32)
    block_sums = jnp.einsum(
        "ro,frc->foc", patch_selector_hot, got_flux, precision=lax.Precision.HIGHEST
    )
    counts = jnp.sum(patch_selector_hot, axis=0)
    coarse = coarse_interface_exchange.reshape(FIELDS, MARINE_PATCHES, EXCHANGE_PATCH)
    uncovered = (counts == 0.0).astype(jnp.float32)
    forcing_ocean = (block_sums + coarse * uncovered[None, :, None]) / jnp.maximum(counts, 1.0)[
        None, :, None
    ]
    forced = marine_stratum_values.at[:, 0, :].set(
        marine_stratum_values[:, 0, :]
        + forcing_ocean.reshape(FIELDS, MARINE_PATCHES * EXCHANGE_PATCH)
    )
    refreshed_marine_values = jnp.einsum(
        "lk,fkc->flc", diffusion_solver_operator, forced, precision=lax.Precision.HIGHEST
    )
    skin_heat_gather = refreshed_marine_values[0, 0].reshape(MARINE_PATCHES, EXCHANGE_PATCH)
    returned_patches = jnp.dot(
        patch_selector_hot, skin_heat_gather, precision=lax.Precision.HIGHEST
    )
    arrived_patches = lax.all_to_all(
        returned_patches.reshape(devices, capacity * EXCHANGE_PATCH),
        ("gx", "gy"),
        split_axis=0,
        concat_axis=0,
        tiled=True,
    )
    arrived_patches = arrived_patches.reshape(devices * capacity, EXCHANGE_PATCH)
    fine_refreshed_skin_heat = arrived_patches[fine_grid_position].reshape(
        tile_column_index, tile_row_index
    )
    return (present_fine_values, refreshed_marine_values, fine_refreshed_skin_heat)


def solution(mesh):
    in_specs = (
        P(None, "gx", "gy"),
        P("gx", "gy"),
        P(None, "gx", "gy"),
        P(),
        P(),
        P(("gx", "gy"), None),
        P(("gx", "gy")),
        P(None, ("gx", "gy")),
        P(None, None, ("gx", "gy")),
        P(),
    )
    out_specs = (P(None, "gx", "gy"), P(None, None, ("gx", "gy")), P("gx", "gy"))
    return jax.shard_map(
        on_device, mesh=mesh, in_specs=in_specs, out_specs=out_specs, check_vma=False
    )
```

profile of v0, /device:TPU:1, one launch (start us, length us, event | category | flops | bytes accessed | tf_op | source)
XLA Modules:
  0.0 304.0 jit_solution(16181235761219582611)
XLA Ops:
  8.3 3.3 %collective-permute-start = (f32[4,1,96]{1,2,0:T(8,128)S(1)}, f32[4,1,96]{1,2,0:T(8,128)S(1)}, u32[]{:S(2)}, u32[]{:S(2)}) collective-permute-start(f32[4,1,96]{1,2,0:T(8,128)S(1)} %copy.47), channel_id=1, source_target_pairs={{16,0},{32,16},{48,32},{64,48},{80,64},{96,80},{112,96},{17,1},{33... | collective-permute-start | bytes 4616 | tf_op jit(solution)/shard_map/ppermute | solution.py:30
  11.8 3.1 %collective-permute-start.1 = (f32[4,1,96]{1,2,0:T(8,128)S(1)}, f32[4,1,96]{1,2,0:T(8,128)S(1)}, u32[]{:S(2)}, u32[]{:S(2)}) collective-permute-start(f32[4,1,96]{1,2,0:T(8,128)S(1)} %copy.49), channel_id=1, source_target_pairs={{0,16},{16,32},{32,48},{48,64},{64,80},{80,96},{96,112},{1,17},{17... | collective-permute-start | bytes 4616 | tf_op jit(solution)/shard_map/ppermute | solution.py:29
  20.4 4.0 %collective-permute-start.3 = (f32[4,194,1]{1,2,0:T(1,128)S(1)}, f32[4,194,1]{1,2,0:T(1,128)S(1)}, u32[]{:S(2)}, u32[]{:S(2)}) collective-permute-start(f32[4,194,1]{1,2,0:T(1,128)S(1)} %get-tuple-element.33), channel_id=1, source_target_pairs={{0,1},{1,2},{2,3},{3,4},{4,5},{5,6},{6,7},{7,8},{8,9},{9,10},{10,1... | collective-permute-start | bytes 9320 | tf_op jit(solution)/shard_map/ppermute | solution.py:29
  25.1 141.2 %all-reduce.3.cloned.1.call-done = bf16[4,384,384]{2,1,0:T(8,128)(2,1)} async-done(((bf16[4,384,384]{2,1,0:T(8,128)(2,1)}), bf16[4,384,384]{2,1,0:T(8,128)(2,1)}) %all-reduce.3.cloned.1.call-update) | async-done | bytes 1179664 | tf_op jit(solution)/shard_map/psum | solution.py:19
  166.3 2.1 fusion.28
  168.5 2.8 collective-permute-start.4
  171.3 2.7 collective-permute-start.5
  178.0 4.0 %collective-permute-start.7 = (f32[4,194,1]{1,2,0:T(1,128)S(1)}, f32[4,194,1]{1,2,0:T(1,128)S(1)}, u32[]{:S(2)}, u32[]{:S(2)}) collective-permute-start(f32[4,194,1]{1,2,0:T(1,128)S(1)} %get-tuple-element.31), channel_id=1, source_target_pairs={{0,1},{1,2},{2,3},{3,4},{4,5},{5,6},{6,7},{7,8},{8,9},{9,10},{10,1... | collective-permute-start | bytes 9320 | tf_op jit(solution)/shard_map/ppermute | solution.py:29
  183.5 1.9 collective-permute-start.8
  185.4 5.5 %collective-permute-start.9 = (f32[4,1,96]{1,2,0:T(8,128)S(1)}, f32[4,1,96]{1,2,0:T(8,128)S(1)}, u32[]{:S(2)}, u32[]{:S(2)}) collective-permute-start(f32[4,1,96]{1,2,0:T(8,128)S(1)} %get-tuple-element.38), channel_id=1, source_target_pairs={{0,16},{16,32},{32,48},{48,64},{64,80},{80,96},{96,112},{1,17},{17... | collective-permute-start | bytes 4616 | tf_op jit(solution)/shard_map/ppermute | solution.py:29
  194.9 4.5 %collective-permute-start.11 = (f32[4,194,1]{1,2,0:T(1,128)S(1)}, f32[4,194,1]{1,2,0:T(1,128)S(1)}, u32[]{:S(2)}, u32[]{:S(2)}) collective-permute-start(f32[4,194,1]{1,2,0:T(1,128)S(1)} %get-tuple-element.29), channel_id=1, source_target_pairs={{0,1},{1,2},{2,3},{3,4},{4,5},{5,6},{6,7},{7,8},{8,9},{9,10},{10,1... | collective-permute-start | bytes 9320 | tf_op jit(solution)/shard_map/ppermute | solution.py:29
  202.8 5.2 %collective-permute-start.13 = (f32[4,1,96]{1,2,0:T(8,128)S(1)}, f32[4,1,96]{1,2,0:T(8,128)S(1)}, u32[]{:S(2)}, u32[]{:S(2)}) collective-permute-start(f32[4,1,96]{1,2,0:T(8,128)S(1)} %get-tuple-element.36), channel_id=1, source_target_pairs={{0,16},{16,32},{32,48},{48,64},{64,80},{80,96},{96,112},{1,17},{17... | collective-permute-start | bytes 4616 | tf_op jit(solution)/shard_map/ppermute | solution.py:29
  212.0 4.5 %collective-permute-start.15 = (f32[4,194,1]{1,2,0:T(1,128)S(1)}, f32[4,194,1]{1,2,0:T(1,128)S(1)}, u32[]{:S(2)}, u32[]{:S(2)}) collective-permute-start(f32[4,194,1]{1,2,0:T(1,128)S(1)} %get-tuple-element.27), channel_id=1, source_target_pairs={{0,1},{1,2},{2,3},{3,4},{4,5},{5,6},{6,7},{7,8},{8,9},{9,10},{10,1... | collective-permute-start | bytes 9320 | tf_op jit(solution)/shard_map/ppermute | solution.py:29
  218.6 14.0 %all-to-all-start.1 = ((s32[1,128,3]{2,0,1:T(1,128)}), s32[1,128,3]{2,0,1:T(1,128)S(1)}, u32[]{:S(2)}, u32[]{:S(2)}) async-start(s32[1,128,3]{2,0,1:T(1,128)} %bitcast.18), calls=%async_computation.1 | async-start | bytes 131072 | tf_op jit(solution)/shard_map/all_to_all | solution.py:128
  234.5 4.8 %scatter_fusion = f32[4,384,128]{2,0,1:T(4,128)S(1)} fusion(f32[4,384,128]{2,0,1:T(4,128)S(1)} %broadcast_in_dim.7, s32[144]{0:T(256)S(1)} %bitcast.86, f32[144,4,128]{2,1,0:T(4,128)S(1)} %copy.63), kind=kCustom, calls=%fused_computation.1 | custom fusion | bytes 885312 | tf_op jit(solution)/shard_map/scatter | solution.py:113
  239.3 3.0 all-to-all-done.1
  242.3 8.1 %all-to-all-start = ((f32[4,128,384]{2,0,1:T(4,128)}), f32[4,128,384]{2,0,1:T(4,128)}, u32[]{:S(2)}, u32[]{:S(2)}) async-start(f32[4,128,384]{2,0,1:T(4,128)} %bitcast.74), calls=%async_computation | async-start | bytes 1572864 | tf_op jit(solution)/shard_map/all_to_all | solution.py:121
  252.1 14.7 %all-to-all-done = f32[4,128,384]{2,0,1:T(4,128)} async-done(((f32[4,128,384]{2,0,1:T(4,128)}), f32[4,128,384]{2,0,1:T(4,128)}, u32[]{:S(2)}, u32[]{:S(2)}) %all-to-all-start) | async-done | bytes 786464 | tf_op jit(solution)/shard_map/all_to_all | solution.py:121
  266.8 2.1 copy.66
  268.8 2.1 reshape.124
  272.5 5.5 %convolution_bitcast_fusion = f32[4,41,4096]{2,1,0:T(8,128)S(1)} fusion(f32[4,41,4096]{2,0,1:T(4,128)S(1)} %add_dynamic-update-slice_fusion, f32[41,41]{1,0:T(8,128)S(1)} %copy-done), kind=kOutput, calls=%fused_computation.3 | convolution fusion | flops 330498048 | bytes 5380676 | tf_op jit(solution)/shard_map/lk,fkc->flc/dot_general | solution.py:154
  280.7 4.1 %all-to-all-start.2 = ((f32[128,1,384]{2,1,0:T(1,128)}), f32[128,1,384]{2,1,0:T(1,128)S(1)}, u32[]{:S(2)}, u32[]{:S(2)}) async-start(f32[128,1,384]{2,1,0:T(1,128)} %bitcast.24), calls=%async_computation.2 | async-start | bytes 393216 | tf_op jit(solution)/shard_map/all_to_all | solution.py:161
  285.7 5.1 %copy.71 = f32[4,41,4096]{2,0,1:T(4,128)} copy(f32[4,41,4096]{2,1,0:T(8,128)} %copy-done.2) | data formatting | bytes 5373952
  290.9 4.8 %all-to-all-done.2 = f32[128,1,384]{2,1,0:T(1,128)S(1)} async-done(((f32[128,1,384]{2,1,0:T(1,128)}), f32[128,1,384]{2,1,0:T(1,128)S(1)}, u32[]{:S(2)}, u32[]{:S(2)}) %all-to-all-start.2) | async-done | bytes 196640 | tf_op jit(solution)/shard_map/all_to_all | solution.py:161
  (105 shorter events, 34.2 us)
Async XLA Ops:
  7.2 265.3 %copy-start = (f32[41,41]{1,0:T(8,128)S(1)}, f32[41,41]{1,0:T(8,128)}, u32[]{:S(2)}) copy-start(f32[41,41]{1,0:T(8,128)} %param.21) | copy-start | bytes 20176
  7.2 159.1 %all-reduce.3.cloned.1.call-start = ((), (), s32[]{:S(2)}) async-start(), calls=%async_computation.3 | async-start | bytes 2359296 | tf_op jit(solution)/shard_map/psum | solution.py:19
  8.3 10.6 %collective-permute-start = (f32[4,1,96]{1,2,0:T(8,128)S(1)}, f32[4,1,96]{1,2,0:T(8,128)S(1)}, u32[]{:S(2)}, u32[]{:S(2)}) collective-permute-start(f32[4,1,96]{1,2,0:T(8,128)S(1)} %copy.47), channel_id=1, source_target_pairs={{16,0},{32,16},{48,32},{64,48},{80,64},{96,80},{112,96},{17,1},{33... | collective-permute-start | bytes 4616 | tf_op jit(solution)/shard_map/ppermute | solution.py:30
  11.8 7.2 %collective-permute-start.1 = (f32[4,1,96]{1,2,0:T(8,128)S(1)}, f32[4,1,96]{1,2,0:T(8,128)S(1)}, u32[]{:S(2)}, u32[]{:S(2)}) collective-permute-start(f32[4,1,96]{1,2,0:T(8,128)S(1)} %copy.49), channel_id=1, source_target_pairs={{0,16},{16,32},{32,48},{48,64},{64,80},{80,96},{96,112},{1,17},{17... | collective-permute-start | bytes 4616 | tf_op jit(solution)/shard_map/ppermute | solution.py:29
  19.1 5.3 %collective-permute-start.2 = (f32[4,194,1]{1,2,0:T(1,128)S(1)}, f32[4,194,1]{1,2,0:T(1,128)S(1)}, u32[]{:S(2)}, u32[]{:S(2)}) collective-permute-start(f32[4,194,1]{1,2,0:T(1,128)S(1)} %get-tuple-element.32), channel_id=1, source_target_pairs={{1,0},{2,1},{3,2},{4,3},{5,4},{6,5},{7,6},{8,7},{9,8},{10,9},{11,1... | collective-permute-start | bytes 9320 | tf_op jit(solution)/shard_map/ppermute | solution.py:30
  20.4 4.7 %collective-permute-start.3 = (f32[4,194,1]{1,2,0:T(1,128)S(1)}, f32[4,194,1]{1,2,0:T(1,128)S(1)}, u32[]{:S(2)}, u32[]{:S(2)}) collective-permute-start(f32[4,194,1]{1,2,0:T(1,128)S(1)} %get-tuple-element.33), channel_id=1, source_target_pairs={{0,1},{1,2},{2,3},{3,4},{4,5},{5,6},{6,7},{7,8},{8,9},{9,10},{10,1... | collective-permute-start | bytes 9320 | tf_op jit(solution)/shard_map/ppermute | solution.py:29
  168.5 7.0 %collective-permute-start.4 = (f32[4,1,96]{1,2,0:T(8,128)S(1)}, f32[4,1,96]{1,2,0:T(8,128)S(1)}, u32[]{:S(2)}, u32[]{:S(2)}) collective-permute-start(f32[4,1,96]{1,2,0:T(8,128)S(1)} %get-tuple-element.41), channel_id=1, source_target_pairs={{16,0},{32,16},{48,32},{64,48},{80,64},{96,80},{112,96},{17,1},{33... | collective-permute-start | bytes 4616 | tf_op jit(solution)/shard_map/ppermute | solution.py:30
  171.3 5.3 %collective-permute-start.5 = (f32[4,1,96]{1,2,0:T(8,128)S(1)}, f32[4,1,96]{1,2,0:T(8,128)S(1)}, u32[]{:S(2)}, u32[]{:S(2)}) collective-permute-start(f32[4,1,96]{1,2,0:T(8,128)S(1)} %get-tuple-element.40), channel_id=1, source_target_pairs={{0,16},{16,32},{32,48},{48,64},{64,80},{80,96},{96,112},{1,17},{17... | collective-permute-start | bytes 4616 | tf_op jit(solution)/shard_map/ppermute | solution.py:29
  176.7 5.4 %collective-permute-start.6 = (f32[4,194,1]{1,2,0:T(1,128)S(1)}, f32[4,194,1]{1,2,0:T(1,128)S(1)}, u32[]{:S(2)}, u32[]{:S(2)}) collective-permute-start(f32[4,194,1]{1,2,0:T(1,128)S(1)} %get-tuple-element.30), channel_id=1, source_target_pairs={{1,0},{2,1},{3,2},{4,3},{5,4},{6,5},{7,6},{8,7},{9,8},{10,9},{11,1... | collective-permute-start | bytes 9320 | tf_op jit(solution)/shard_map/ppermute | solution.py:30
  178.0 4.7 %collective-permute-start.7 = (f32[4,194,1]{1,2,0:T(1,128)S(1)}, f32[4,194,1]{1,2,0:T(1,128)S(1)}, u32[]{:S(2)}, u32[]{:S(2)}) collective-permute-start(f32[4,194,1]{1,2,0:T(1,128)S(1)} %get-tuple-element.31), channel_id=1, source_target_pairs={{0,1},{1,2},{2,3},{3,4},{4,5},{5,6},{6,7},{7,8},{8,9},{9,10},{10,1... | collective-permute-start | bytes 9320 | tf_op jit(solution)/shard_map/ppermute | solution.py:29
  183.3 49.3 %copy-start.6 = (f32[192,96]{1,0:T(8,128)S(1)}, f32[192,96]{1,0:T(8,128)}, u32[]{:S(2)}) copy-start(f32[192,96]{1,0:T(8,128)} %param.13) | copy-start | bytes 221188
  183.5 8.9 %collective-permute-start.8 = (f32[4,1,96]{1,2,0:T(8,128)S(1)}, f32[4,1,96]{1,2,0:T(8,128)S(1)}, u32[]{:S(2)}, u32[]{:S(2)}) collective-permute-start(f32[4,1,96]{1,2,0:T(8,128)S(1)} %get-tuple-element.39), channel_id=1, source_target_pairs={{16,0},{32,16},{48,32},{64,48},{80,64},{96,80},{112,96},{17,1},{33... | collective-permute-start | bytes 4616 | tf_op jit(solution)/shard_map/ppermute | solution.py:30
  185.4 8.1 %collective-permute-start.9 = (f32[4,1,96]{1,2,0:T(8,128)S(1)}, f32[4,1,96]{1,2,0:T(8,128)S(1)}, u32[]{:S(2)}, u32[]{:S(2)}) collective-permute-start(f32[4,1,96]{1,2,0:T(8,128)S(1)} %get-tuple-element.38), channel_id=1, source_target_pairs={{0,16},{16,32},{32,48},{48,64},{64,80},{80,96},{96,112},{1,17},{17... | collective-permute-start | bytes 4616 | tf_op jit(solution)/shard_map/ppermute | solution.py:29
  193.6 5.9 %collective-permute-start.10 = (f32[4,194,1]{1,2,0:T(1,128)S(1)}, f32[4,194,1]{1,2,0:T(1,128)S(1)}, u32[]{:S(2)}, u32[]{:S(2)}) collective-permute-start(f32[4,194,1]{1,2,0:T(1,128)S(1)} %get-tuple-element.28), channel_id=1, source_target_pairs={{1,0},{2,1},{3,2},{4,3},{5,4},{6,5},{7,6},{8,7},{9,8},{10,9},{11,1... | collective-permute-start | bytes 9320 | tf_op jit(solution)/shard_map/ppermute | solution.py:30
  194.9 5.3 %collective-permute-start.11 = (f32[4,194,1]{1,2,0:T(1,128)S(1)}, f32[4,194,1]{1,2,0:T(1,128)S(1)}, u32[]{:S(2)}, u32[]{:S(2)}) collective-permute-start(f32[4,194,1]{1,2,0:T(1,128)S(1)} %get-tuple-element.29), channel_id=1, source_target_pairs={{0,1},{1,2},{2,3},{3,4},{4,5},{5,6},{6,7},{7,8},{8,9},{9,10},{10,1... | collective-permute-start | bytes 9320 | tf_op jit(solution)/shard_map/ppermute | solution.py:29
  200.9 8.6 %collective-permute-start.12 = (f32[4,1,96]{1,2,0:T(8,128)S(1)}, f32[4,1,96]{1,2,0:T(8,128)S(1)}, u32[]{:S(2)}, u32[]{:S(2)}) collective-permute-start(f32[4,1,96]{1,2,0:T(8,128)S(1)} %get-tuple-element.37), channel_id=1, source_target_pairs={{16,0},{32,16},{48,32},{64,48},{80,64},{96,80},{112,96},{17,1},{33... | collective-permute-start | bytes 4616 | tf_op jit(solution)/shard_map/ppermute | solution.py:30
  202.8 7.8 %collective-permute-start.13 = (f32[4,1,96]{1,2,0:T(8,128)S(1)}, f32[4,1,96]{1,2,0:T(8,128)S(1)}, u32[]{:S(2)}, u32[]{:S(2)}) collective-permute-start(f32[4,1,96]{1,2,0:T(8,128)S(1)} %get-tuple-element.36), channel_id=1, source_target_pairs={{0,16},{16,32},{32,48},{48,64},{64,80},{80,96},{96,112},{1,17},{17... | collective-permute-start | bytes 4616 | tf_op jit(solution)/shard_map/ppermute | solution.py:29
  210.7 22.0 %collective-permute-start.14 = (f32[4,194,1]{1,2,0:T(1,128)S(1)}, f32[4,194,1]{1,2,0:T(1,128)S(1)}, u32[]{:S(2)}, u32[]{:S(2)}) collective-permute-start(f32[4,194,1]{1,2,0:T(1,128)S(1)} %get-tuple-element.26), channel_id=1, source_target_pairs={{1,0},{2,1},{3,2},{4,3},{5,4},{6,5},{7,6},{8,7},{9,8},{10,9},{11,1... | collective-permute-start | bytes 9320 | tf_op jit(solution)/shard_map/ppermute | solution.py:30
  212.0 20.7 %collective-permute-start.15 = (f32[4,194,1]{1,2,0:T(1,128)S(1)}, f32[4,194,1]{1,2,0:T(1,128)S(1)}, u32[]{:S(2)}, u32[]{:S(2)}) collective-permute-start(f32[4,194,1]{1,2,0:T(1,128)S(1)} %get-tuple-element.27), channel_id=1, source_target_pairs={{0,1},{1,2},{2,3},{3,4},{4,5},{5,6},{6,7},{7,8},{8,9},{9,10},{10,1... | collective-permute-start | bytes 9320 | tf_op jit(solution)/shard_map/ppermute | solution.py:29
  218.6 23.7 %all-to-all-start.1 = ((s32[1,128,3]{2,0,1:T(1,128)}), s32[1,128,3]{2,0,1:T(1,128)S(1)}, u32[]{:S(2)}, u32[]{:S(2)}) async-start(s32[1,128,3]{2,0,1:T(1,128)} %bitcast.18), calls=%async_computation.1 | async-start | bytes 131072 | tf_op jit(solution)/shard_map/all_to_all | solution.py:128
  234.5 36.4 %copy-start.7 = (f32[4,4096]{1,0:T(4,128)S(1)}, f32[4,4096]{1,0:T(4,128)}, u32[]{:S(2)}) copy-start(f32[4,4096]{1,0:T(4,128)} %param.19) | copy-start | bytes 196612
  242.3 30.1 %copy-start.1 = (f32[4,41,4096]{2,0,1:T(4,128)S(1)}, f32[4,41,4096]{2,0,1:T(4,128)}, u32[]{:S(2)}) copy-start(f32[4,41,4096]{2,0,1:T(4,128)} %param.20) | copy-start | bytes 8060932
  242.3 24.4 %all-to-all-start = ((f32[4,128,384]{2,0,1:T(4,128)}), f32[4,128,384]{2,0,1:T(4,128)}, u32[]{:S(2)}, u32[]{:S(2)}) async-start(f32[4,128,384]{2,0,1:T(4,128)} %bitcast.74), calls=%async_computation | async-start | bytes 1572864 | tf_op jit(solution)/shard_map/all_to_all | solution.py:121
  280.7 15.0 %all-to-all-start.2 = ((f32[128,1,384]{2,1,0:T(1,128)}), f32[128,1,384]{2,1,0:T(1,128)S(1)}, u32[]{:S(2)}, u32[]{:S(2)}) async-start(f32[128,1,384]{2,1,0:T(1,128)} %bitcast.24), calls=%async_computation.2 | async-start | bytes 393216 | tf_op jit(solution)/shard_map/all_to_all | solution.py:161
  (6 other events, 32.3 us)
Sparse Core Ops, SparseCore 0:
  16.9 149.3 all-reduce.2
where the time goes:
time: 305 us; the launch traced here: 304 us
  waiting for transfers between devices  173 us (57%)
  starting transfers between devices  75 us (25%)
  local copies, waits for them, and re-layouts  24.3 us (8%)
  between operations  16.7 us (5%)
  matrix products  10.1 us (3%)
  other arithmetic  4.74 us (2%)
    psum x1, waiting for transfers between devices, spread(): return lax.psum(jnp.where(mine, value, jnp.zeros_like(value)), axis)  141 us
    ppermute x8, starting transfers between devices, extended(): before = lax.ppermute(last, axis, up)  33.6 us
    ppermute x8, starting transfers between devices, extended(): after = lax.ppermute(initial, axis, down)  15.2 us
    all_to_all x1, waiting for transfers between devices, on_device(): lax.all_to_all(send_flux.reshape(FIELDS, devices, capacity * EXCHANGE_PAT...  14.7 us
    all_to_all x1, starting transfers between devices, on_device(): lax.all_to_all(send_slot.reshape(1, devices, capacity), ('gx', 'gy'), spl...  14 us
    unnamed x25, local copies, waits for them, and re-layouts  8.95 us
    all_to_all x1, starting transfers between devices, on_device(): lax.all_to_all(send_flux.reshape(FIELDS, devices, capacity * EXCHANGE_PAT...  8.09 us
  transfers between devices with their start and end apart: 20, of which 13 were waited for; matrix products, arithmetic and copies ran while one was open for 6% of the time, Pallas kernels for 0%

commit v1 on v0

v1 whole, which is shorter than its diff:
```python
import functools

import jax
import jax.numpy as jnp
from jax import lax
from jax.experimental import pallas as pl
from jax.experimental.pallas import tpu as pltpu
from jax.sharding import PartitionSpec as P

F = 4
CELLS = 128
OCEAN = 32
STEPS = 4
TX, TY = 192, 96
GX, GY = 8, 16
DEV = GX * GY
PC = 384
CAP = 3
NB = 144
HALO = 4
ROWS_X = TX + 2 * HALO
WP = 32
WQ = 18
ROWS = 20
GROUP = 4 * ROWS
PROW = 256
LEFT = tuple(
    i for i in range(GX) if i < GX - 1 and (4 * (TX * i + TX + 2) - 11) // 26 + 1 - (4 * (TX * i - 3) - 11) // 26 >= WP
)
f32, bf16, i32 = jnp.float32, jnp.bfloat16, jnp.int32

diffuse_coef = 0.24
relax_coef = 0.3
drag_coefficient = 0.5


def iota(shape, dim):
    return lax.broadcasted_iota(i32, shape, dim)


def first_x(i):
    return (4 * (TX * i - 3) - 11) // 26


def first_y(j):
    return (4 * (TY * j - 3) - 11) // 26


def first_y_of(j):
    return ((4 * TY * j + 3) * 2521 >> 16) - 1


def first_x_of(i):
    return ((4 * TX * i + 3) * 2521 >> 16) - 1


def dot(a, b):
    return jnp.dot(a, b, preferred_element_type=f32)


def dot_nt(a, b):
    return lax.dot_general(a, b, (((1,), (1,)), ((), ())), preferred_element_type=f32)


def split3(x):
    high = x.astype(bf16)
    rest = x - high.astype(f32)
    mid = rest.astype(bf16)
    return high, mid, (rest - mid.astype(f32)).astype(bf16)


def column_of(row):
    n = row.shape[1]
    return jnp.sum(jnp.where(iota((n, n), 0) == iota((n, n), 1), row, 0), axis=1, keepdims=True)


def pack_kernel(holder_ref, corner_ref, owner_ref, place_ref, parent_ref, out_ref, z_ref):
    me = lax.axis_index("gx") * GY + lax.axis_index("gy")
    mine = me == holder_ref[0]
    cx, cy = corner_ref[0], corner_ref[1]

    @pl.when(mine)
    def _():
        base = pl.multiple_of(jnp.minimum(jnp.maximum(cx - 1, 0) // 16 * 16, PC - PROW), 16)
        row = iota((GY * ROWS, 1), 0)
        j = row * 3277 >> 16
        r = row - j * ROWS
        wanted = jnp.where(r < WQ, cy + first_y_of(j) + r, -1)
        pick_y = (wanted == iota((GY * ROWS, PC), 1)).astype(f32).astype(bf16)
        parts = [parent_ref[f, pl.ds(base, PROW), :] for f in range(F)]
        across = jnp.concatenate([dot_nt(pick_y, parts[f]).astype(bf16) for f in range(F)], axis=1)
        lane = iota((1, 2 * CELLS), 1)
        for pair in range(GX // 2):
            first = jnp.where(lane < CELLS, first_x(2 * pair), first_x(2 * pair + 1))
            p = cx - base + first + (lane & (WP - 1))
            target = jnp.where((p >= 0) & (p < PROW), (lane >> 5 & 3) * PROW + p, -1)
            pick_x = (iota((F * PROW, 2 * CELLS), 0) == target).astype(f32).astype(bf16)
            window = dot(across, pick_x)
            for k in range(2):
                i = 2 * pair + k
                z_ref[pl.ds(i * GY * ROWS, GY * ROWS), :] = window[:, k * CELLS : (k + 1) * CELLS]
        j16 = iota((GY, PC), 0)
        q = iota((GY, PC), 1) - (cy + first_y_of(j16))
        inside = (q >= 0) & (q < WQ)
        lanes = iota((GY, CELLS), 1) >> 5
        erow = iota((8, PROW), 0)
        target = jnp.full((8, PROW), -1, i32)
        for k, i in enumerate(LEFT):
            target = jnp.where(erow == k, cx - base + first_x(i) + WP, target)
        pick_row = (target == iota((8, PROW), 1)).astype(f32).astype(bf16)
        left = [jnp.zeros((GY, CELLS), f32) for _ in LEFT]
        for f in range(F):
            rows = dot(pick_row, parts[f])
            for k in range(len(LEFT)):
                kept = jnp.where(inside, rows[k : k + 1, :], 0.0)
                folded = kept[:, :128] + kept[:, 128:256] + kept[:, 256:]
                folded = folded + pltpu.roll(folded, 64, 1)
                folded = folded + pltpu.roll(folded, 32, 1)
                left[k] = jnp.where(lanes == f, folded, left[k])
        for k, i in enumerate(LEFT):
            z_ref[pl.ds(i * GY * ROWS + WQ, GY, stride=ROWS), :] = left[k]

    @pl.when(jnp.logical_not(mine))
    def _():
        z_ref[...] = jnp.zeros_like(z_ref)

    owner = owner_ref[...]
    rank = jnp.sum(
        jnp.where((column_of(owner) == owner) & (iota((NB, NB), 0) < iota((NB, NB), 1)), 1, 0), axis=0, keepdims=True
    )
    named = iota((DEV, NB), 0) == owner
    slots = jnp.zeros((DEV, CELLS), f32)
    for s in range(CAP):
        value = jnp.sum(jnp.where(named & (rank == s), place_ref[...] + 1, 0).astype(f32), axis=1, keepdims=True) - 1.0
        slots = jnp.where(iota((DEV, CELLS), 1) == s, value, slots)
    z_ref[pl.ds(ROWS - 1, DEV, stride=ROWS), :] = slots
    out_ref[...] = z_ref[...].astype(bf16)


def pack(holder, corner, owner, place, parent):
    smem = pl.BlockSpec(memory_space=pltpu.SMEM)
    vmem = pl.BlockSpec(memory_space=pltpu.VMEM)
    return pl.pallas_call(
        pack_kernel,
        out_shape=jax.ShapeDtypeStruct((DEV * ROWS, CELLS), bf16),
        in_specs=[smem, smem, vmem, vmem, vmem],
        out_specs=vmem,
        scratch_shapes=[pltpu.VMEM((DEV * ROWS, CELLS), f32)],
        compiler_params=pltpu.CompilerParams(vmem_limit_bytes=32 << 20),
    )(holder, corner, owner, place, parent)


def hat(fine, anchor, coarse):
    centre = (fine.astype(f32) + 0.5) * (2.0 / 13.0) - 0.5 + anchor.astype(f32)
    return jnp.maximum(0.0, 1.0 - jnp.abs(centre - coarse.astype(f32)))


def tables_kernel(holder_ref, corner_ref, owner_ref, owner_t_ref, wx_ref, wy_ref, wyc_ref, wlast_ref, mask_ref, send_ref, back_ref):
    ix, iy = lax.axis_index("gx"), lax.axis_index("gy")
    cx, cy = corner_ref[0], corner_ref[1]
    x0, y0 = ix * TX - HALO, iy * TY - HALO
    px, qy = cx + first_x_of(ix), cy + first_y_of(iy)
    lane = iota((ROWS_X, CELLS), 1)
    row = iota((ROWS_X, CELLS), 0)
    weight = hat(row + x0, cx, (lane & (WP - 1)) + px)
    for f in range(F):
        wx_ref[f * ROWS_X : (f + 1) * ROWS_X, :] = jnp.where(lane >> 5 == f, weight, 0.0).astype(bf16)
    wlast_ref[...] = hat(row + x0, cx, jnp.full_like(row, WP) + px).astype(bf16).astype(f32)
    inside = (row + x0 >= 0) & (row + x0 < GX * TX) & (lane + y0 >= 0) & (lane + y0 < GY * TY)
    mask_ref[...] = jnp.where(inside, 1.0, 0.0)
    at = iota((CELLS, GROUP), 1) - (holder_ref[0] & 3) * ROWS
    wy_ref[...] = jnp.where(
        (at >= 0) & (at < WQ), hat(iota((CELLS, GROUP), 0) + y0, cy, at + qy), 0.0
    ).astype(bf16)
    lane = iota((CELLS, CELLS), 1)
    wyc_ref[...] = hat(iota((CELLS, CELLS), 0) + y0, cy, qy + ((lane - qy) & (WP - 1))).astype(bf16)
    owner, owner_t = owner_ref[...], owner_t_ref[...]
    at = iota((1, NB), 1)
    third = (at >= NB // CAP).astype(i32) + (at >= 2 * (NB // CAP)).astype(i32)
    number = CAP * (at - third * (NB // CAP)) + third
    rank = jnp.sum(jnp.where((column_of(owner) == owner_t) & (iota((NB, NB), 0) < number), 1, 0), axis=0, keepdims=True)
    send_ref[...] = (iota((CAP * DEV, NB), 0) == rank * DEV + owner_t).astype(f32).astype(bf16)
    back_ref[...] = (column_of(owner_t * CAP + rank) == iota((NB, CAP * DEV), 1)).astype(f32).astype(bf16)


def tables(holder, corner, owner, owner_t):
    smem = pl.BlockSpec(memory_space=pltpu.SMEM)
    vmem = pl.BlockSpec(memory_space=pltpu.VMEM)
    shapes = (
        ((F * ROWS_X, CELLS), bf16),
        ((CELLS, GROUP), bf16),
        ((CELLS, CELLS), bf16),
        ((ROWS_X, CELLS), f32),
        ((ROWS_X, CELLS), f32),
        ((CAP * DEV, NB), bf16),
        ((NB, CAP * DEV), bf16),
    )
    return pl.pallas_call(
        tables_kernel,
        out_shape=tuple(jax.ShapeDtypeStruct(s, d) for s, d in shapes),
        in_specs=[smem, smem, vmem, vmem],
        out_specs=tuple(vmem for _ in shapes),
    )(holder, corner, owner, owner_t)


def columns_kernel(s_ref, low_ref, high_ref):
    for f in range(F):
        turned = jnp.swapaxes(s_ref[f], 0, 1)
        low_ref[f * HALO : (f + 1) * HALO, :] = turned[:HALO, :]
        high_ref[f * HALO : (f + 1) * HALO, :] = turned[TY - HALO :, :]


def widen_kernel(s_ref, left_ref, right_ref, out_ref, low_ref, high_ref):
    n = F * HALO
    both = jnp.concatenate([left_ref[...], right_ref[...], jnp.zeros((CELLS - 2 * n, TX), f32)], axis=0)
    turned = jnp.swapaxes(both, 0, 1)
    lane = iota((TX, CELLS), 1)
    for f in range(F):
        out_ref[f] = jnp.zeros((TX, CELLS), f32)
        out_ref[f, :, HALO : HALO + TY] = s_ref[f]
        before = turned if f == 0 else pltpu.roll(turned, CELLS - HALO * f, 1)
        after = pltpu.roll(turned, TY + HALO - n - HALO * f, 1)
        wide = jnp.where(lane < HALO, before, jnp.where((lane >= TY + HALO) & (lane < TY + 2 * HALO), after, out_ref[f]))
        out_ref[f] = wide
        low_ref[f * HALO : (f + 1) * HALO, :] = wide[:HALO]
        high_ref[f * HALO : (f + 1) * HALO, :] = wide[TX - HALO :]


def nest_kernel(
    holder_ref, got_ref, wx_ref, wy_ref, wyc_ref, wlast_ref, mask_ref, s_ref, before_ref, after_ref, skin_ref, send_ref,
    next_ref, out_ref, state_ref, force_ref, flux_ref, z_ref,
):
    got = got_ref[...]
    partial = dot(wy_ref[...], got).astype(bf16)
    last = jnp.sum(
        jnp.where(iota((GROUP, CELLS), 0) == (holder_ref[0] & 3) * ROWS + WQ, got.astype(f32), 0.0), axis=0, keepdims=True
    )
    field = iota((8, CELLS), 0)
    last = jnp.where(iota((8, CELLS), 1) >> 5 == field, last, 0.0).astype(bf16)
    partial_last = dot_nt(last, wyc_ref[...]).astype(bf16).astype(f32)
    force_ref[...] = dot_nt(wx_ref[...], partial)
    mask = mask_ref[...]
    for f in range(F):
        force = force_ref[f * ROWS_X : (f + 1) * ROWS_X, :] + wlast_ref[...] * partial_last[f : f + 1, :]
        force = relax_coef * force
        state_ref[:HALO, :] = before_ref[f * HALO : (f + 1) * HALO, :]
        state_ref[HALO : HALO + TX, :] = s_ref[f]
        state_ref[HALO + TX :, :] = after_ref[f * HALO : (f + 1) * HALO, :]
        s = state_ref[...]
        for _ in range(STEPS):
            beside = (
                pltpu.roll(s, 1, 0) + pltpu.roll(s, ROWS_X - 1, 0) + pltpu.roll(s, 1, 1) + pltpu.roll(s, CELLS - 1, 1)
            )
            s = mask * ((1.0 - 4.0 * diffuse_coef - relax_coef) * s + diffuse_coef * beside + force)
        state_ref[...] = pltpu.roll(s, CELLS - HALO, 1)
        next_ref[f] = state_ref[HALO : HALO + TX, :TY]
    u, v, ta, qa = next_ref[0], next_ref[1], next_ref[2], next_ref[3]
    half = drag_coefficient * jnp.sqrt(1.0 + u * u + v * v)
    skin = skin_ref[...]
    flux = (half * (ta - skin), half * (qa - 0.5 * skin), half * u, half * v)
    rows = NB // CAP
    lane = iota((rows, CELLS), 1)
    blocks = []
    for f in range(F):
        flux_ref[:, :TY] = flux[f]
        m = [flux_ref[pl.ds(k, rows, stride=4), :] for k in range(4)]
        r1, r2, r3 = pltpu.roll(m[1], 96, 1), pltpu.roll(m[2], 64, 1), pltpu.roll(m[3], 32, 1)
        blocks.append(
            jnp.concatenate(
                [jnp.where(lane < 96, m[0], r1), jnp.where(lane < 64, r1, r2), jnp.where(lane < 32, r2, r3)], axis=0
            ).astype(bf16)
        )
    sent = dot(send_ref[...], jnp.concatenate(blocks, axis=1))
    for slot in range(CAP):
        for f in range(F):
            z_ref[pl.ds(slot * F + f, DEV, stride=CAP * F), :] = sent[
                slot * DEV : (slot + 1) * DEV, f * CELLS : (f + 1) * CELLS
            ]
    out_ref[...] = z_ref[...].astype(bf16)


def nest(holder, got, wx, wy, wyc, wlast, mask, s, before, after, skin, send):
    def whole(shape):
        return pl.BlockSpec(shape, lambda _, h: (0,) * len(shape))

    rest = (wx, wy, wyc, wlast, mask, s, before, after, skin, send)
    return pl.pallas_call(
        nest_kernel,
        out_shape=(
            jax.ShapeDtypeStruct((F, TX, TY), f32),
            jax.ShapeDtypeStruct((DEV * CAP * F, CELLS), bf16),
        ),
        grid_spec=pltpu.PrefetchScalarGridSpec(
            num_scalar_prefetch=1,
            grid=(1,),
            in_specs=[pl.BlockSpec((GROUP, CELLS), lambda _, h: (h[0] >> 2, 0))] + [whole(a.shape) for a in rest],
            out_specs=(whole((F, TX, TY)), whole((DEV * CAP * F, CELLS))),
            scratch_shapes=[
                pltpu.VMEM((ROWS_X, CELLS), f32),
                pltpu.VMEM((F * ROWS_X, CELLS), f32),
                pltpu.VMEM((TX, CELLS), f32),
                pltpu.VMEM((DEV * CAP * F, CELLS), f32),
            ],
        ),
        compiler_params=pltpu.CompilerParams(vmem_limit_bytes=32 << 20),
    )(holder, got, *rest)


def ocean_kernel(scale_ref, got_ref, hot_ref, inverse_ref, kept_ref, base_ref, give_ref, forcing_ref, out_ref):
    forcing = dot(hot_ref[...], got_ref[...]) * inverse_ref[...] + kept_ref[...]
    forcing_ref[...] = forcing
    top = base_ref[...] + scale_ref[0, 0] * forcing
    back = dot(give_ref[...], jnp.concatenate(split3(top), axis=1))
    out_ref[...] = back[:, :CELLS] + back[:, CELLS : 2 * CELLS] + back[:, 2 * CELLS :]


def skin_kernel(got_ref, back_ref, out_ref, tile_ref):
    x = dot(back_ref[...], jnp.concatenate(split3(got_ref[...]), axis=1))
    x = x[:, :CELLS] + x[:, CELLS : 2 * CELLS] + x[:, 2 * CELLS :]
    rows = NB // CAP
    t0, t1, t2 = x[:rows], x[rows : 2 * rows], x[2 * rows :]
    lane = iota((rows, CELLS), 1)
    tile_ref[pl.ds(0, rows, stride=4), :] = t0
    tile_ref[pl.ds(1, rows, stride=4), :] = pltpu.roll(jnp.where(lane < 64, t1, t0), 32, 1)
    tile_ref[pl.ds(2, rows, stride=4), :] = pltpu.roll(jnp.where(lane < 32, t2, t1), 64, 1)
    tile_ref[pl.ds(3, rows, stride=4), :] = pltpu.roll(t2, 96, 1)
    out_ref[...] = tile_ref[:, :TY]


def call(kernel, outs, *args, smem=(), scratch=()):
    vmem = pl.BlockSpec(memory_space=pltpu.VMEM)
    return pl.pallas_call(
        kernel,
        out_shape=outs,
        in_specs=[pl.BlockSpec(memory_space=pltpu.SMEM) if k in smem else vmem for k in range(len(args))],
        out_specs=jax.tree.map(lambda _: vmem, outs),
        scratch_shapes=scratch,
    )(*args)


def shift(value, axis, by):
    n = lax.axis_size(axis)
    return lax.ppermute(value, axis, [(i, i + by) for i in range(n) if 0 <= i + by < n])


def exchange(value, rows):
    split = value.reshape(rows)
    return lax.all_to_all(split, ("gx", "gy"), split_axis=0, concat_axis=0, tiled=True).reshape(value.shape)


def by_block(value):
    return value.reshape(F, OCEAN, CELLS).transpose(1, 0, 2).reshape(OCEAN * F, CELLS)


def on_device(
    fine_atmospheric_values,
    fine_skin_heat,
    coarse_lowest_values,
    holder_flat,
    corner_offset,
    exchange_patch_holder,
    holder_patch_position,
    coarse_interface_exchange,
    marine_stratum_values,
    diffusion_solver_operator,
):
    sds = jax.ShapeDtypeStruct
    owner = exchange_patch_holder.reshape(1, NB)
    owner_t = owner.reshape(NB // CAP, CAP).T.reshape(1, NB)
    place = holder_patch_position.reshape(1, NB)
    windows = pack(holder_flat, corner_offset, owner, place, coarse_lowest_values)
    got = exchange(windows, (DEV, ROWS // 4, 4, CELLS))
    strip = sds((F * HALO, TX), f32)
    low, high = call(columns_kernel, (strip, strip), fine_atmospheric_values)
    left, right = shift(high, "gy", 1), shift(low, "gy", -1)
    strip = sds((F * HALO, CELLS), f32)
    wide, low, high = call(
        widen_kernel, (sds((F, TX, CELLS), f32), strip, strip), fine_atmospheric_values, left, right
    )
    before, after = shift(high, "gx", 1), shift(low, "gx", -1)
    *weights, send, back = tables(holder_flat, corner_offset, owner, owner_t)
    nest_next, flux = nest(holder_flat, got, *weights, wide, before, after, fine_skin_heat, send)
    got_flux = exchange(flux, (DEV, CAP, F, CELLS))
    marine = marine_stratum_values.transpose(1, 0, 2)
    base = jnp.einsum("lk,kfc->lfc", diffusion_solver_operator, marine, precision=lax.Precision.HIGHEST)
    slot = got.reshape(DEV, ROWS, CELLS)[:, ROWS - 1, :CAP].astype(i32).reshape(DEV * CAP)
    target = jnp.where(slot >= 0, slot * F, -F)[:, None] + jnp.arange(F)[None, :]
    hot = jnp.arange(OCEAN * F)[:, None] == target.reshape(1, DEV * CAP * F)
    give = (slot[:, None] * F == jnp.arange(OCEAN * F)[None, :]).astype(bf16)
    count = jnp.sum(hot.astype(f32), axis=1, keepdims=True)
    ones = jnp.ones((1, CELLS), f32)
    inverse = ones / jnp.maximum(count, 1.0)
    kept = by_block(coarse_interface_exchange) * (count == 0.0).astype(f32)
    block = sds((OCEAN * F, CELLS), f32)
    forcing, returned = call(
        ocean_kernel, (block, sds((DEV * CAP, CELLS), f32)),
        diffusion_solver_operator, got_flux, hot.astype(bf16), inverse, kept, by_block(base[0]), give, smem=(0,),
    )
    arrived = exchange(returned, (DEV, 1, CAP * CELLS))
    cells = forcing.reshape(OCEAN, F, CELLS).transpose(1, 0, 2).reshape(F, OCEAN * CELLS)
    refreshed = base + diffusion_solver_operator[:, 0][:, None, None] * cells[None]
    skin = call(
        skin_kernel, sds((TX, TY), f32), arrived, back, scratch=[pltpu.VMEM((TX, CELLS), f32)]
    )
    return (nest_next, refreshed.transpose(1, 0, 2), skin)


def solution(mesh):
    in_specs = (
        P(None, "gx", "gy"),
        P("gx", "gy"),
        P(None, "gx", "gy"),
        P(),
        P(),
        P(("gx", "gy"), None),
        P(("gx", "gy")),
        P(None, ("gx", "gy")),
        P(None, None, ("gx", "gy")),
        P(),
    )
    out_specs = (P(None, "gx", "gy"), P(None, None, ("gx", "gy")), P("gx", "gy"))
    return jax.shard_map(
        on_device, mesh=mesh, in_specs=in_specs, out_specs=out_specs, check_vma=False
    )
```

time: 305 us -> 104 us (0.34)
  waiting for transfers between devices: 173 us -> 16.6 us
  starting transfers between devices: 75 us -> 36.8 us
  between operations: 16.7 us -> 1.68 us
  Pallas kernels: 0 us -> 13.8 us
  matrix products: 10.1 us -> 5.94 us
    psum x1 -> x0, waiting for transfers between devices: 141 us -> none  [spread(): return lax.psum(jnp.where(mine, value, jnp.zeros_like(value)), axis)]
    ppermute x16 -> x4, starting transfers between devices: 48.8 us -> 10.1 us  [shift(): lax.ppermute(value, axis, [(i, i + by) for i in range(n) if 0 <= i + by <...]
    pallas_call x0 -> x7, Pallas kernels: none -> 13.8 us  [the longest x4 8.27 us: call(): pl.pallas_call(kernel, out_shape=outs, in_specs=[pl.BlockSpec(memory_spac...]
    ppermute x16 -> x4, waiting for transfers between devices: 9.51 us -> 0.01 us  [shift(): lax.ppermute(value, axis, [(i, i + by) for i in range(n) if 0 <= i + by <...]
    unnamed x25 -> x46, local copies, waits for them, and re-layouts: 8.95 us -> 16.8 us
    scatter x2 -> x0, local copies, waits for them, and re-layouts: 6 us -> none  [the longest x1 4.8 us: on_device(): send_flux = jnp.zeros((FIELDS, devices * capacity, EXCHANGE_PATCH), jnp.f...]
    all_to_all x3, waiting for transfers between devices: 22.5 us -> 16.6 us  [exchange(): lax.all_to_all(split, ('gx', 'gy'), split_axis=0, concat_axis=0, tiled=True)]
    dot_general x4 -> x1, matrix products: 10.1 us -> 5.94 us  [on_device(): jnp.einsum('lk,kfc->lfc', diffusion_solver_operator, marine, precision=la...]
  transfers between devices with their start and end apart: 20 -> 7, of which waited for: 13 -> 2; matrix products, arithmetic and copies ran while one was open for 6% -> 20% of each run, Pallas kernels for 0% -> 6%
where the time goes in v1:
time: 104 us; the launch traced here: 103 us
  starting transfers between devices  36.8 us (35%)
  local copies, waits for them, and re-layouts  21.8 us (21%)
  waiting for transfers between devices  16.6 us (16%)
  Pallas kernels  13.8 us (13%)
  other arithmetic  6.23 us (6%)
  matrix products  5.94 us (6%)
  between operations  1.68 us (2%)
    all_to_all x3, starting transfers between devices, exchange(): lax.all_to_all(split, ('gx', 'gy'), split_axis=0, concat_axis=0, tiled=True)  26.7 us
    unnamed x46, local copies, waits for them, and re-layouts  16.8 us
    all_to_all x3, waiting for transfers between devices, exchange(): lax.all_to_all(split, ('gx', 'gy'), split_axis=0, concat_axis=0, tiled=True)  16.6 us
    ppermute x4, starting transfers between devices, shift(): lax.ppermute(value, axis, [(i, i + by) for i in range(n) if 0 <= i + by <...  10.1 us
    pallas_call x4, Pallas kernels, call(): pl.pallas_call(kernel, out_shape=outs, in_specs=[pl.BlockSpec(memory_spac...  8.27 us
    dot_general x1, matrix products, on_device(): jnp.einsum('lk,kfc->lfc', diffusion_solver_operator, marine, precision=la...  5.94 us
    pallas_call x1, Pallas kernels, nest(): pl.pallas_call(nest_kernel, out_shape=(jax.ShapeDtypeStruct((F, TX, TY),...  2.78 us
    add x1, other arithmetic, on_device(): base + diffusion_solver_operator[:, 0][:, None, None] * cells[None]  2.31 us
  transfers between devices with their start and end apart: 7, of which 2 were waited for; matrix products, arithmetic and copies ran while one was open for 20% of the time, Pallas kernels for 6%

profile of v1, /device:TPU:1, one launch (start us, length us, event | category | flops | bytes accessed | tf_op | source)
XLA Modules:
  0.0 102.9 jit_solution(6308074897944153281)
XLA Ops:
  1.5 1.3 %copy-done.2 = bf16[4,384,384]{2,1,0:T(8,128)(2,1)S(1)} copy-done((bf16[4,384,384]{2,1,0:T(8,128)(2,1)S(1)}, bf16[4,384,384]{2,1,0:T(8,128)(2,1)}, u32[]{:S(2)}) %copy-start.2) | copy-done | bytes 1179672
  4.7 0.9 shard_map.121
  6.5 11.5 %all-to-all-start = ((bf16[128,5,4,128]{3,2,1,0:T(4,128)(2,1)}), bf16[128,5,4,128]{3,2,1,0:T(4,128)(2,1)S(1)}, u32[]{:S(2)}, u32[]{:S(2)}) async-start(bf16[128,5,4,128]{3,2,1,0:T(4,128)(2,1)} %bitcast.37), calls=%async_computation | async-start | bytes 1310720 | tf_op jit(solution)/shard_map/all_to_all | solution.py:348
  18.0 1.8 %shard_map.123 = (f32[16,192]{1,0:T(8,128)}, f32[16,192]{1,0:T(8,128)}) custom-call(f32[4,192,96]{2,1,0:T(8,128)} %s_ref.3), custom_call_target="tpu_custom_call" | custom-call | tf_op jit(solution)/shard_map/pallas_call | solution.py:332
  19.8 3.3 %collective-permute-start = (f32[16,192]{1,0:T(8,128)}, f32[16,192]{1,0:T(8,128)S(1)}, u32[]{:S(2)}, u32[]{:S(2)}) collective-permute-start(f32[16,192]{1,0:T(8,128)} %get-tuple-element.24), channel_id=1, source_target_pairs={{0,1},{1,2},{2,3},{3,4},{4,5},{5,6},{6,7},{7,8},{8,9},{9,10},{10,1... | collective-permute-start | bytes 36872 | tf_op jit(solution)/shard_map/ppermute | solution.py:343
  23.1 1.3 %collective-permute-start.1 = (f32[16,192]{1,0:T(8,128)}, f32[16,192]{1,0:T(8,128)S(1)}, u32[]{:S(2)}, u32[]{:S(2)}) collective-permute-start(f32[16,192]{1,0:T(8,128)} %get-tuple-element.25), channel_id=1, source_target_pairs={{1,0},{2,1},{3,2},{4,3},{5,4},{6,5},{7,6},{8,7},{9,8},{10,9},{11,1... | collective-permute-start | bytes 36872 | tf_op jit(solution)/shard_map/ppermute | solution.py:343
  24.5 5.9 %fusion = f32[41,4,4096]{2,0,1:T(8,128)} fusion(f32[41,4,4096]{2,1,0:T(4,128)S(1)} %bitcast.35, f32[41,41]{1,0:T(8,128)S(1)} %copy-done.18), kind=kOutput, calls=%fused_computation.1 | convolution fusion | flops 330498048 | bytes 5380676 | tf_op jit(solution)/shard_map/lk,kfc->lfc/dot_general | solution.py:385
  32.6 1.8 %shard_map.122 = (bf16[800,128]{1,0:T(8,128)(2,1)}, bf16[128,80]{1,0:T(8,128)(2,1)}, bf16[128,128]{1,0:T(8,128)(2,1)}, f32[200,128]{1,0:T(8,128)}, f32[200,128]{...) custom-call(s32[1]{0:T(128)S(6)} %copy.34.holder_ref, s32[2]{0:T(128)} %corner_ref.3, ...), custom_call_target="tpu_custom_call" | custom-call | tf_op jit(solution)/shard_map/pallas_call | solution.py:198
  34.4 1.1 %slice.13 = f32[1,4,4096]{2,0,1:T(1,128)S(1)} slice(f32[41,4,4096]{2,0,1:T(8,128)} %fusion), slice={[0:1], [0:4], [0:4096]} | slice | bytes 131072 | tf_op jit(solution)/shard_map/slice | solution.py:397
  37.4 2.2 %shard_map.124 = (f32[4,192,128]{2,1,0:T(8,128)}, f32[16,128]{1,0:T(8,128)}, f32[16,128]{1,0:T(8,128)}) custom-call(f32[4,192,96]{2,1,0:T(8,128)} %s_ref.3, f32[16,192]{1,0:T(8,128)} %copy-done.20, f32[16,192]{1,0:T(8,128)} %copy-done.21), custom_call_target="tpu_custom_call" | custom-call | tf_op jit(solution)/shard_map/pallas_call | solution.py:332
  39.5 3.6 %collective-permute-start.2 = (f32[16,128]{1,0:T(8,128)}, f32[16,128]{1,0:T(8,128)S(1)}, u32[]{:S(2)}, u32[]{:S(2)}) collective-permute-start(f32[16,128]{1,0:T(8,128)} %get-tuple-element.27), channel_id=1, source_target_pairs={{0,16},{16,32},{32,48},{48,64},{64,80},{80,96},{96,112},{1,17},{17... | collective-permute-start | bytes 24584 | tf_op jit(solution)/shard_map/ppermute | solution.py:343
  43.1 1.9 %collective-permute-start.3 = (f32[16,128]{1,0:T(8,128)}, f32[16,128]{1,0:T(8,128)S(1)}, u32[]{:S(2)}, u32[]{:S(2)}) collective-permute-start(f32[16,128]{1,0:T(8,128)} %get-tuple-element.28), channel_id=1, source_target_pairs={{16,0},{32,16},{48,32},{64,48},{80,64},{96,80},{112,96},{17,1},{33... | collective-permute-start | bytes 24584 | tf_op jit(solution)/shard_map/ppermute | solution.py:343
  47.3 1.1 %add.27 = s32[1536]{0:T(1024)S(1)} reshape(s32[384,4]{1,0:T(8,128)} %iota_add_fusion) | data formatting | bytes 12288 | tf_op jit(solution)/shard_map/add | solution.py:387
  48.6 1.0 copy-done.4
  49.5 0.9 copy-done.5
  54.7 2.8 %shard_map.125 = (f32[4,192,96]{2,1,0:T(8,128)}, bf16[1536,128]{1,0:T(8,128)(2,1)S(1)}) custom-call(s32[1]{0:T(128)S(6)} %copy.34.holder_ref, bf16[2560,128]{1,0:T(8,128)(2,1)S(1)} %bitcast.36, bf16[800,128]{1,0:T(8,128)(2,1)S(1)} %copy-done.5, bf16[128,80]{1,0:T(8,128)(2,1)S(1)} %copy-done.10, bf16[128,128]{1,0:T(8,128)(2,1)S(1)} %copy-done.11, ...), custom_call_target="tpu_custom_call" | custom-call | tf_op jit(solution)/shard_map/pallas_call | solution.py:287
  58.2 11.0 %all-to-all-start.1 = ((bf16[128,3,4,128]{3,2,1,0:T(4,128)(2,1)}), bf16[128,3,4,128]{3,2,1,0:T(4,128)(2,1)S(1)}, u32[]{:S(2)}, u32[]{:S(2)}) async-start(bf16[128,3,4,128]{3,2,1,0:T(4,128)(2,1)} %bitcast.38), calls=%async_computation.1 | async-start | bytes 786432 | tf_op jit(solution)/shard_map/all_to_all | solution.py:348
  70.8 11.2 %all-to-all-done.1 = bf16[128,3,4,128]{3,2,1,0:T(4,128)(2,1)S(1)} async-done(((bf16[128,3,4,128]{3,2,1,0:T(4,128)(2,1)}), bf16[128,3,4,128]{3,2,1,0:T(4,128)(2,1)S(1)}, u32[]{:S(2)}, u32[]{:S(2)}) %all-to-all-start.1) | async-done | bytes 393248 | tf_op jit(solution)/shard_map/all_to_all | solution.py:348
  82.8 2.3 %shard_map.126 = (f32[128,128]{1,0:T(8,128)}, f32[384,128]{1,0:T(8,128)}) custom-call(f32[41,41]{1,0:T(8,128)} %scale_ref.1, bf16[1536,128]{1,0:T(8,128)(2,1)} %bitcast.42, bf16[128,1536]{1,0:T(8,128)(2,1)} %fusion.2.hot_ref, f32[128,128]{1,0:T(8,128)} %div.9.inverse_ref, f32[128,128]{1,0:T(8,128)} %broadcast_multiply_fusion.kept_ref, f32[128,128]{1,0:T(8,128)} %bitcast.46, ...), custom_call_target="tpu_custom_call" | custom-call | tf_op jit(solution)/shard_map/pallas_call | solution.py:332
  85.1 4.1 %all-to-all-start.2 = ((f32[128,1,384]{2,1,0:T(1,128)}), f32[128,1,384]{2,1,0:T(1,128)S(1)}, u32[]{:S(2)}, u32[]{:S(2)}) async-start(f32[128,1,384]{2,1,0:T(1,128)} %bitcast.48), calls=%async_computation.2 | async-start | bytes 393216 | tf_op jit(solution)/shard_map/all_to_all | solution.py:348
  89.3 2.3 %bitcast_add_fusion = f32[4,41,4096]{2,1,0:T(8,128)S(1)} fusion(f32[41,4,4096]{2,0,1:T(8,128)} %fusion, f32[4,4096]{1,0:T(4,128)} %bitcast.50, f32[41]{0:T(128)S(1)} %slice_reduce_fusion), kind=kLoop, calls=%fused_computation | loop fusion | flops 1343488 | bytes 5439652 | tf_op jit(solution)/shard_map/add | solution.py:401
  91.6 3.2 %copy.31 = f32[4,41,4096]{2,0,1:T(4,128)} copy(f32[4,41,4096]{2,1,0:T(8,128)S(1)} %bitcast_add_fusion) | data formatting | bytes 5373952
  94.8 5.4 %all-to-all-done.2 = f32[128,1,384]{2,1,0:T(1,128)S(1)} async-done(((f32[128,1,384]{2,1,0:T(1,128)}), f32[128,1,384]{2,1,0:T(1,128)S(1)}, u32[]{:S(2)}, u32[]{:S(2)}) %all-to-all-start.2) | async-done | bytes 196640 | tf_op jit(solution)/shard_map/all_to_all | solution.py:348
  100.9 2.0 %shard_map.127 = f32[192,96]{1,0:T(8,128)} custom-call(f32[384,128]{1,0:T(8,128)} %bitcast.45, bf16[144,384]{1,0:T(8,128)(2,1)} %get-tuple-element.34.back_ref), custom_call_target="tpu_custom_call" | custom-call | tf_op jit(solution)/shard_map/pallas_call | solution.py:332
  (67 shorter events, 17.2 us)
Async XLA Ops:
  0.6 23.8 %copy-start = (f32[4,41,4096]{2,0,1:T(4,128)S(1)}, f32[4,41,4096]{2,0,1:T(4,128)}, u32[]{:S(2)}) copy-start(f32[4,41,4096]{2,0,1:T(4,128)} %param.18) | copy-start | bytes 8060932
  1.4 1.3 %copy-start.2 = (bf16[4,384,384]{2,1,0:T(8,128)(2,1)S(1)}, bf16[4,384,384]{2,1,0:T(8,128)(2,1)}, u32[]{:S(2)}) copy-start(bf16[4,384,384]{2,1,0:T(8,128)(2,1)} %parent_ref.1) | copy-start | bytes 3538948
  4.7 19.7 %copy-start.18 = (f32[41,41]{1,0:T(8,128)S(1)}, f32[41,41]{1,0:T(8,128)}, u32[]{:S(2)}) copy-start(f32[41,41]{1,0:T(8,128)} %scale_ref.1) | copy-start | bytes 20176
  5.7 0.8 copy-start.1
  6.5 38.5 %all-to-all-start = ((bf16[128,5,4,128]{3,2,1,0:T(4,128)(2,1)}), bf16[128,5,4,128]{3,2,1,0:T(4,128)(2,1)S(1)}, u32[]{:S(2)}, u32[]{:S(2)}) async-start(bf16[128,5,4,128]{3,2,1,0:T(4,128)(2,1)} %bitcast.37), calls=%async_computation | async-start | bytes 1310720 | tf_op jit(solution)/shard_map/all_to_all | solution.py:348
  19.8 16.3 %collective-permute-start = (f32[16,192]{1,0:T(8,128)}, f32[16,192]{1,0:T(8,128)S(1)}, u32[]{:S(2)}, u32[]{:S(2)}) collective-permute-start(f32[16,192]{1,0:T(8,128)} %get-tuple-element.24), channel_id=1, source_target_pairs={{0,1},{1,2},{2,3},{3,4},{4,5},{5,6},{6,7},{7,8},{8,9},{9,10},{10,1... | collective-permute-start | bytes 36872 | tf_op jit(solution)/shard_map/ppermute | solution.py:343
  23.1 13.0 %collective-permute-start.1 = (f32[16,192]{1,0:T(8,128)}, f32[16,192]{1,0:T(8,128)S(1)}, u32[]{:S(2)}, u32[]{:S(2)}) collective-permute-start(f32[16,192]{1,0:T(8,128)} %get-tuple-element.25), channel_id=1, source_target_pairs={{1,0},{2,1},{3,2},{4,3},{5,4},{6,5},{7,6},{8,7},{9,8},{10,9},{11,1... | collective-permute-start | bytes 36872 | tf_op jit(solution)/shard_map/ppermute | solution.py:343
  24.4 6.7 %copy-start.13 = (s32[144,1]{0,1:T(1,128)S(1)}, s32[144,1]{0,1:T(1,128)}, u32[]{:S(2)}) copy-start(s32[144,1]{0,1:T(1,128)} %param.15) | copy-start | bytes 1732
  24.5 24.1 %copy-start.9 = (f32[192,96]{1,0:T(8,128)S(1)}, f32[192,96]{1,0:T(8,128)}, u32[]{:S(2)}) copy-start(f32[192,96]{1,0:T(8,128)} %skin_ref.1) | copy-start | bytes 221188
  39.5 9.0 %collective-permute-start.2 = (f32[16,128]{1,0:T(8,128)}, f32[16,128]{1,0:T(8,128)S(1)}, u32[]{:S(2)}, u32[]{:S(2)}) collective-permute-start(f32[16,128]{1,0:T(8,128)} %get-tuple-element.27), channel_id=1, source_target_pairs={{0,16},{16,32},{32,48},{48,64},{64,80},{80,96},{96,112},{1,17},{17... | collective-permute-start | bytes 24584 | tf_op jit(solution)/shard_map/ppermute | solution.py:343
  43.1 5.4 %collective-permute-start.3 = (f32[16,128]{1,0:T(8,128)}, f32[16,128]{1,0:T(8,128)S(1)}, u32[]{:S(2)}, u32[]{:S(2)}) collective-permute-start(f32[16,128]{1,0:T(8,128)} %get-tuple-element.28), channel_id=1, source_target_pairs={{16,0},{32,16},{48,32},{64,48},{80,64},{96,80},{112,96},{17,1},{33... | collective-permute-start | bytes 24584 | tf_op jit(solution)/shard_map/ppermute | solution.py:343
  45.7 23.6 %copy-start.19 = (f32[4,4096]{1,0:T(4,128)S(1)}, f32[4,4096]{1,0:T(4,128)}, u32[]{:S(2)}) copy-start(f32[4,4096]{1,0:T(4,128)} %param.17) | copy-start | bytes 196612
  48.5 1.0 copy-start.4
  49.5 0.9 copy-start.5
  50.5 0.9 copy-start.6
  51.4 0.9 copy-start.7
  52.3 0.9 copy-start.8
  53.2 0.8 copy-start.10
  53.9 0.8 copy-start.11
  57.5 0.7 copy-start.3
  58.2 23.8 %all-to-all-start.1 = ((bf16[128,3,4,128]{3,2,1,0:T(4,128)(2,1)}), bf16[128,3,4,128]{3,2,1,0:T(4,128)(2,1)S(1)}, u32[]{:S(2)}, u32[]{:S(2)}) async-start(bf16[128,3,4,128]{3,2,1,0:T(4,128)(2,1)} %bitcast.38), calls=%async_computation.1 | async-start | bytes 786432 | tf_op jit(solution)/shard_map/all_to_all | solution.py:348
  82.0 0.7 copy-start.16
  85.1 15.1 %all-to-all-start.2 = ((f32[128,1,384]{2,1,0:T(1,128)}), f32[128,1,384]{2,1,0:T(1,128)S(1)}, u32[]{:S(2)}, u32[]{:S(2)}) async-start(f32[128,1,384]{2,1,0:T(1,128)} %bitcast.48), calls=%async_computation.2 | async-start | bytes 393216 | tf_op jit(solution)/shard_map/all_to_all | solution.py:348
  100.2 0.7 copy-start.17
  (5 other events, 3.2 us)

commit v2 on v1

v2 whole, which is shorter than its diff:
```python
import jax
import jax.numpy as jnp
from jax import lax
from jax.experimental import pallas as pl
from jax.experimental.pallas import tpu as pltpu
from jax.sharding import PartitionSpec as P

F = 4
CELLS = 128
OCEAN = 32
STEPS = 4
TX, TY = 192, 96
GX, GY = 8, 16
DEV = GX * GY
PC = 384
CAP = 3
NB = 144
HALO = 4
ROWS_X = TX + 2 * HALO
WP = 32
WQ = 18
ROWS = 20
GROUP = 4 * ROWS
PROW = 256
LEFT = tuple(
    i for i in range(GX) if i < GX - 1 and (4 * (TX * i + TX + 2) - 11) // 26 + 1 - (4 * (TX * i - 3) - 11) // 26 >= WP
)
f32, bf16, i32 = jnp.float32, jnp.bfloat16, jnp.int32

diffuse_coef = 0.24
relax_coef = 0.3
drag_coefficient = 0.5


def iota(shape, dim):
    return lax.broadcasted_iota(i32, shape, dim)


def first_x(i):
    return (4 * (TX * i - 3) - 11) // 26


def first_y(j):
    return (4 * (TY * j - 3) - 11) // 26


def first_y_of(j):
    return ((4 * TY * j + 3) * 2521 >> 16) - 1


def first_x_of(i):
    return ((4 * TX * i + 3) * 2521 >> 16) - 1


def dot(a, b):
    return jnp.dot(a, b, preferred_element_type=f32)


def dot_nt(a, b):
    return lax.dot_general(a, b, (((1,), (1,)), ((), ())), preferred_element_type=f32)


def split3(x):
    high = x.astype(bf16)
    rest = x - high.astype(f32)
    mid = rest.astype(bf16)
    return high, mid, (rest - mid.astype(f32)).astype(bf16)


def column_of(row):
    n = row.shape[1]
    return jnp.sum(jnp.where(iota((n, n), 0) == iota((n, n), 1), row, 0), axis=1, keepdims=True)


def fetch(pairs, sems):
    copies = [pltpu.make_async_copy(src, dst, sems.at[k]) for k, (src, dst) in enumerate(pairs)]
    for copy in copies:
        copy.start()
    return copies


def rank_of(column, row, number):
    return jnp.sum(jnp.where((column == row) & (iota((NB, NB), 0) < number), 1, 0), axis=0, keepdims=True)


def by_thirds(column):
    at = iota((1, NB), 1)
    third = (at >= NB // CAP).astype(i32) + (at >= 2 * (NB // CAP)).astype(i32)
    number = CAP * (at - third * (NB // CAP)) + third
    return number, jnp.sum(jnp.where(iota((NB, NB), 0) == number, column, 0), axis=0, keepdims=True)


def pack_kernel(holder_ref, corner_ref, owner_any, place_any, parent_any, out_any, owner_ref, place_ref, parent_ref, z_ref, out_ref, sems):
    me = lax.axis_index("gx") * GY + lax.axis_index("gy")
    mine = me == holder_ref[0]
    cx, cy = corner_ref[0], corner_ref[1]
    base = pl.multiple_of(jnp.minimum(jnp.maximum(cx - 1, 0) // 16 * 16, PC - PROW), 16)
    small = fetch([(owner_any, owner_ref), (place_any, place_ref)], sems)
    tile = pltpu.make_async_copy(parent_any.at[:, pl.ds(base, PROW), :], parent_ref, sems.at[2])

    @pl.when(mine)
    def _():
        tile.start()

    for copy in small:
        copy.wait()
    owner = owner_ref[...]
    rank = rank_of(column_of(owner), owner, iota((NB, NB), 1))
    named = iota((DEV, NB), 0) == owner
    slots = jnp.zeros((DEV, CELLS), f32)
    for s in range(CAP):
        value = jnp.sum(jnp.where(named & (rank == s), place_ref[...] + 1, 0).astype(f32), axis=1, keepdims=True) - 1.0
        slots = jnp.where(iota((DEV, CELLS), 1) == s, value, slots)

    @pl.when(mine)
    def _():
        row = iota((GY * ROWS, 1), 0)
        j = row * 3277 >> 16
        r = row - j * ROWS
        wanted = jnp.where(r < WQ, cy + first_y_of(j) + r, -1)
        pick_y = (wanted == iota((GY * ROWS, PC), 1)).astype(f32).astype(bf16)
        tile.wait()
        parts = [parent_ref[f] for f in range(F)]
        across = jnp.concatenate([dot_nt(pick_y, parts[f]).astype(bf16) for f in range(F)], axis=1)
        lane = iota((1, 2 * CELLS), 1)
        for pair in range(GX // 2):
            first = jnp.where(lane < CELLS, first_x(2 * pair), first_x(2 * pair + 1))
            p = cx - base + first + (lane & (WP - 1))
            target = jnp.where((p >= 0) & (p < PROW), (lane >> 5 & 3) * PROW + p, -1)
            pick_x = (iota((F * PROW, 2 * CELLS), 0) == target).astype(f32).astype(bf16)
            window = dot(across, pick_x)
            for k in range(2):
                i = 2 * pair + k
                z_ref[pl.ds(i * GY * ROWS, GY * ROWS), :] = window[:, k * CELLS : (k + 1) * CELLS]
        j16 = iota((GY, PC), 0)
        q = iota((GY, PC), 1) - (cy + first_y_of(j16))
        inside = (q >= 0) & (q < WQ)
        lanes = iota((GY, CELLS), 1) >> 5
        erow = iota((8, PROW), 0)
        target = jnp.full((8, PROW), -1, i32)
        for k, i in enumerate(LEFT):
            target = jnp.where(erow == k, cx - base + first_x(i) + WP, target)
        pick_row = (target == iota((8, PROW), 1)).astype(f32).astype(bf16)
        left = [jnp.zeros((GY, CELLS), f32) for _ in LEFT]
        for f in range(F):
            rows = dot(pick_row, parts[f])
            for k in range(len(LEFT)):
                kept = jnp.where(inside, rows[k : k + 1, :], 0.0)
                folded = kept[:, :128] + kept[:, 128:256] + kept[:, 256:]
                folded = folded + pltpu.roll(folded, 64, 1)
                folded = folded + pltpu.roll(folded, 32, 1)
                left[k] = jnp.where(lanes == f, folded, left[k])
        for k, i in enumerate(LEFT):
            z_ref[pl.ds(i * GY * ROWS + WQ, GY, stride=ROWS), :] = left[k]

    @pl.when(jnp.logical_not(mine))
    def _():
        z_ref[...] = jnp.zeros_like(z_ref)

    z_ref[pl.ds(ROWS - 1, DEV, stride=ROWS), :] = slots
    out_ref[...] = z_ref[...].astype(bf16)
    done = pltpu.make_async_copy(out_ref, out_any, sems.at[3])
    done.start()
    done.wait()


def hat(fine, anchor, coarse):
    centre = (fine.astype(f32) + 0.5) * (2.0 / 13.0) - 0.5 + anchor.astype(f32)
    return jnp.maximum(0.0, 1.0 - jnp.abs(centre - coarse.astype(f32)))


def columns_kernel(s_ref, low_ref, high_ref, wide_ref):
    field = iota((TX, CELLS), 1) >> 2
    wide_ref[...] = jnp.zeros_like(wide_ref)
    low, high = jnp.zeros((TX, CELLS), f32), jnp.zeros((TX, CELLS), f32)
    for f in range(F):
        wide_ref[:, :TY] = s_ref[f]
        s = wide_ref[...]
        low = jnp.where(field == f, s if f == 0 else pltpu.roll(s, HALO * f, 1), low)
        high = jnp.where(field == f, pltpu.roll(s, CELLS - TY + HALO + HALO * f, 1), high)
    low_ref[...] = low
    high_ref[...] = high


def widened(s, left, right, f):
    lane = iota(s.shape, 1)
    before = left if f == 0 else pltpu.roll(left, CELLS - HALO * f, 1)
    after = pltpu.roll(right, TY + HALO - HALO * f, 1)
    wide = jnp.where(lane < TY + HALO, pltpu.roll(s, HALO, 1), after)
    return jnp.where(lane < HALO, before, jnp.where(lane < TY + 2 * HALO, wide, 0.0))


def rows_kernel(s_any, left_any, right_any, low_ref, high_ref, s_ref, left_ref, right_ref, wide_ref, sems):
    ends = ((0, 0), (8, TX - 8))
    pairs = [(s_any.at[:, pl.ds(src, 8), :], s_ref.at[:, pl.ds(dst, 8), :]) for dst, src in ends]
    pairs += [(left_any.at[pl.ds(src, 8), :], left_ref.at[pl.ds(dst, 8), :]) for dst, src in ends]
    pairs += [(right_any.at[pl.ds(src, 8), :], right_ref.at[pl.ds(dst, 8), :]) for dst, src in ends]
    for copy in fetch(pairs, sems):
        copy.wait()
    wide_ref[...] = jnp.zeros_like(wide_ref)
    for f in range(F):
        wide_ref[:, :TY] = s_ref[f]
        wide = widened(wide_ref[...], left_ref[...], right_ref[...], f)
        low_ref[f * HALO : (f + 1) * HALO, :] = wide[:HALO]
        high_ref[f * HALO : (f + 1) * HALO, :] = wide[16 - HALO :]


def nest_kernel(
    holder_ref, corner_ref, got_any, s_any, left_any, right_any, before_any, after_any, skin_any, owner_any,
    next_any, out_any,
    got_ref, s_ref, left_ref, right_ref, before_ref, after_ref, skin_ref, owner_ref, next_ref, out_ref,
    wx_ref, wide_ref, state_ref, force_ref, flux_ref, z_ref, sems,
):
    group = pl.multiple_of((holder_ref[0] >> 2) * GROUP, GROUP)
    pairs = [
        (owner_any, owner_ref), (got_any.at[pl.ds(group, GROUP), :], got_ref), (s_any, s_ref), (left_any, left_ref),
        (right_any, right_ref), (before_any, before_ref), (after_any, after_ref), (skin_any, skin_ref),
    ]
    copies = fetch(pairs, sems)
    ix, iy = lax.axis_index("gx"), lax.axis_index("gy")
    cx, cy = corner_ref[0], corner_ref[1]
    x0, y0 = ix * TX - HALO, iy * TY - HALO
    px, qy = cx + first_x_of(ix), cy + first_y_of(iy)
    lane = iota((ROWS_X, CELLS), 1)
    row = iota((ROWS_X, CELLS), 0)
    weight = hat(row + x0, cx, (lane & (WP - 1)) + px)
    for f in range(F):
        wx_ref[f * ROWS_X : (f + 1) * ROWS_X, :] = jnp.where(lane >> 5 == f, weight, 0.0).astype(bf16)
    weight_last = relax_coef * hat(row + x0, cx, jnp.full_like(row, WP) + px).astype(bf16).astype(f32)
    inside = (row + x0 >= 0) & (row + x0 < GX * TX) & (lane + y0 >= 0) & (lane + y0 < GY * TY)
    mask = jnp.where(inside, 1.0, 0.0)
    at = iota((CELLS, GROUP), 1) - (holder_ref[0] & 3) * ROWS
    weight_y = jnp.where((at >= 0) & (at < WQ), hat(iota((CELLS, GROUP), 0) + y0, cy, at + qy), 0.0).astype(bf16)
    lane = iota((CELLS, CELLS), 1)
    weight_c = hat(iota((CELLS, CELLS), 0) + y0, cy, qy + ((lane - qy) & (WP - 1))).astype(bf16)
    wide_ref[...] = jnp.zeros_like(wide_ref)
    flux_ref[...] = jnp.zeros_like(flux_ref)
    copies[0].wait()
    column = column_of(owner_ref[...])
    number, owner = by_thirds(column)
    send = (iota((CAP * DEV, NB), 0) == rank_of(column, owner, number) * DEV + owner).astype(f32).astype(bf16)
    copies[1].wait()
    got = got_ref[...]
    partial = dot(weight_y, got).astype(bf16)
    last = jnp.sum(
        jnp.where(iota((GROUP, CELLS), 0) == (holder_ref[0] & 3) * ROWS + WQ, got.astype(f32), 0.0), axis=0, keepdims=True
    )
    last = jnp.where(iota((8, CELLS), 1) >> 5 == iota((8, CELLS), 0), last, 0.0).astype(bf16)
    partial_last = dot_nt(last, weight_c).astype(bf16).astype(f32)
    force_ref[...] = dot_nt(wx_ref[...], partial)
    for copy in copies[2:]:
        copy.wait()
    left, right = left_ref[...], right_ref[...]
    written = []
    for f in range(F):
        force = relax_coef * force_ref[f * ROWS_X : (f + 1) * ROWS_X, :] + weight_last * partial_last[f : f + 1, :]
        wide_ref[:, :TY] = s_ref[f]
        state_ref[:HALO, :] = before_ref[f * HALO : (f + 1) * HALO, :]
        state_ref[HALO : HALO + TX, :] = widened(wide_ref[...], left, right, f)
        state_ref[HALO + TX :, :] = after_ref[f * HALO : (f + 1) * HALO, :]
        s = state_ref[...]
        for _ in range(STEPS):
            beside = (
                pltpu.roll(s, 1, 0) + pltpu.roll(s, ROWS_X - 1, 0) + pltpu.roll(s, 1, 1) + pltpu.roll(s, CELLS - 1, 1)
            )
            s = mask * ((1.0 - 4.0 * diffuse_coef - relax_coef) * s + diffuse_coef * beside + force)
        state_ref[...] = pltpu.roll(s, CELLS - HALO, 1)
        next_ref[f] = state_ref[HALO : HALO + TX, :TY]
        written.append(pltpu.make_async_copy(next_ref.at[f], next_any.at[f], sems.at[len(pairs) + f]))
        written[f].start()
    u, v, ta, qa = next_ref[0], next_ref[1], next_ref[2], next_ref[3]
    half = drag_coefficient * jnp.sqrt(1.0 + u * u + v * v)
    skin = skin_ref[...]
    flux = (half * (ta - skin), half * (qa - 0.5 * skin), half * u, half * v)
    rows = NB // CAP
    lane = iota((rows, CELLS), 1)
    blocks = []
    for f in range(F):
        flux_ref[:, :TY] = flux[f]
        m = [flux_ref[pl.ds(k, rows, stride=4), :] for k in range(4)]
        r1, r2, r3 = pltpu.roll(m[1], 96, 1), pltpu.roll(m[2], 64, 1), pltpu.roll(m[3], 32, 1)
        blocks.append(
            jnp.concatenate(
                [jnp.where(lane < 96, m[0], r1), jnp.where(lane < 64, r1, r2), jnp.where(lane < 32, r2, r3)], axis=0
            ).astype(bf16)
        )
    sent = dot(send, jnp.concatenate(blocks, axis=1))
    for slot in range(CAP):
        for f in range(F):
            z_ref[pl.ds(slot * F + f, DEV, stride=CAP * F), :] = sent[
                slot * DEV : (slot + 1) * DEV, f * CELLS : (f + 1) * CELLS
            ]
    out_ref[...] = z_ref[...].astype(bf16)
    written.append(pltpu.make_async_copy(out_ref, out_any, sems.at[len(pairs) + F]))
    written[F].start()
    for copy in written:
        copy.wait()


def hot_kernel(got_any, kept_any, hot_ref, give_ref, inverse_ref, cover_ref, got_ref, kept_ref, z_ref, slot_ref, row_ref, sems):
    copies = fetch([(got_any, got_ref), (kept_any, kept_ref)], sems)
    for copy in copies:
        copy.wait()
    slot_ref[...] = got_ref[...].astype(f32)
    slots = slot_ref[pl.ds(ROWS - 1, DEV, stride=ROWS), :].astype(i32)
    lane = iota((DEV, OCEAN * F), 1)
    for s in range(CAP):
        target = slots[:, s : s + 1] * F
        for f in range(F):
            z_ref[pl.ds(s * F + f, DEV, stride=CAP * F), :] = (lane == jnp.where(target < 0, -1, target + f)).astype(f32)
        row_ref[pl.ds(s, DEV, stride=CAP), :] = (lane == target).astype(f32)
    give_ref[...] = row_ref[...].astype(bf16)
    hot = jnp.swapaxes(z_ref[...], 0, 1)
    hot_ref[...] = hot.astype(bf16)
    count = jnp.sum(hot, axis=1, keepdims=True)
    inverse_ref[...] = jnp.broadcast_to(1.0 / jnp.maximum(count, 1.0), (OCEAN * F, CELLS))
    cover_ref[...] = jnp.where(count == 0.0, kept_ref[...], 0.0)


def top_kernel(scale_ref, marine_ref, out_ref):
    total = scale_ref[0, 0] * marine_ref[0]
    for k in range(1, marine_ref.shape[0]):
        total = total + scale_ref[0, k] * marine_ref[k]
    out_ref[: OCEAN * F, :] = total
    out_ref[OCEAN * F :, :] = jnp.full((8, CELLS), scale_ref[0, 0], f32)


def ocean_kernel(
    got_any, hot_any, inverse_any, cover_any, top_any, give_any, forcing_any, out_any,
    got_ref, hot_ref, inverse_ref, cover_ref, top_ref, give_ref, forcing_ref, out_ref, sems,
):
    pairs = [
        (hot_any, hot_ref), (got_any, got_ref), (inverse_any, inverse_ref), (cover_any, cover_ref), (top_any, top_ref),
        (give_any, give_ref),
    ]
    for copy in fetch(pairs, sems):
        copy.wait()
    forcing = dot(hot_ref[...], got_ref[...]) * inverse_ref[...] + cover_ref[...]
    forcing_ref[...] = forcing
    top = top_ref[: OCEAN * F, :] + top_ref[OCEAN * F : OCEAN * F + 1, :] * forcing
    back = dot(give_ref[...], jnp.concatenate(split3(top), axis=1))
    out_ref[...] = back[:, :CELLS] + back[:, CELLS : 2 * CELLS] + back[:, 2 * CELLS :]
    a = pltpu.make_async_copy(out_ref, out_any, sems.at[0])
    b = pltpu.make_async_copy(forcing_ref, forcing_any, sems.at[1])
    a.start()
    b.start()
    a.wait()
    b.wait()


def mix_kernel(scale_ref, forcing_ref, marine_ref, out_ref, high_ref, low_ref):
    layers = marine_ref.shape[0]
    n = 8 * layers

    @pl.when(pl.program_id(0) == 0)
    def _():
        spread = (iota((n, layers), 0) >> 3 == iota((n, layers), 1)).astype(f32).astype(bf16)
        same = (iota((n, n), 0) & 7) == (iota((n, n), 1) & 7)
        scale = scale_ref[...]
        high = scale.astype(bf16)
        low = (scale - high.astype(f32)).astype(bf16)
        for part, ref in ((high, high_ref), (low, low_ref)):
            wide = dot_nt(dot(spread, part).astype(bf16), spread)
            ref[...] = jnp.where(same, wide, 0.0).astype(bf16)

    groups = marine_ref.shape[1] // 8
    columns = []
    for g in range(groups):
        x = marine_ref[:, 8 * g : 8 * g + 8, :].reshape(n, CELLS)
        first = x[:8] + forcing_ref[8 * g : 8 * g + 8, :]
        columns.append(jnp.concatenate([first, x[8:]], axis=0))
    x = jnp.concatenate(columns, axis=1)
    high = x.astype(bf16)
    low = (x - high.astype(f32)).astype(bf16)
    y = dot(high_ref[...], high) + (dot(high_ref[...], low) + dot(low_ref[...], high))
    for g in range(groups):
        out_ref[:, 8 * g : 8 * g + 8, :] = y[:, g * CELLS : (g + 1) * CELLS].reshape(layers, 8, CELLS)


def skin_kernel(got_any, owner_any, out_ref, got_ref, owner_ref, tile_ref, sems):
    copies = fetch([(owner_any, owner_ref), (got_any, got_ref)], sems)
    copies[0].wait()
    column = column_of(owner_ref[...])
    number, owner = by_thirds(column)
    source = column_of(owner * CAP + rank_of(column, owner, number))
    back = (source == iota((NB, CAP * DEV), 1)).astype(f32).astype(bf16)
    copies[1].wait()
    x = dot(back, jnp.concatenate(split3(got_ref[...]), axis=1))
    x = x[:, :CELLS] + x[:, CELLS : 2 * CELLS] + x[:, 2 * CELLS :]
    rows = NB // CAP
    t0, t1, t2 = x[:rows], x[rows : 2 * rows], x[2 * rows :]
    lane = iota((rows, CELLS), 1)
    tile_ref[pl.ds(0, rows, stride=4), :] = t0
    tile_ref[pl.ds(1, rows, stride=4), :] = pltpu.roll(jnp.where(lane < 64, t1, t0), 32, 1)
    tile_ref[pl.ds(2, rows, stride=4), :] = pltpu.roll(jnp.where(lane < 32, t2, t1), 64, 1)
    tile_ref[pl.ds(3, rows, stride=4), :] = pltpu.roll(t2, 96, 1)
    out_ref[...] = tile_ref[:, :TY]


SPACES = {
    "s": pl.BlockSpec(memory_space=pltpu.SMEM),
    "v": pl.BlockSpec(memory_space=pltpu.VMEM),
    "h": pl.BlockSpec(memory_space=pltpu.HBM),
    "a": pl.BlockSpec(memory_space=pl.ANY),
}


def call(kernel, ins, outs, args, shapes, scratch=(), copies=0):
    return pl.pallas_call(
        kernel,
        out_shape=tuple(jax.ShapeDtypeStruct(s, d) for s, d in shapes),
        in_specs=[SPACES[c] for c in ins],
        out_specs=tuple(SPACES[c] for c in outs),
        scratch_shapes=[pltpu.VMEM(s, d) for s, d in scratch] + ([pltpu.SemaphoreType.DMA((copies,))] if copies else []),
        compiler_params=pltpu.CompilerParams(vmem_limit_bytes=40 << 20),
    )(*args)


def shift(value, axis, by):
    n = lax.axis_size(axis)
    return lax.ppermute(value, axis, [(i, i + by) for i in range(n) if 0 <= i + by < n])


def exchange(value, rows):
    split = value.reshape(rows)
    return lax.all_to_all(split, ("gx", "gy"), split_axis=0, concat_axis=0, tiled=True).reshape(value.shape)


def by_block(value):
    return value.reshape(F, OCEAN, CELLS).transpose(1, 0, 2).reshape(OCEAN * F, CELLS)


def on_device(
    fine_atmospheric_values,
    fine_skin_heat,
    coarse_lowest_values,
    holder_flat,
    corner_offset,
    exchange_patch_holder,
    holder_patch_position,
    coarse_interface_exchange,
    marine_stratum_values,
    diffusion_solver_operator,
):
    owner = exchange_patch_holder.reshape(1, NB)
    place = holder_patch_position.reshape(1, NB)
    names, message = ((1, NB), i32), ((DEV * ROWS, CELLS), bf16)
    (windows,) = call(
        pack_kernel, "ssaaa", "h", (holder_flat, corner_offset, owner, place, coarse_lowest_values), (message,),
        (names, names, ((F, PROW, PC), bf16), ((DEV * ROWS, CELLS), f32), message), 4,
    )
    got = exchange(windows, (DEV, ROWS // 4, 4, CELLS))
    present, windows = lax.optimization_barrier((fine_atmospheric_values, windows))
    strip = ((TX, CELLS), f32)
    low, high = call(columns_kernel, "v", "vv", (present,), (strip, strip), (strip,))
    left, right = shift(high, "gy", 1), shift(low, "gy", -1)
    ends, strip16 = ((F * HALO, CELLS), f32), ((16, CELLS), f32)
    low, high = call(
        rows_kernel, "aaa", "vv", (present, left, right), (ends, ends), (((F, 16, TY), f32), strip16, strip16, strip16), 6
    )
    before, after = shift(high, "gx", 1), shift(low, "gx", -1)
    tile, sent = ((F, TX, TY), f32), ((DEV * CAP * F, CELLS), bf16)
    nest_next, flux = call(
        nest_kernel, "ssaaaaaaaa", "hh",
        (holder_flat, corner_offset, got, present, left, right, before, after, fine_skin_heat, owner), (tile, sent),
        (
            ((GROUP, CELLS), bf16), tile, strip, strip, ends, ends, ((TX, TY), f32), names, tile, sent,
            ((F * ROWS_X, CELLS), bf16), strip, ((ROWS_X, CELLS), f32), ((F * ROWS_X, CELLS), f32), strip,
            ((DEV * CAP * F, CELLS), f32),
        ), 13,
    )
    got_flux = exchange(flux, (DEV, CAP, F, CELLS))
    layers = marine_stratum_values.shape[1]
    marine = marine_stratum_values.reshape(F, layers, OCEAN, CELLS).transpose(1, 2, 0, 3).reshape(layers, OCEAN * F, CELLS)
    marine_late, got_late, flux = lax.optimization_barrier((marine, got, flux))
    block = ((OCEAN * F, CELLS), f32)
    hot, give = ((OCEAN * F, DEV * CAP * F), bf16), ((DEV * CAP, OCEAN * F), bf16)
    hot, give, inverse, cover = call(
        hot_kernel, "aa", "vvvv", (got_late, by_block(coarse_interface_exchange)), (hot, give, block, block),
        (
            message, block, ((DEV * CAP * F, OCEAN * F), f32), ((DEV * ROWS, CELLS), f32), ((DEV * CAP, OCEAN * F), f32),
        ), 2,
    )
    (top,) = call(top_kernel, "sv", "v", (diffusion_solver_operator, marine_late), (((OCEAN * F + 8, CELLS), f32),))
    returned = ((DEV * CAP, CELLS), f32)
    forcing, back = call(
        ocean_kernel, "aaaaaa", "hh", (got_flux, hot, inverse, cover, top, give), (block, returned),
        (
            sent, ((OCEAN * F, DEV * CAP * F), bf16), block, block, ((OCEAN * F + 8, CELLS), f32),
            ((DEV * CAP, OCEAN * F), bf16), block, returned,
        ), 6,
    )
    arrived = exchange(back, (DEV, 1, CAP * CELLS))
    part = 32
    refreshed = pl.pallas_call(
        mix_kernel,
        out_shape=jax.ShapeDtypeStruct((layers, OCEAN * F, CELLS), f32),
        grid=(OCEAN * F // part,),
        in_specs=[
            pl.BlockSpec((layers, layers), lambda g: (0, 0)),
            pl.BlockSpec((part, CELLS), lambda g: (g, 0)),
            pl.BlockSpec((layers, part, CELLS), lambda g: (0, g, 0)),
        ],
        out_specs=pl.BlockSpec((layers, part, CELLS), lambda g: (0, g, 0)),
        scratch_shapes=[pltpu.VMEM((8 * layers, 8 * layers), bf16)] * 2,
        compiler_params=pltpu.CompilerParams(vmem_limit_bytes=40 << 20),
    )(diffusion_solver_operator, forcing, marine)
    refreshed = refreshed.reshape(layers, OCEAN, F, CELLS).transpose(2, 0, 1, 3).reshape(marine_stratum_values.shape)
    (skin,) = call(
        skin_kernel, "aa", "v", (arrived, owner), (((TX, TY), f32),), (returned, names, ((TX, CELLS), f32)), 2
    )
    return (nest_next, refreshed, skin)


def solution(mesh):
    in_specs = (
        P(None, "gx", "gy"),
        P("gx", "gy"),
        P(None, "gx", "gy"),
        P(),
        P(),
        P(("gx", "gy"), None),
        P(("gx", "gy")),
        P(None, ("gx", "gy")),
        P(None, None, ("gx", "gy")),
        P(),
    )
    out_specs = (P(None, "gx", "gy"), P(None, None, ("gx", "gy")), P("gx", "gy"))
    return jax.shard_map(
        on_device, mesh=mesh, in_specs=in_specs, out_specs=out_specs, check_vma=False
    )
```

time: 104 us -> 91.6 us (0.88)
  local copies, waits for them, and re-layouts: 21.8 us -> 13.8 us
  other arithmetic: 6.23 us -> 0 us
  matrix products: 5.94 us -> 0 us
  waiting for transfers between devices: 16.6 us -> 22.5 us
  Pallas kernels: 13.8 us -> 16.9 us
    ppermute x4, waiting for transfers between devices: 0.01 us -> 8.89 us  [shift(): lax.ppermute(value, axis, [(i, i + by) for i in range(n) if 0 <= i + by <...]
    dot_general x1 -> x0, matrix products: 5.94 us -> none  [on_device(): jnp.einsum('lk,kfc->lfc', diffusion_solver_operator, marine, precision=la...]
    add x2 -> x0, other arithmetic: 3.11 us -> none  [the longest x1 2.31 us: on_device(): base + diffusion_solver_operator[:, 0][:, None, None] * cells[None]]
    pallas_call x7 -> x9, Pallas kernels: 13.8 us -> 16.9 us  [the longest x8 12.3 us: call(): pl.pallas_call(kernel, out_shape=tuple((jax.ShapeDtypeStruct(s, d) for s,...]
    unnamed x46 -> x42, local copies, waits for them, and re-layouts: 16.8 us -> 13.8 us
    all_to_all x3, waiting for transfers between devices: 16.6 us -> 13.7 us  [exchange(): lax.all_to_all(split, ('gx', 'gy'), split_axis=0, concat_axis=0, tiled=True)]
    convert_element_type x3 -> x0, other arithmetic: 1.57 us -> none  [the longest x1 0.81 us: on_device(): hot.astype(bf16)]
    slice x2 -> x0, local copies, waits for them, and re-layouts: 1.18 us -> none  [the longest x1 1.08 us: on_device(): base[0]]
  transfers between devices with their start and end apart: 7 -> 7, of which waited for: 2 -> 5; matrix products, arithmetic and copies ran while one was open for 20% -> 0% of each run, Pallas kernels for 6% -> 8%
where the time goes in v2:
time: 91.6 us; the launch traced here: 90.8 us
  starting transfers between devices  36.1 us (39%)
  waiting for transfers between devices  22.5 us (25%)
  Pallas kernels  16.9 us (18%)
  local copies, waits for them, and re-layouts  13.8 us (15%)
  between operations  1.51 us (2%)
    all_to_all x3, starting transfers between devices, exchange(): lax.all_to_all(split, ('gx', 'gy'), split_axis=0, concat_axis=0, tiled=True)  26.1 us
    unnamed x42, local copies, waits for them, and re-layouts  13.8 us
    all_to_all x3, waiting for transfers between devices, exchange(): lax.all_to_all(split, ('gx', 'gy'), split_axis=0, concat_axis=0, tiled=True)  13.7 us
    pallas_call x8, Pallas kernels, call(): pl.pallas_call(kernel, out_shape=tuple((jax.ShapeDtypeStruct(s, d) for s,...  12.3 us
    ppermute x4, starting transfers between devices, shift(): lax.ppermute(value, axis, [(i, i + by) for i in range(n) if 0 <= i + by <...  9.94 us
    ppermute x4, waiting for transfers between devices, shift(): lax.ppermute(value, axis, [(i, i + by) for i in range(n) if 0 <= i + by <...  8.89 us
    pallas_call x1, Pallas kernels, on_device(): pl.pallas_call(mix_kernel, out_shape=jax.ShapeDtypeStruct((layers, OCEAN...  4.55 us
  transfers between devices with their start and end apart: 7, of which 5 were waited for; matrix products, arithmetic and copies ran while one was open for 0% of the time, Pallas kernels for 8%

profile of v2, /device:TPU:1, one launch (start us, length us, event | category | flops | bytes accessed | tf_op | source)
XLA Modules:
  0.0 90.8 jit_solution(14886345348579840557)
XLA Ops:
  1.3 1.3 %copy-done.4 = bf16[4,384,384]{2,1,0:T(8,128)(2,1)S(1)} copy-done((bf16[4,384,384]{2,1,0:T(8,128)(2,1)S(1)}, bf16[4,384,384]{2,1,0:T(8,128)(2,1)}, u32[]{:S(2)}) %copy-start.4) | copy-done | bytes 1179672
  4.6 1.2 %shard_map.121 = bf16[2560,128]{1,0:T(8,128)(2,1)S(1)} custom-call(s32[1]{0:T(128)S(6)} %copy.20.holder_ref, s32[2]{0:T(128)S(1)} %copy-done.18, s32[1,144]{1,0:T(1,128)S(1)} %bitcast.31, s32[1,144]{1,0:T(1,128)S(1)} %bitcast.34, bf16[4,384,384]{2,1,0:T(8,128)(2,1)S(1)} %copy-done.4), custom_call_target="tpu_custom_call" | custom-call | tf_op jit(solution)/shard_map/pallas_call | solution.py:409
  6.7 11.5 %all-to-all-start = ((bf16[128,5,4,128]{3,2,1,0:T(4,128)(2,1)}), bf16[128,5,4,128]{3,2,1,0:T(4,128)(2,1)S(1)}, u32[]{:S(2)}, u32[]{:S(2)}) async-start(bf16[128,5,4,128]{3,2,1,0:T(4,128)(2,1)} %bitcast.27), calls=%async_computation | async-start | bytes 1310720 | tf_op jit(solution)/shard_map/all_to_all | solution.py:426
  18.2 1.0 %copy-done.1 = f32[4,192,96]{2,1,0:T(8,128)S(1)} copy-done((f32[4,192,96]{2,1,0:T(8,128)S(1)}, f32[4,192,96]{2,1,0:T(8,128)}, u32[]{:S(2)}) %copy-start.1) | copy-done | bytes 294936
  19.4 3.3 %collective-permute-start = (f32[192,128]{1,0:T(8,128)S(1)}, f32[192,128]{1,0:T(8,128)S(1)}, u32[]{:S(2)}, u32[]{:S(2)}) collective-permute-start(f32[192,128]{1,0:T(8,128)S(1)} %get-tuple-element.19), channel_id=1, source_target_pairs={{0,1},{1,2},{2,3},{3,4},{4,5},{5,6},{6,7},{7,8},{8,9},{9,10},{10,1... | collective-permute-start | bytes 294920 | tf_op jit(solution)/shard_map/ppermute | solution.py:421
  22.8 1.3 %collective-permute-start.1 = (f32[192,128]{1,0:T(8,128)S(1)}, f32[192,128]{1,0:T(8,128)S(1)}, u32[]{:S(2)}, u32[]{:S(2)}) collective-permute-start(f32[192,128]{1,0:T(8,128)S(1)} %get-tuple-element.20), channel_id=1, source_target_pairs={{1,0},{2,1},{3,2},{4,3},{5,4},{6,5},{7,6},{8,7},{9,8},{10,9},{11,1... | collective-permute-start | bytes 294920 | tf_op jit(solution)/shard_map/ppermute | solution.py:421
  24.1 3.8 %collective-permute-done.left_any = f32[192,128]{1,0:T(8,128)S(1)} collective-permute-done((f32[192,128]{1,0:T(8,128)S(1)}, f32[192,128]{1,0:T(8,128)S(1)}, u32[]{:S(2)}, u32[]{:S(2)}) %collective-permute-start) | collective-permute-done | bytes 98336 | tf_op jit(solution)/shard_map/ppermute | solution.py:421
  27.9 2.0 %collective-permute-done.1.right_any = f32[192,128]{1,0:T(8,128)S(1)} collective-permute-done((f32[192,128]{1,0:T(8,128)S(1)}, f32[192,128]{1,0:T(8,128)S(1)}, u32[]{:S(2)}, u32[]{:S(2)}) %collective-permute-start.1) | collective-permute-done | bytes 98336 | tf_op jit(solution)/shard_map/ppermute | solution.py:421
  30.1 3.4 %collective-permute-start.2 = (f32[16,128]{1,0:T(8,128)S(1)}, f32[16,128]{1,0:T(8,128)S(1)}, u32[]{:S(2)}, u32[]{:S(2)}) collective-permute-start(f32[16,128]{1,0:T(8,128)S(1)} %get-tuple-element.21), channel_id=1, source_target_pairs={{0,16},{16,32},{32,48},{48,64},{64,80},{80,96},{96,112},{1,17},{17... | collective-permute-start | bytes 24584 | tf_op jit(solution)/shard_map/ppermute | solution.py:421
  33.5 1.9 %collective-permute-start.3 = (f32[16,128]{1,0:T(8,128)S(1)}, f32[16,128]{1,0:T(8,128)S(1)}, u32[]{:S(2)}, u32[]{:S(2)}) collective-permute-start(f32[16,128]{1,0:T(8,128)S(1)} %get-tuple-element.22), channel_id=1, source_target_pairs={{16,0},{32,16},{48,32},{64,48},{80,64},{96,80},{112,96},{17,1},{33... | collective-permute-start | bytes 24584 | tf_op jit(solution)/shard_map/ppermute | solution.py:421
  35.5 3.0 %collective-permute-done.3.after_any = f32[16,128]{1,0:T(8,128)S(1)} collective-permute-done((f32[16,128]{1,0:T(8,128)S(1)}, f32[16,128]{1,0:T(8,128)S(1)}, u32[]{:S(2)}, u32[]{:S(2)}) %collective-permute-start.3) | collective-permute-done | bytes 8224 | tf_op jit(solution)/shard_map/ppermute | solution.py:421
  39.1 1.0 %copy-done.2 = f32[4,192,96]{2,1,0:T(8,128)S(1)} copy-done((f32[4,192,96]{2,1,0:T(8,128)S(1)}, f32[4,192,96]{2,1,0:T(8,128)}, u32[]{:S(2)}) %copy-start.2) | copy-done | bytes 294936
  40.1 0.9 copy-done.10
  41.7 4.6 %shard_map.124 = (f32[4,192,96]{2,1,0:T(8,128)}, bf16[1536,128]{1,0:T(8,128)(2,1)S(1)}) custom-call(s32[1]{0:T(128)S(6)} %copy.20.holder_ref, s32[2]{0:T(128)S(1)} %copy-done.19, bf16[2560,128]{1,0:T(8,128)(2,1)S(1)} %bitcast.25, f32[4,192,96]{2,1,0:T(8,128)S(1)} %copy-done.2, f32[192,128]{1,0:T(8,128)S(1)} %collective-permute-done.left_any, ...), custom_call_target="tpu_custom_call" | custom-call | tf_op jit(solution)/shard_map/pallas_call | solution.py:409
  47.1 10.6 %all-to-all-start.1 = ((bf16[128,3,4,128]{3,2,1,0:T(4,128)(2,1)}), bf16[128,3,4,128]{3,2,1,0:T(4,128)(2,1)}, u32[]{:S(2)}, u32[]{:S(2)}) async-start(bf16[128,3,4,128]{3,2,1,0:T(4,128)(2,1)} %bitcast.29), calls=%async_computation.1 | async-start | bytes 786432 | tf_op jit(solution)/shard_map/all_to_all | solution.py:426
  58.6 1.0 %shard_map.125 = (bf16[128,1536]{1,0:T(8,128)(2,1)S(1)}, bf16[384,128]{1,0:T(8,128)(2,1)S(1)}, f32[128,128]{1,0:T(8,128)S(1)}, f32[128,128]{1,0:T(8,128)S(1)}) custom-call(bf16[2560,128]{1,0:T(8,128)(2,1)S(1)} %bitcast.26, f32[128,128]{1,0:T(8,128)S(1)} %bitcast.30), custom_call_target="tpu_custom_call" | custom-call | tf_op jit(solution)/shard_map/pallas_call | solution.py:409
  61.7 1.1 %shard_map.126.top_any = f32[136,128]{1,0:T(8,128)S(1)} custom-call(f32[41,41]{1,0:T(8,128)S(1)} %copy-done.8, f32[41,128,128]{2,1,0:T(8,128)S(1)} %bitcast.23), custom_call_target="tpu_custom_call" | custom-call | tf_op jit(solution)/shard_map/pallas_call | solution.py:409
  62.9 7.3 %all-to-all-done.1 = bf16[128,3,4,128]{3,2,1,0:T(4,128)(2,1)} async-done(((bf16[128,3,4,128]{3,2,1,0:T(4,128)(2,1)}), bf16[128,3,4,128]{3,2,1,0:T(4,128)(2,1)}, u32[]{:S(2)}, u32[]{:S(2)}) %all-to-all-start.1) | async-done | bytes 393248 | tf_op jit(solution)/shard_map/all_to_all | solution.py:426
  70.2 1.0 %copy-done.7 = bf16[128,1536]{1,0:T(8,128)(2,1)S(1)} copy-done((bf16[128,1536]{1,0:T(8,128)(2,1)S(1)}, bf16[128,1536]{1,0:T(8,128)(2,1)}, u32[]{:S(2)}) %copy-start.7) | copy-done | bytes 393240
  72.0 2.4 %shard_map.127 = (f32[128,128]{1,0:T(8,128)S(1)}, f32[384,128]{1,0:T(8,128)}) custom-call(bf16[1536,128]{1,0:T(8,128)(2,1)} %bitcast.5.got_any, bf16[128,1536]{1,0:T(8,128)(2,1)S(1)} %copy-done.7, f32[128,128]{1,0:T(8,128)S(1)} %get-tuple-element.27.inverse_any, f32[128,128]{1,0:T(8,128)S(1)} %copy-done.12, f32[136,128]{1,0:T(8,128)S(1)} %shard_map.126.top_any, ...), custom_call_target="tpu_custom_call" | custom-call | tf_op jit(solution)/shard_map/pallas_call | solution.py:409
  74.4 4.0 %all-to-all-start.2 = ((f32[128,1,384]{2,1,0:T(1,128)}), f32[128,1,384]{2,1,0:T(1,128)S(1)}, u32[]{:S(2)}, u32[]{:S(2)}) async-start(f32[128,1,384]{2,1,0:T(1,128)} %bitcast.15), calls=%async_computation.2 | async-start | bytes 393216 | tf_op jit(solution)/shard_map/all_to_all | solution.py:426
  78.4 4.6 %shard_map.128 = f32[41,128,128]{2,1,0:T(8,128)} custom-call(f32[41,41]{1,0:T(8,128)S(1)} %copy-done.9, f32[128,128]{1,0:T(8,128)S(1)} %get-tuple-element.31.forcing_ref, f32[41,128,128]{2,1,0:T(8,128)S(1)} %bitcast.24), custom_call_target="tpu_custom_call" | custom-call | tf_op jit(solution)/shard_map/pallas_call | solution.py:495
  83.0 6.3 %all-to-all-done.2 = f32[128,1,384]{2,1,0:T(1,128)S(1)} async-done(((f32[128,1,384]{2,1,0:T(1,128)}), f32[128,1,384]{2,1,0:T(1,128)S(1)}, u32[]{:S(2)}, u32[]{:S(2)}) %all-to-all-start.2) | async-done | bytes 196640 | tf_op jit(solution)/shard_map/all_to_all | solution.py:426
  89.3 1.5 %shard_map.129 = f32[192,96]{1,0:T(8,128)} custom-call(f32[384,128]{1,0:T(8,128)S(1)} %bitcast.28, s32[1,144]{1,0:T(1,128)S(1)} %bitcast.33), custom_call_target="tpu_custom_call" | custom-call | tf_op jit(solution)/shard_map/pallas_call | solution.py:409
  (41 shorter events, 9.1 us)
Async XLA Ops:
  0.6 38.5 %copy-start.19 = (s32[2]{0:T(128)S(1)}, s32[2]{0:T(128)}, u32[]{:S(2)}) copy-start(s32[2]{0:T(128)} %corner_ref.3) | copy-start | bytes 28
  0.6 38.5 %copy-start.15 = (s32[144,1]{0,1:T(1,128)S(1)}, s32[144,1]{0,1:T(1,128)}, u32[]{:S(2)}) copy-start(s32[144,1]{0,1:T(1,128)} %param.15) | copy-start | bytes 1732
  1.3 1.3 %copy-start.4 = (bf16[4,384,384]{2,1,0:T(8,128)(2,1)S(1)}, bf16[4,384,384]{2,1,0:T(8,128)(2,1)}, u32[]{:S(2)}) copy-start(bf16[4,384,384]{2,1,0:T(8,128)(2,1)} %parent_any.1) | copy-start | bytes 3538948
  2.6 0.7 copy-start.14
  5.8 0.8 copy-start.3
  6.7 54.3 %copy-start = (f32[4,41,4096]{2,0,1:T(4,128)S(1)}, f32[4,41,4096]{2,0,1:T(4,128)}, u32[]{:S(2)}) copy-start(f32[4,41,4096]{2,0,1:T(4,128)} %param.18) | copy-start | bytes 8060932
  6.7 32.4 %all-to-all-start = ((bf16[128,5,4,128]{3,2,1,0:T(4,128)(2,1)}), bf16[128,5,4,128]{3,2,1,0:T(4,128)(2,1)S(1)}, u32[]{:S(2)}, u32[]{:S(2)}) async-start(bf16[128,5,4,128]{3,2,1,0:T(4,128)(2,1)} %bitcast.27), calls=%async_computation | async-start | bytes 1310720 | tf_op jit(solution)/shard_map/all_to_all | solution.py:426
  18.2 1.0 %copy-start.1 = (f32[4,192,96]{2,1,0:T(8,128)S(1)}, f32[4,192,96]{2,1,0:T(8,128)}, u32[]{:S(2)}) copy-start(f32[4,192,96]{2,1,0:T(8,128)} %s_any.1) | copy-start | bytes 884740
  19.4 8.4 %collective-permute-start = (f32[192,128]{1,0:T(8,128)S(1)}, f32[192,128]{1,0:T(8,128)S(1)}, u32[]{:S(2)}, u32[]{:S(2)}) collective-permute-start(f32[192,128]{1,0:T(8,128)S(1)} %get-tuple-element.19), channel_id=1, source_target_pairs={{0,1},{1,2},{2,3},{3,4},{4,5},{5,6},{6,7},{7,8},{8,9},{9,10},{10,1... | collective-permute-start | bytes 294920 | tf_op jit(solution)/shard_map/ppermute | solution.py:421
  22.8 7.2 %collective-permute-start.1 = (f32[192,128]{1,0:T(8,128)S(1)}, f32[192,128]{1,0:T(8,128)S(1)}, u32[]{:S(2)}, u32[]{:S(2)}) collective-permute-start(f32[192,128]{1,0:T(8,128)S(1)} %get-tuple-element.20), channel_id=1, source_target_pairs={{1,0},{2,1},{3,2},{4,3},{5,4},{6,5},{7,6},{8,7},{9,8},{10,9},{11,1... | collective-permute-start | bytes 294920 | tf_op jit(solution)/shard_map/ppermute | solution.py:421
  30.1 5.4 %collective-permute-start.2 = (f32[16,128]{1,0:T(8,128)S(1)}, f32[16,128]{1,0:T(8,128)S(1)}, u32[]{:S(2)}, u32[]{:S(2)}) collective-permute-start(f32[16,128]{1,0:T(8,128)S(1)} %get-tuple-element.21), channel_id=1, source_target_pairs={{0,16},{16,32},{32,48},{48,64},{64,80},{80,96},{96,112},{1,17},{17... | collective-permute-start | bytes 24584 | tf_op jit(solution)/shard_map/ppermute | solution.py:421
  33.5 5.0 %collective-permute-start.3 = (f32[16,128]{1,0:T(8,128)S(1)}, f32[16,128]{1,0:T(8,128)S(1)}, u32[]{:S(2)}, u32[]{:S(2)}) collective-permute-start(f32[16,128]{1,0:T(8,128)S(1)} %get-tuple-element.22), channel_id=1, source_target_pairs={{16,0},{32,16},{48,32},{64,48},{80,64},{96,80},{112,96},{17,1},{33... | collective-permute-start | bytes 24584 | tf_op jit(solution)/shard_map/ppermute | solution.py:421
  39.1 1.0 %copy-start.2 = (f32[4,192,96]{2,1,0:T(8,128)S(1)}, f32[4,192,96]{2,1,0:T(8,128)}, u32[]{:S(2)}) copy-start(f32[4,192,96]{2,1,0:T(8,128)} %s_any.1) | copy-start | bytes 884740
  40.1 0.9 copy-start.10
  41.0 0.7 copy-start.17
  46.4 0.7 copy-start.5
  47.1 23.1 %all-to-all-start.1 = ((bf16[128,3,4,128]{3,2,1,0:T(4,128)(2,1)}), bf16[128,3,4,128]{3,2,1,0:T(4,128)(2,1)}, u32[]{:S(2)}, u32[]{:S(2)}) async-start(bf16[128,3,4,128]{3,2,1,0:T(4,128)(2,1)} %bitcast.29), calls=%async_computation.1 | async-start | bytes 786432 | tf_op jit(solution)/shard_map/all_to_all | solution.py:426
  57.7 20.7 %copy-start.9 = (f32[41,41]{1,0:T(8,128)S(1)}, f32[41,41]{1,0:T(8,128)}, u32[]{:S(2)}) copy-start(f32[41,41]{1,0:T(8,128)} %scale_ref.3) | copy-start | bytes 20176
  57.8 0.8 copy-start.13
  59.6 0.8 copy-start.6
  61.0 0.7 copy-start.8
  70.2 1.0 %copy-start.7 = (bf16[128,1536]{1,0:T(8,128)(2,1)S(1)}, bf16[128,1536]{1,0:T(8,128)(2,1)}, u32[]{:S(2)}) copy-start(bf16[128,1536]{1,0:T(8,128)(2,1)} %copy-done.6) | copy-start | bytes 1179652
  71.2 0.8 copy-start.12
  74.4 14.9 %all-to-all-start.2 = ((f32[128,1,384]{2,1,0:T(1,128)}), f32[128,1,384]{2,1,0:T(1,128)S(1)}, u32[]{:S(2)}, u32[]{:S(2)}) async-start(f32[128,1,384]{2,1,0:T(1,128)} %bitcast.15), calls=%async_computation.2 | async-start | bytes 393216 | tf_op jit(solution)/shard_map/all_to_all | solution.py:426
  (4 other events, 2.6 us)

commit v3 on v2

v3 whole, which is shorter than its diff:
```python
import jax
import jax.numpy as jnp
from jax import lax
from jax.experimental import pallas as pl
from jax.experimental.pallas import tpu as pltpu
from jax.sharding import PartitionSpec as P

F = 4
CELLS = 128
OCEAN = 32
STEPS = 4
TX, TY = 192, 96
GX, GY = 8, 16
DEV = GX * GY
PC = 384
CAP = 3
NB = 144
HALO = 4
ROWS_X = TX + 2 * HALO
WP = 32
WQ = 18
ROWS = 20
GROUP = 4 * ROWS
PROW = 256
LEFT = tuple(
    i for i in range(GX) if i < GX - 1 and (4 * (TX * i + TX + 2) - 11) // 26 + 1 - (4 * (TX * i - 3) - 11) // 26 >= WP
)
f32, bf16, i32 = jnp.float32, jnp.bfloat16, jnp.int32

diffuse_coef = 0.24
relax_coef = 0.3
drag_coefficient = 0.5


def iota(shape, dim):
    return lax.broadcasted_iota(i32, shape, dim)


def first_x(i):
    return (4 * (TX * i - 3) - 11) // 26


def first_y(j):
    return (4 * (TY * j - 3) - 11) // 26


def first_y_of(j):
    return ((4 * TY * j + 3) * 2521 >> 16) - 1


def first_x_of(i):
    return ((4 * TX * i + 3) * 2521 >> 16) - 1


def dot(a, b):
    return jnp.dot(a, b, preferred_element_type=f32)


def dot_nt(a, b):
    return lax.dot_general(a, b, (((1,), (1,)), ((), ())), preferred_element_type=f32)


def split3(x):
    high = x.astype(bf16)
    rest = x - high.astype(f32)
    mid = rest.astype(bf16)
    return high, mid, (rest - mid.astype(f32)).astype(bf16)


def column_of(row):
    n = row.shape[1]
    return jnp.sum(jnp.where(iota((n, n), 0) == iota((n, n), 1), row, 0), axis=1, keepdims=True)


def fetch(pairs, sems):
    copies = [pltpu.make_async_copy(src, dst, sems.at[k]) for k, (src, dst) in enumerate(pairs)]
    for copy in copies:
        copy.start()
    return copies


def rank_of(column, row, number):
    return jnp.sum(jnp.where((column == row) & (iota((NB, NB), 0) < number), 1, 0), axis=0, keepdims=True)


def by_thirds(column):
    at = iota((1, NB), 1)
    third = (at >= NB // CAP).astype(i32) + (at >= 2 * (NB // CAP)).astype(i32)
    number = CAP * (at - third * (NB // CAP)) + third
    return number, jnp.sum(jnp.where(iota((NB, NB), 0) == number, column, 0), axis=0, keepdims=True)


def pack_kernel(
    corner_ref, owner_ref, place_ref, parent_ref, s_ref, out_any, low_ref, high_ref, wide_ref, z_ref, out_ref, sems,
):
    wide_ref[...] = jnp.zeros_like(wide_ref)
    cx, cy = corner_ref[0], corner_ref[1]
    base = pl.multiple_of(jnp.minimum(jnp.maximum(cx - 1, 0) // 16 * 16, PC - PROW), 16)
    owner = owner_ref[...]
    rank = rank_of(column_of(owner), owner, iota((NB, NB), 1))
    named = iota((DEV, NB), 0) == owner
    slots = jnp.zeros((DEV, CELLS), f32)
    for s in range(CAP):
        value = jnp.sum(jnp.where(named & (rank == s), place_ref[...] + 1, 0).astype(f32), axis=1, keepdims=True) - 1.0
        slots = jnp.where(iota((DEV, CELLS), 1) == s, value, slots)
    columns(s_ref, low_ref, high_ref, wide_ref)

    row = iota((GY * ROWS, 1), 0)
    j = row * 3277 >> 16
    r = row - j * ROWS
    wanted = jnp.where(r < WQ, cy + first_y_of(j) + r, -1)
    pick_y = (wanted == iota((GY * ROWS, PC), 1)).astype(f32).astype(bf16)
    parts = [parent_ref[f, pl.ds(base, PROW), :] for f in range(F)]
    across = jnp.concatenate([dot_nt(pick_y, parts[f]).astype(bf16) for f in range(F)], axis=1)
    lane = iota((1, 2 * CELLS), 1)
    for pair in range(GX // 2):
        first = jnp.where(lane < CELLS, first_x(2 * pair), first_x(2 * pair + 1))
        p = cx - base + first + (lane & (WP - 1))
        target = jnp.where((p >= 0) & (p < PROW), (lane >> 5 & 3) * PROW + p, -1)
        pick_x = (iota((F * PROW, 2 * CELLS), 0) == target).astype(f32).astype(bf16)
        window = dot(across, pick_x)
        for k in range(2):
            i = 2 * pair + k
            z_ref[pl.ds(i * GY * ROWS, GY * ROWS), :] = window[:, k * CELLS : (k + 1) * CELLS]
    j16 = iota((GY, PC), 0)
    q = iota((GY, PC), 1) - (cy + first_y_of(j16))
    inside = (q >= 0) & (q < WQ)
    lanes = iota((GY, CELLS), 1) >> 5
    erow = iota((8, PROW), 0)
    target = jnp.full((8, PROW), -1, i32)
    for k, i in enumerate(LEFT):
        target = jnp.where(erow == k, cx - base + first_x(i) + WP, target)
    pick_row = (target == iota((8, PROW), 1)).astype(f32).astype(bf16)
    left = [jnp.zeros((GY, CELLS), f32) for _ in LEFT]
    for f in range(F):
        rows = dot(pick_row, parts[f])
        for k in range(len(LEFT)):
            kept = jnp.where(inside, rows[k : k + 1, :], 0.0)
            folded = kept[:, :128] + kept[:, 128:256] + kept[:, 256:]
            folded = folded + pltpu.roll(folded, 64, 1)
            folded = folded + pltpu.roll(folded, 32, 1)
            left[k] = jnp.where(lanes == f, folded, left[k])
    for k, i in enumerate(LEFT):
        z_ref[pl.ds(i * GY * ROWS + WQ, GY, stride=ROWS), :] = left[k]
    z_ref[pl.ds(ROWS - 1, DEV, stride=ROWS), :] = slots
    write(z_ref, out_ref, out_any, sems, 4)


def write(z_ref, out_ref, out_any, sems, parts):
    rows = z_ref.shape[0] // parts
    copies = []
    for k in range(parts):
        at = pl.ds(k * rows, rows)
        out_ref[at, :] = z_ref[at, :].astype(bf16)
        copies.append(pltpu.make_async_copy(out_ref.at[at, :], out_any.at[at, :], sems.at[k]))
        copies[k].start()
    for copy in copies:
        copy.wait()


def hat(fine, anchor, coarse):
    centre = (fine.astype(f32) + 0.5) * (2.0 / 13.0) - 0.5 + anchor.astype(f32)
    return jnp.maximum(0.0, 1.0 - jnp.abs(centre - coarse.astype(f32)))


def columns(s_ref, low_ref, high_ref, wide_ref):
    field = iota((TX, CELLS), 1) >> 2
    low, high = jnp.zeros((TX, CELLS), f32), jnp.zeros((TX, CELLS), f32)
    for f in range(F):
        wide_ref[:, :TY] = s_ref[f]
        s = wide_ref[...]
        low = jnp.where(field == f, s if f == 0 else pltpu.roll(s, HALO * f, 1), low)
        high = jnp.where(field == f, pltpu.roll(s, CELLS - TY + HALO + HALO * f, 1), high)
    low_ref[...] = low
    high_ref[...] = high


def widened(s, left, right, f):
    lane = iota(s.shape, 1)
    before = left if f == 0 else pltpu.roll(left, CELLS - HALO * f, 1)
    after = pltpu.roll(right, TY + HALO - HALO * f, 1)
    wide = jnp.where(lane < TY + HALO, pltpu.roll(s, HALO, 1), after)
    return jnp.where(lane < HALO, before, jnp.where(lane < TY + 2 * HALO, wide, 0.0))


def rows_kernel(s_any, left_ref, right_ref, low_ref, high_ref, s_ref, wide_ref, sems):
    ends = ((0, 0), (8, TX - 8))
    for copy in fetch([(s_any.at[:, pl.ds(src, 8), :], s_ref.at[:, pl.ds(dst, 8), :]) for dst, src in ends], sems):
        copy.wait()
    left = jnp.concatenate([left_ref[:8, :], left_ref[TX - 8 :, :]], axis=0)
    right = jnp.concatenate([right_ref[:8, :], right_ref[TX - 8 :, :]], axis=0)
    wide_ref[...] = jnp.zeros_like(wide_ref)
    for f in range(F):
        wide_ref[:, :TY] = s_ref[f]
        wide = widened(wide_ref[...], left, right, f)
        low_ref[f * HALO : (f + 1) * HALO, :] = wide[:HALO]
        high_ref[f * HALO : (f + 1) * HALO, :] = wide[16 - HALO :]


def ready_kernel(
    holder_ref, corner_ref, owner_ref, s_ref, left_ref, right_ref, before_ref, after_ref,
    wx_ref, wlast_ref, mask_ref, wy_ref, wyc_ref, send_ref, back_ref, state_ref, wide_ref,
):
    ix, iy = lax.axis_index("gx"), lax.axis_index("gy")
    cx, cy = corner_ref[0], corner_ref[1]
    x0, y0 = ix * TX - HALO, iy * TY - HALO
    px, qy = cx + first_x_of(ix), cy + first_y_of(iy)
    lane = iota((ROWS_X, CELLS), 1)
    row = iota((ROWS_X, CELLS), 0)
    weight = hat(row + x0, cx, (lane & (WP - 1)) + px)
    for f in range(F):
        wx_ref[f * ROWS_X : (f + 1) * ROWS_X, :] = jnp.where(lane >> 5 == f, weight, 0.0).astype(bf16)
    wlast_ref[...] = relax_coef * hat(row + x0, cx, jnp.full_like(row, WP) + px).astype(bf16).astype(f32)
    inside = (row + x0 >= 0) & (row + x0 < GX * TX) & (lane + y0 >= 0) & (lane + y0 < GY * TY)
    mask_ref[...] = jnp.where(inside, 1.0, 0.0)
    at = iota((CELLS, GROUP), 1) - (holder_ref[0] & 3) * ROWS
    wy_ref[...] = jnp.where((at >= 0) & (at < WQ), hat(iota((CELLS, GROUP), 0) + y0, cy, at + qy), 0.0).astype(bf16)
    lane = iota((CELLS, CELLS), 1)
    wyc_ref[...] = hat(iota((CELLS, CELLS), 0) + y0, cy, qy + ((lane - qy) & (WP - 1))).astype(bf16)
    wide_ref[...] = jnp.zeros_like(wide_ref)
    column = column_of(owner_ref[...])
    number, owner = by_thirds(column)
    rank = rank_of(column, owner, number)
    send_ref[...] = (iota((CAP * DEV, NB), 0) == rank * DEV + owner).astype(f32).astype(bf16)
    back_ref[...] = (column_of(owner * CAP + rank) == iota((NB, CAP * DEV), 1)).astype(f32).astype(bf16)
    left, right = left_ref[...], right_ref[...]
    for f in range(F):
        wide_ref[:, :TY] = s_ref[f]
        state_ref[f, :HALO, :] = before_ref[f * HALO : (f + 1) * HALO, :]
        state_ref[f, HALO : HALO + TX, :] = widened(wide_ref[...], left, right, f)
        state_ref[f, HALO + TX :, :] = after_ref[f * HALO : (f + 1) * HALO, :]


def nest_kernel(
    holder_ref, got_ref, wx_ref, wlast_ref, mask_ref, wy_ref, wyc_ref, send_ref, begin_ref, skin_ref, next_any, out_any,
    next_ref, out_ref, state_ref, force_ref, flux_ref, z_ref, sems,
):
    group = pl.multiple_of((holder_ref[0] >> 2) * GROUP, 16)
    got = got_ref[pl.ds(group, GROUP), :]
    partial = dot(wy_ref[...], got).astype(bf16)
    last = jnp.sum(
        jnp.where(iota((GROUP, CELLS), 0) == (holder_ref[0] & 3) * ROWS + WQ, got.astype(f32), 0.0), axis=0, keepdims=True
    )
    last = jnp.where(iota((8, CELLS), 1) >> 5 == iota((8, CELLS), 0), last, 0.0).astype(bf16)
    partial_last = dot_nt(last, wyc_ref[...]).astype(bf16).astype(f32)
    force_ref[...] = dot_nt(wx_ref[...], partial)
    flux_ref[...] = jnp.zeros_like(flux_ref)
    mask = mask_ref[...]
    written = []
    for f in range(F):
        force = relax_coef * force_ref[f * ROWS_X : (f + 1) * ROWS_X, :] + wlast_ref[...] * partial_last[f : f + 1, :]
        s = begin_ref[f]
        for _ in range(STEPS):
            beside = (
                pltpu.roll(s, 1, 0) + pltpu.roll(s, ROWS_X - 1, 0) + pltpu.roll(s, 1, 1) + pltpu.roll(s, CELLS - 1, 1)
            )
            s = mask * ((1.0 - 4.0 * diffuse_coef - relax_coef) * s + diffuse_coef * beside + force)
        state_ref[...] = pltpu.roll(s, CELLS - HALO, 1)
        next_ref[f] = state_ref[HALO : HALO + TX, :TY]
        written.append(pltpu.make_async_copy(next_ref.at[f], next_any.at[f], sems.at[f]))
        written[f].start()
    u, v, ta, qa = next_ref[0], next_ref[1], next_ref[2], next_ref[3]
    half = drag_coefficient * jnp.sqrt(1.0 + u * u + v * v)
    skin = skin_ref[...]
    flux = (half * (ta - skin), half * (qa - 0.5 * skin), half * u, half * v)
    rows = NB // CAP
    lane = iota((rows, CELLS), 1)
    blocks = []
    for f in range(F):
        flux_ref[:, :TY] = flux[f]
        m = [flux_ref[pl.ds(k, rows, stride=4), :] for k in range(4)]
        r1, r2, r3 = pltpu.roll(m[1], 96, 1), pltpu.roll(m[2], 64, 1), pltpu.roll(m[3], 32, 1)
        blocks.append(
            jnp.concatenate(
                [jnp.where(lane < 96, m[0], r1), jnp.where(lane < 64, r1, r2), jnp.where(lane < 32, r2, r3)], axis=0
            ).astype(bf16)
        )
    sent = dot(send_ref[...], jnp.concatenate(blocks, axis=1))
    for slot in range(CAP):
        for f in range(F):
            z_ref[pl.ds(slot * F + f, DEV, stride=CAP * F), :] = sent[
                slot * DEV : (slot + 1) * DEV, f * CELLS : (f + 1) * CELLS
            ]
    for copy in written:
        copy.wait()
    write(z_ref, out_ref, out_any, sems, 4)


def hot_kernel(got_ref, kept_ref, hot_ref, give_ref, inverse_ref, cover_ref, z_ref, slot_ref, row_ref):
    slot_ref[...] = got_ref[...].astype(f32)
    slots = slot_ref[pl.ds(ROWS - 1, DEV, stride=ROWS), :].astype(i32)
    lane = iota((DEV, OCEAN * F), 1)
    for s in range(CAP):
        target = slots[:, s : s + 1] * F
        for f in range(F):
            z_ref[pl.ds(s * F + f, DEV, stride=CAP * F), :] = (lane == jnp.where(target < 0, -1, target + f)).astype(f32)
        row_ref[pl.ds(s, DEV, stride=CAP), :] = (lane == target).astype(f32)
    give_ref[...] = row_ref[...].astype(bf16)
    hot = jnp.swapaxes(z_ref[...], 0, 1)
    hot_ref[...] = hot.astype(bf16)
    count = jnp.sum(hot, axis=1, keepdims=True)
    inverse_ref[...] = jnp.broadcast_to(1.0 / jnp.maximum(count, 1.0), (OCEAN * F, CELLS))
    cover_ref[...] = jnp.where(count == 0.0, kept_ref[...], 0.0)


def top_kernel(scale_ref, marine_ref, out_ref):
    total = scale_ref[0, 0] * marine_ref[0]
    for k in range(1, marine_ref.shape[0]):
        total = total + scale_ref[0, k] * marine_ref[k]
    out_ref[: OCEAN * F, :] = total
    out_ref[OCEAN * F :, :] = jnp.full((8, CELLS), scale_ref[0, 0], f32)


def ocean_kernel(got_ref, hot_ref, inverse_ref, cover_ref, top_ref, give_ref, forcing_ref, out_ref):
    forcing = dot(hot_ref[...], got_ref[...]) * inverse_ref[...] + cover_ref[...]
    forcing_ref[...] = forcing
    top = top_ref[: OCEAN * F, :] + top_ref[OCEAN * F : OCEAN * F + 1, :] * forcing
    back = dot(give_ref[...], jnp.concatenate(split3(top), axis=1))
    out_ref[...] = back[:, :CELLS] + back[:, CELLS : 2 * CELLS] + back[:, 2 * CELLS :]

def mix_kernel(scale_ref, forcing_ref, marine_ref, out_ref, high_ref, low_ref):
    layers = marine_ref.shape[0]
    n = 8 * layers

    @pl.when(pl.program_id(0) == 0)
    def _():
        spread = (iota((n, layers), 0) >> 3 == iota((n, layers), 1)).astype(f32).astype(bf16)
        same = (iota((n, n), 0) & 7) == (iota((n, n), 1) & 7)
        scale = scale_ref[...]
        high = scale.astype(bf16)
        low = (scale - high.astype(f32)).astype(bf16)
        for part, ref in ((high, high_ref), (low, low_ref)):
            wide = dot_nt(dot(spread, part).astype(bf16), spread)
            ref[...] = jnp.where(same, wide, 0.0).astype(bf16)

    groups = marine_ref.shape[1] // 8
    columns = []
    for g in range(groups):
        x = marine_ref[:, 8 * g : 8 * g + 8, :].reshape(n, CELLS)
        first = x[:8] + forcing_ref[8 * g : 8 * g + 8, :]
        columns.append(jnp.concatenate([first, x[8:]], axis=0))
    x = jnp.concatenate(columns, axis=1)
    high = x.astype(bf16)
    low = (x - high.astype(f32)).astype(bf16)
    y = dot(high_ref[...], high) + (dot(high_ref[...], low) + dot(low_ref[...], high))
    for g in range(groups):
        out_ref[:, 8 * g : 8 * g + 8, :] = y[:, g * CELLS : (g + 1) * CELLS].reshape(layers, 8, CELLS)


def skin_kernel(got_ref, back_ref, out_ref, tile_ref):
    x = dot(back_ref[...], jnp.concatenate(split3(got_ref[...]), axis=1))
    x = x[:, :CELLS] + x[:, CELLS : 2 * CELLS] + x[:, 2 * CELLS :]
    rows = NB // CAP
    t0, t1, t2 = x[:rows], x[rows : 2 * rows], x[2 * rows :]
    lane = iota((rows, CELLS), 1)
    tile_ref[pl.ds(0, rows, stride=4), :] = t0
    tile_ref[pl.ds(1, rows, stride=4), :] = pltpu.roll(jnp.where(lane < 64, t1, t0), 32, 1)
    tile_ref[pl.ds(2, rows, stride=4), :] = pltpu.roll(jnp.where(lane < 32, t2, t1), 64, 1)
    tile_ref[pl.ds(3, rows, stride=4), :] = pltpu.roll(t2, 96, 1)
    out_ref[...] = tile_ref[:, :TY]


MEMORY = {"h": pltpu.HBM, "v": pltpu.VMEM, "H": pltpu.HBM, "S": pltpu.HBM}
SPACES = {"h": pltpu.HBM, "v": pltpu.VMEM, "H": pltpu.HBM, "S": pltpu.HBM, "p": pltpu.VMEM, "s": pltpu.SMEM}


def call(kernel, ins, outs, args, shapes, scratch=(), copies=0):
    args = [pltpu.with_memory_space_constraint(a, MEMORY[c]) if c in MEMORY else a for c, a in zip(ins, args)]
    letters = ins + outs
    kinds = [(a.shape, a.dtype) for a in args] + list(shapes)
    moved = [k for k, c in enumerate(letters) if c in "HS"]
    own = len(scratch) + (1 if copies else 0)

    def body(*refs):
        arrays, rest = list(refs[: len(letters)]), refs[len(letters) :]
        sems = rest[-1]
        far = [arrays[k] for k in moved]
        for n, k in enumerate(moved):
            arrays[k] = rest[own + n]
        pending = [
            pltpu.make_async_copy(far[n], arrays[k], sems.at[n]) for n, k in enumerate(moved) if k < len(ins)
        ]
        for copy in pending:
            copy.start()
        for copy in pending:
            copy.wait()
        kernel(*arrays, *rest[:own])
        done = [pltpu.make_async_copy(arrays[k], far[n], sems.at[n]) for n, k in enumerate(moved) if k >= len(ins)]
        for copy in done:
            copy.start()
        for copy in done:
            copy.wait()

    return pl.pallas_call(
        body,
        out_shape=tuple(MEMORY[c](s, d) if c in MEMORY else jax.ShapeDtypeStruct(s, d) for c, (s, d) in zip(outs, shapes)),
        in_specs=[pl.BlockSpec(memory_space=SPACES[c]) for c in ins],
        out_specs=tuple(pl.BlockSpec(memory_space=SPACES[c]) for c in outs),
        scratch_shapes=[pltpu.VMEM(s, d) for s, d in scratch]
        + ([pltpu.SemaphoreType.DMA((copies,))] if copies else [])
        + [(pltpu.SMEM if letters[k] == "S" else pltpu.VMEM)(*kinds[k]) for k in moved]
        + [pltpu.SemaphoreType.DMA((max(1, len(moved)),))],
        compiler_params=pltpu.CompilerParams(vmem_limit_bytes=32 << 20),
    )(*args)


def shift(value, axis, by):
    n = lax.axis_size(axis)
    return lax.ppermute(value, axis, [(i, i + by) for i in range(n) if 0 <= i + by < n])


def exchange(value, rows):
    split = value.reshape(rows)
    return lax.all_to_all(split, ("gx", "gy"), split_axis=0, concat_axis=0, tiled=True).reshape(value.shape)


def by_block(value):
    return value.reshape(F, OCEAN, CELLS).transpose(1, 0, 2).reshape(OCEAN * F, CELLS)


def on_device(
    fine_atmospheric_values,
    fine_skin_heat,
    coarse_lowest_values,
    holder_flat,
    corner_offset,
    exchange_patch_holder,
    holder_patch_position,
    coarse_interface_exchange,
    marine_stratum_values,
    diffusion_solver_operator,
):
    owner = exchange_patch_holder.reshape(1, NB)
    place = holder_patch_position.reshape(1, NB)
    names, message, tile, strip = ((1, NB), i32), ((DEV * ROWS, CELLS), bf16), ((F, TX, TY), f32), ((TX, CELLS), f32)
    windows, low, high = call(
        pack_kernel, "SHHHH", "hvv",
        (corner_offset, owner, place, coarse_lowest_values, fine_atmospheric_values), (message, strip, strip),
        (strip, ((DEV * ROWS, CELLS), f32), message), 4,
    )
    left, right = shift(high, "gy", 1), shift(low, "gy", -1)
    got = exchange(windows, (DEV, ROWS // 4, 4, CELLS))
    ends = ((F * HALO, CELLS), f32)
    low, high = call(
        rows_kernel, "hvv", "vv", (fine_atmospheric_values, left, right), (ends, ends),
        (((F, 16, TY), f32), ((16, CELLS), f32)), 2,
    )
    before, after = shift(high, "gx", 1), shift(low, "gx", -1)
    holder, _ = lax.optimization_barrier((holder_flat, low))
    holder = jnp.minimum(holder, DEV - 1)
    wide = (ROWS_X, CELLS)
    *weights, send, back, state = call(
        ready_kernel, "sSHHvvvv", "HHHHHHHH",
        (holder, corner_offset, owner, fine_atmospheric_values, left, right, before, after),
        (
            ((F * ROWS_X, CELLS), bf16), (wide, f32), (wide, f32), ((CELLS, GROUP), bf16), ((CELLS, CELLS), bf16),
            ((CAP * DEV, NB), bf16), ((NB, CAP * DEV), bf16), ((F,) + wide, f32),
        ), (strip,),
    )
    sent = ((DEV * CAP * F, CELLS), bf16)
    nest_next, flux = call(
        nest_kernel, "svHHHHHHHH", "hh", (holder, got, *weights, send, state, fine_skin_heat), (tile, sent),
        (tile, sent, (wide, f32), ((F * ROWS_X, CELLS), f32), strip, ((DEV * CAP * F, CELLS), f32)), F,
    )
    got_flux = exchange(flux, (DEV, CAP, F, CELLS))
    layers = marine_stratum_values.shape[1]
    marine = marine_stratum_values.reshape(F, layers, OCEAN, CELLS).transpose(1, 2, 0, 3).reshape(layers, OCEAN * F, CELLS)
    marine_late, got_late, flux = lax.optimization_barrier((marine, got, flux))
    block = ((OCEAN * F, CELLS), f32)
    hot, give = ((OCEAN * F, DEV * CAP * F), bf16), ((DEV * CAP, OCEAN * F), bf16)
    hot, give, inverse, cover = call(
        hot_kernel, "vH", "HHHH", (got_late, by_block(coarse_interface_exchange)), (hot, give, block, block),
        (((DEV * CAP * F, OCEAN * F), f32), ((DEV * ROWS, CELLS), f32), ((DEV * CAP, OCEAN * F), f32)),
    )
    (top,) = call(top_kernel, "Sp", "H", (diffusion_solver_operator, marine_late), (((OCEAN * F + 8, CELLS), f32),))
    returned = ((DEV * CAP, CELLS), f32)
    forcing, skins = call(
        ocean_kernel, "HHHHHH", "HH", (got_flux, hot, inverse, cover, top, give), (block, returned)
    )
    arrived = exchange(skins, (DEV, 1, CAP * CELLS))
    part = 32
    refreshed = pl.pallas_call(
        mix_kernel,
        out_shape=jax.ShapeDtypeStruct((layers, OCEAN * F, CELLS), f32),
        grid=(OCEAN * F // part,),
        in_specs=[
            pl.BlockSpec((layers, layers), lambda g: (0, 0)),
            pl.BlockSpec((part, CELLS), lambda g: (g, 0)),
            pl.BlockSpec((layers, part, CELLS), lambda g: (0, g, 0)),
        ],
        out_specs=pl.BlockSpec((layers, part, CELLS), lambda g: (0, g, 0)),
        scratch_shapes=[pltpu.VMEM((8 * layers, 8 * layers), bf16)] * 2,
        compiler_params=pltpu.CompilerParams(vmem_limit_bytes=40 << 20),
    )(diffusion_solver_operator, forcing, marine)
    refreshed = refreshed.reshape(layers, OCEAN, F, CELLS).transpose(2, 0, 1, 3).reshape(marine_stratum_values.shape)
    (skin,) = call(skin_kernel, "vH", "p", (arrived, back), (((TX, TY), f32),), (((TX, CELLS), f32),))
    return (nest_next, refreshed, skin)


def solution(mesh):
    in_specs = (
        P(None, "gx", "gy"),
        P("gx", "gy"),
        P(None, "gx", "gy"),
        P(),
        P(),
        P(("gx", "gy"), None),
        P(("gx", "gy")),
        P(None, ("gx", "gy")),
        P(None, None, ("gx", "gy")),
        P(),
    )
    out_specs = (P(None, "gx", "gy"), P(None, None, ("gx", "gy")), P("gx", "gy"))
    return jax.shard_map(
        on_device, mesh=mesh, in_specs=in_specs, out_specs=out_specs, check_vma=False
    )
```

time: 91.6 us -> 85.8 us (0.937)
  local copies, waits for them, and re-layouts: 13.8 us -> 0.85 us
  Pallas kernels: 16.9 us -> 24.5 us
  starting transfers between devices: 36.1 us -> 34.7 us
  waiting for transfers between devices: 22.5 us -> 23.6 us
    unnamed x42 -> x6, local copies, waits for them, and re-layouts: 13.8 us -> 0.85 us
    pallas_call x8, Pallas kernels: 12.3 us -> 20 us  [call(): pl.pallas_call(body, out_shape=tuple((MEMORY[c](s, d) if c in MEMORY else...]
    ppermute x4, starting transfers between devices: 9.94 us -> 9.01 us  [shift(): lax.ppermute(value, axis, [(i, i + by) for i in range(n) if 0 <= i + by <...]
    ppermute x4, waiting for transfers between devices: 8.89 us -> 9.82 us  [shift(): lax.ppermute(value, axis, [(i, i + by) for i in range(n) if 0 <= i + by <...]
  transfers between devices with their start and end apart: 7 -> 7, of which waited for: 5 -> 5; matrix products, arithmetic and copies ran while one was open for 0% -> 0% of each run, Pallas kernels for 8% -> 14%
where the time goes in v3:
time: 85.8 us; the launch traced here: 85.2 us
  starting transfers between devices  34.7 us (40%)
  Pallas kernels  24.5 us (29%)
  waiting for transfers between devices  23.6 us (28%)
  between operations  1.45 us (2%)
    all_to_all x3, starting transfers between devices, exchange(): lax.all_to_all(split, ('gx', 'gy'), split_axis=0, concat_axis=0, tiled=True)  25.7 us
    pallas_call x8, Pallas kernels, call(): pl.pallas_call(body, out_shape=tuple((MEMORY[c](s, d) if c in MEMORY else...  20 us
    all_to_all x3, waiting for transfers between devices, exchange(): lax.all_to_all(split, ('gx', 'gy'), split_axis=0, concat_axis=0, tiled=True)  13.8 us
    ppermute x4, waiting for transfers between devices, shift(): lax.ppermute(value, axis, [(i, i + by) for i in range(n) if 0 <= i + by <...  9.82 us
    ppermute x4, starting transfers between devices, shift(): lax.ppermute(value, axis, [(i, i + by) for i in range(n) if 0 <= i + by <...  9.01 us
    pallas_call x1, Pallas kernels, on_device(): pl.pallas_call(mix_kernel, out_shape=jax.ShapeDtypeStruct((layers, OCEAN...  4.54 us
  transfers between devices with their start and end apart: 7, of which 5 were waited for; matrix products, arithmetic and copies ran while one was open for 0% of the time, Pallas kernels for 14%

profile of v3, /device:TPU:1, one launch (start us, length us, event | category | flops | bytes accessed | tf_op | source)
XLA Modules:
  0.0 85.2 jit_solution(14496246576891289596)
XLA Ops:
  0.6 3.9 %shard_map.121 = (bf16[2560,128]{1,0:T(8,128)(2,1)}, f32[192,128]{1,0:T(8,128)S(1)}, f32[192,128]{1,0:T(8,128)S(1)}) custom-call(s32[2]{0:T(128)} %refs_1_.1, s32[1,144]{1,0:T(1,128)} %bitcast.33, s32[1,144]{1,0:T(1,128)} %bitcast.35, bf16[4,384,384]{2,1,0:T(8,128)(2,1)} %refs_3_.2, f32[4,192,96]{2,1,0:T(8,128)} %refs_3_.3), custom_call_target="tpu_custom_call" | custom-call | tf_op jit(solution)/shard_map/pallas_call | solution.py:394
  4.6 0.0 copy-start
  4.6 11.5 %all-to-all-start = ((bf16[128,5,4,128]{3,2,1,0:T(4,128)(2,1)}), bf16[128,5,4,128]{3,2,1,0:T(4,128)(2,1)S(1)}, u32[]{:S(2)}, u32[]{:S(2)}) async-start(bf16[128,5,4,128]{3,2,1,0:T(4,128)(2,1)} %bitcast.29), calls=%async_computation | async-start | bytes 1310720 | tf_op jit(solution)/shard_map/all_to_all | solution.py:414
  16.1 3.3 %collective-permute-start = (f32[192,128]{1,0:T(8,128)S(1)}, f32[192,128]{1,0:T(8,128)S(1)}, u32[]{:S(2)}, u32[]{:S(2)}) collective-permute-start(f32[192,128]{1,0:T(8,128)S(1)} %get-tuple-element.27), channel_id=1, source_target_pairs={{0,1},{1,2},{2,3},{3,4},{4,5},{5,6},{6,7},{7,8},{8,9},{9,10},{10,1... | collective-permute-start | bytes 294920 | tf_op jit(solution)/shard_map/ppermute | solution.py:409
  19.4 1.3 %collective-permute-start.1 = (f32[192,128]{1,0:T(8,128)S(1)}, f32[192,128]{1,0:T(8,128)S(1)}, u32[]{:S(2)}, u32[]{:S(2)}) collective-permute-start(f32[192,128]{1,0:T(8,128)S(1)} %get-tuple-element.28), channel_id=1, source_target_pairs={{1,0},{2,1},{3,2},{4,3},{5,4},{6,5},{7,6},{8,7},{9,8},{10,9},{11,1... | collective-permute-start | bytes 294920 | tf_op jit(solution)/shard_map/ppermute | solution.py:409
  20.7 4.8 %collective-permute-done.refs_1_.refs_4_ = f32[192,128]{1,0:T(8,128)S(1)} collective-permute-done((f32[192,128]{1,0:T(8,128)S(1)}, f32[192,128]{1,0:T(8,128)S(1)}, u32[]{:S(2)}, u32[]{:S(2)}) %collective-permute-start) | collective-permute-done | bytes 98336 | tf_op jit(solution)/shard_map/ppermute | solution.py:409
  25.5 2.7 %collective-permute-done.1.refs_2_.refs_5_ = f32[192,128]{1,0:T(8,128)S(1)} collective-permute-done((f32[192,128]{1,0:T(8,128)S(1)}, f32[192,128]{1,0:T(8,128)S(1)}, u32[]{:S(2)}, u32[]{:S(2)}) %collective-permute-start.1) | collective-permute-done | bytes 98336 | tf_op jit(solution)/shard_map/ppermute | solution.py:409
  28.1 0.9 %shard_map.122 = (f32[16,128]{1,0:T(8,128)S(1)}, f32[16,128]{1,0:T(8,128)S(1)}) custom-call(f32[4,192,96]{2,1,0:T(8,128)} %refs_3_.3, f32[192,128]{1,0:T(8,128)S(1)} %collective-permute-done.refs_1_.refs_4_, f32[192,128]{1,0:T(8,128)S(1)} %collective-permute-done.1.refs_2_.refs_5_), custom_call_target="tpu_custom_call" | custom-call | tf_op jit(solution)/shard_map/pallas_call | solution.py:394
  29.0 2.5 %collective-permute-start.2 = (f32[16,128]{1,0:T(8,128)S(1)}, f32[16,128]{1,0:T(8,128)S(1)}, u32[]{:S(2)}, u32[]{:S(2)}) collective-permute-start(f32[16,128]{1,0:T(8,128)S(1)} %get-tuple-element.32), channel_id=1, source_target_pairs={{0,16},{16,32},{32,48},{48,64},{64,80},{80,96},{96,112},{1,17},{17... | collective-permute-start | bytes 24584 | tf_op jit(solution)/shard_map/ppermute | solution.py:409
  31.5 1.9 %collective-permute-start.3 = (f32[16,128]{1,0:T(8,128)S(1)}, f32[16,128]{1,0:T(8,128)S(1)}, u32[]{:S(2)}, u32[]{:S(2)}) collective-permute-start(f32[16,128]{1,0:T(8,128)S(1)} %get-tuple-element.29), channel_id=1, source_target_pairs={{16,0},{32,16},{48,32},{64,48},{80,64},{96,80},{112,96},{17,1},{33... | collective-permute-start | bytes 24584 | tf_op jit(solution)/shard_map/ppermute | solution.py:409
  34.1 2.4 %collective-permute-done.3.refs_7_ = f32[16,128]{1,0:T(8,128)S(1)} collective-permute-done((f32[16,128]{1,0:T(8,128)S(1)}, f32[16,128]{1,0:T(8,128)S(1)}, u32[]{:S(2)}, u32[]{:S(2)}) %collective-permute-start.3) | collective-permute-done | bytes 8224 | tf_op jit(solution)/shard_map/ppermute | solution.py:409
  36.5 2.7 %shard_map.123 = (bf16[800,128]{1,0:T(8,128)(2,1)}, f32[200,128]{1,0:T(8,128)}, f32[200,128]{1,0:T(8,128)}, bf16[128,80]{1,0:T(8,128)(2,1)}, bf16[128,128]{1,0:T...) custom-call(s32[1]{0:T(128)S(6)} %min.3.refs_0_, s32[2]{0:T(128)} %refs_1_.1, ...), custom_call_target="tpu_custom_call" | custom-call | tf_op jit(solution)/shard_map/pallas_call | solution.py:394
  39.2 4.1 %shard_map.124 = (f32[4,192,96]{2,1,0:T(8,128)}, bf16[1536,128]{1,0:T(8,128)(2,1)}) custom-call(s32[1]{0:T(128)S(6)} %min.3.refs_0_, bf16[2560,128]{1,0:T(8,128)(2,1)S(1)} %bitcast.25, bf16[800,128]{1,0:T(8,128)(2,1)} %get-tuple-element.33.refs_2_, f32[200,128]{1,0:T(8,128)} %get-tuple-element.34.refs_3_, f32[200,128]{1,0:T(8,128)} %get-tuple-element.35.refs_4_, ...), custom_call_target="tpu_custom_call" | custom-call | tf_op jit(solution)/shard_map/pallas_call | solution.py:394
  43.3 10.2 %all-to-all-start.1 = ((bf16[128,3,4,128]{3,2,1,0:T(4,128)(2,1)}), bf16[128,3,4,128]{3,2,1,0:T(4,128)(2,1)}, u32[]{:S(2)}, u32[]{:S(2)}) async-start(bf16[128,3,4,128]{3,2,1,0:T(4,128)(2,1)} %bitcast.30), calls=%async_computation.1 | async-start | bytes 786432 | tf_op jit(solution)/shard_map/all_to_all | solution.py:414
  53.5 0.0 copy-start.1
  53.5 2.3 %shard_map.125 = (bf16[128,1536]{1,0:T(8,128)(2,1)}, bf16[384,128]{1,0:T(8,128)(2,1)}, f32[128,128]{1,0:T(8,128)}, f32[128,128]{1,0:T(8,128)}) custom-call(bf16[2560,128]{1,0:T(8,128)(2,1)S(1)} %bitcast.26, f32[128,128]{1,0:T(8,128)} %bitcast.32), custom_call_target="tpu_custom_call" | custom-call | tf_op jit(solution)/shard_map/pallas_call | solution.py:394
  55.8 1.9 %shard_map.126.refs_4_ = f32[136,128]{1,0:T(8,128)} custom-call(f32[41,41]{1,0:T(8,128)} %scale_ref.1, f32[41,128,128]{2,1,0:T(8,128)S(1)} %bitcast.23), custom_call_target="tpu_custom_call" | custom-call | tf_op jit(solution)/shard_map/pallas_call | solution.py:394
  57.7 8.3 %all-to-all-done.1 = bf16[128,3,4,128]{3,2,1,0:T(4,128)(2,1)} async-done(((bf16[128,3,4,128]{3,2,1,0:T(4,128)(2,1)}), bf16[128,3,4,128]{3,2,1,0:T(4,128)(2,1)}, u32[]{:S(2)}, u32[]{:S(2)}) %all-to-all-start.1) | async-done | bytes 393248 | tf_op jit(solution)/shard_map/all_to_all | solution.py:414
  66.0 2.4 %shard_map.127 = (f32[128,128]{1,0:T(8,128)}, f32[384,128]{1,0:T(8,128)}) custom-call(bf16[1536,128]{1,0:T(8,128)(2,1)} %bitcast.5.refs_0_, bf16[128,1536]{1,0:T(8,128)(2,1)} %get-tuple-element.43.refs_1_, f32[128,128]{1,0:T(8,128)} %get-tuple-element.44.refs_2_, f32[128,128]{1,0:T(8,128)} %get-tuple-element.45.refs_3_, f32[136,128]{1,0:T(8,128)} %shard_map.126.refs_4_, ...), custom_call_target="tpu_custom_call" | custom-call | tf_op jit(solution)/shard_map/pallas_call | solution.py:394
  68.4 4.0 %all-to-all-start.2 = ((f32[128,1,384]{2,1,0:T(1,128)}), f32[128,1,384]{2,1,0:T(1,128)S(1)}, u32[]{:S(2)}, u32[]{:S(2)}) async-start(f32[128,1,384]{2,1,0:T(1,128)} %bitcast.31), calls=%async_computation.2 | async-start | bytes 393216 | tf_op jit(solution)/shard_map/all_to_all | solution.py:414
  72.4 0.8 copy-done.2
  73.2 4.5 %shard_map.128 = f32[41,128,128]{2,1,0:T(8,128)} custom-call(f32[41,41]{1,0:T(8,128)S(1)} %copy-done.1, f32[128,128]{1,0:T(8,128)S(1)} %copy-done.2, f32[41,128,128]{2,1,0:T(8,128)S(1)} %bitcast.24), custom_call_target="tpu_custom_call" | custom-call | tf_op jit(solution)/shard_map/pallas_call | solution.py:482
  77.8 5.5 %all-to-all-done.2 = f32[128,1,384]{2,1,0:T(1,128)S(1)} async-done(((f32[128,1,384]{2,1,0:T(1,128)}), f32[128,1,384]{2,1,0:T(1,128)S(1)}, u32[]{:S(2)}, u32[]{:S(2)}) %all-to-all-start.2) | async-done | bytes 196640 | tf_op jit(solution)/shard_map/all_to_all | solution.py:414
  83.3 1.9 %shard_map.129 = f32[192,96]{1,0:T(8,128)} custom-call(f32[384,128]{1,0:T(8,128)S(1)} %bitcast.27, bf16[144,384]{1,0:T(8,128)(2,1)} %get-tuple-element.50.refs_1_), custom_call_target="tpu_custom_call" | custom-call | tf_op jit(solution)/shard_map/pallas_call | solution.py:394
  (5 shorter events, 0.0 us)
Async XLA Ops:
  4.6 51.2 %copy-start = (f32[4,41,4096]{2,0,1:T(4,128)S(1)}, f32[4,41,4096]{2,0,1:T(4,128)}, u32[]{:S(2)}) copy-start(f32[4,41,4096]{2,0,1:T(4,128)} %param.18) | copy-start | bytes 8060932
  4.6 34.6 %all-to-all-start = ((bf16[128,5,4,128]{3,2,1,0:T(4,128)(2,1)}), bf16[128,5,4,128]{3,2,1,0:T(4,128)(2,1)S(1)}, u32[]{:S(2)}, u32[]{:S(2)}) async-start(bf16[128,5,4,128]{3,2,1,0:T(4,128)(2,1)} %bitcast.29), calls=%async_computation | async-start | bytes 1310720 | tf_op jit(solution)/shard_map/all_to_all | solution.py:414
  16.1 9.4 %collective-permute-start = (f32[192,128]{1,0:T(8,128)S(1)}, f32[192,128]{1,0:T(8,128)S(1)}, u32[]{:S(2)}, u32[]{:S(2)}) collective-permute-start(f32[192,128]{1,0:T(8,128)S(1)} %get-tuple-element.27), channel_id=1, source_target_pairs={{0,1},{1,2},{2,3},{3,4},{4,5},{5,6},{6,7},{7,8},{8,9},{9,10},{10,1... | collective-permute-start | bytes 294920 | tf_op jit(solution)/shard_map/ppermute | solution.py:409
  19.4 8.7 %collective-permute-start.1 = (f32[192,128]{1,0:T(8,128)S(1)}, f32[192,128]{1,0:T(8,128)S(1)}, u32[]{:S(2)}, u32[]{:S(2)}) collective-permute-start(f32[192,128]{1,0:T(8,128)S(1)} %get-tuple-element.28), channel_id=1, source_target_pairs={{1,0},{2,1},{3,2},{4,3},{5,4},{6,5},{7,6},{8,7},{9,8},{10,9},{11,1... | collective-permute-start | bytes 294920 | tf_op jit(solution)/shard_map/ppermute | solution.py:409
  29.0 5.1 %collective-permute-start.2 = (f32[16,128]{1,0:T(8,128)S(1)}, f32[16,128]{1,0:T(8,128)S(1)}, u32[]{:S(2)}, u32[]{:S(2)}) collective-permute-start(f32[16,128]{1,0:T(8,128)S(1)} %get-tuple-element.32), channel_id=1, source_target_pairs={{0,16},{16,32},{32,48},{48,64},{64,80},{80,96},{96,112},{1,17},{17... | collective-permute-start | bytes 24584 | tf_op jit(solution)/shard_map/ppermute | solution.py:409
  31.5 5.0 %collective-permute-start.3 = (f32[16,128]{1,0:T(8,128)S(1)}, f32[16,128]{1,0:T(8,128)S(1)}, u32[]{:S(2)}, u32[]{:S(2)}) collective-permute-start(f32[16,128]{1,0:T(8,128)S(1)} %get-tuple-element.29), channel_id=1, source_target_pairs={{16,0},{32,16},{48,32},{64,48},{80,64},{96,80},{112,96},{17,1},{33... | collective-permute-start | bytes 24584 | tf_op jit(solution)/shard_map/ppermute | solution.py:409
  43.3 22.7 %all-to-all-start.1 = ((bf16[128,3,4,128]{3,2,1,0:T(4,128)(2,1)}), bf16[128,3,4,128]{3,2,1,0:T(4,128)(2,1)}, u32[]{:S(2)}, u32[]{:S(2)}) async-start(bf16[128,3,4,128]{3,2,1,0:T(4,128)(2,1)} %bitcast.30), calls=%async_computation.1 | async-start | bytes 786432 | tf_op jit(solution)/shard_map/all_to_all | solution.py:414
  53.5 18.9 %copy-start.1 = (f32[41,41]{1,0:T(8,128)S(1)}, f32[41,41]{1,0:T(8,128)}, u32[]{:S(2)}) copy-start(f32[41,41]{1,0:T(8,128)} %scale_ref.1) | copy-start | bytes 20176
  68.4 14.9 %all-to-all-start.2 = ((f32[128,1,384]{2,1,0:T(1,128)}), f32[128,1,384]{2,1,0:T(1,128)S(1)}, u32[]{:S(2)}, u32[]{:S(2)}) async-start(f32[128,1,384]{2,1,0:T(1,128)} %bitcast.31), calls=%async_computation.2 | async-start | bytes 393216 | tf_op jit(solution)/shard_map/all_to_all | solution.py:414
  72.4 0.8 copy-start.2

commit v4 on v3

--- a/solution.py
+++ b/solution.py
@@ -90,10 +90,40 @@
     return number, jnp.sum(jnp.where(iota((NB, NB), 0) == number, column, 0), axis=0, keepdims=True)
 
 
+PARTS = 3
+EDGE = 3
+CORNER = F * EDGE * EDGE
+FREE = 16
+CORNERS = ((-1, -1), (-1, 1), (1, -1), (1, 1))
+
+
+def neighbour(step):
+    x, y = lax.axis_index("gx") + step[0], lax.axis_index("gy") + step[1]
+    there = (x >= 0) & (x < GX) & (y >= 0) & (y < GY)
+    return jnp.where(there, x * GY + y, 0), there
+
+
+def corner_rows(s_ref, wide_ref):
+    lane, sub = iota((8, CELLS), 1), iota((8, CELLS), 0)
+    wide_ref[...] = jnp.zeros_like(wide_ref)
+    out = jnp.zeros((8, CELLS), f32)
+    for f in range(F):
+        wide_ref[:, :TY] = s_ref[f]
+        for k, (dx, dy) in enumerate(CORNERS):
+            for r in range(EDGE):
+                row = r if dx < 0 else 16 - EDGE + r
+                column = 0 if dy < 0 else TY - EDGE
+                at = FREE + (f * EDGE + r) * EDGE
+                moved = pltpu.roll(jnp.broadcast_to(wide_ref[row : row + 1, :], (8, CELLS)), (at - column) % CELLS, 1)
+                out = jnp.where((sub == k) & (lane >= at) & (lane < at + EDGE), moved, out)
+    high, mid, low = (x.astype(f32) for x in split3(out))
+    return high + pltpu.roll(mid, CORNER, 1) + pltpu.roll(low, 2 * CORNER, 1)
+
+
 def pack_kernel(
-    corner_ref, owner_ref, place_ref, parent_ref, s_ref, out_any, low_ref, high_ref, wide_ref, z_ref, out_ref, sems,
+    corner_ref, owner_ref, place_ref, parent_ref, s_any, out_any, s_ref, wide_ref, z_ref, out_ref, sems,
 ):
-    wide_ref[...] = jnp.zeros_like(wide_ref)
+    ends = fetch([(s_any.at[:, pl.ds(src, 8), :], s_ref.at[:, pl.ds(dst, 8), :]) for dst, src in ((0, 0), (8, TX - 8))], sems)
     cx, cy = corner_ref[0], corner_ref[1]
     base = pl.multiple_of(jnp.minimum(jnp.maximum(cx - 1, 0) // 16 * 16, PC - PROW), 16)
     owner = owner_ref[...]
@@ -103,8 +133,6 @@
     for s in range(CAP):
         value = jnp.sum(jnp.where(named & (rank == s), place_ref[...] + 1, 0).astype(f32), axis=1, keepdims=True) - 1.0
         slots = jnp.where(iota((DEV, CELLS), 1) == s, value, slots)
-    columns(s_ref, low_ref, high_ref, wide_ref)
-
     row = iota((GY * ROWS, 1), 0)
     j = row * 3277 >> 16
     r = row - j * ROWS
@@ -143,6 +171,17 @@
     for k, i in enumerate(LEFT):
         z_ref[pl.ds(i * GY * ROWS + WQ, GY, stride=ROWS), :] = left[k]
     z_ref[pl.ds(ROWS - 1, DEV, stride=ROWS), :] = slots
+    for copy in ends:
+        copy.wait()
+    corners = corner_rows(s_ref, wide_ref)
+    for k, step in enumerate(CORNERS):
+        other, there = neighbour(step)
+        at = pl.ds(other * ROWS + ROWS - 1, 1)
+
+        @pl.when(there)
+        def _():
+            z_ref[at, :] = z_ref[at, :] + corners[k : k + 1, :]
+
     write(z_ref, out_ref, out_any, sems, 4)
 
 
@@ -163,14 +202,17 @@
     return jnp.maximum(0.0, 1.0 - jnp.abs(centre - coarse.astype(f32)))
 
 
-def columns(s_ref, low_ref, high_ref, wide_ref):
+def strips_kernel(s_ref, low_ref, high_ref, top_ref, bottom_ref, wide_ref):
     field = iota((TX, CELLS), 1) >> 2
+    wide_ref[...] = jnp.zeros_like(wide_ref)
     low, high = jnp.zeros((TX, CELLS), f32), jnp.zeros((TX, CELLS), f32)
     for f in range(F):
         wide_ref[:, :TY] = s_ref[f]
         s = wide_ref[...]
         low = jnp.where(field == f, s if f == 0 else pltpu.roll(s, HALO * f, 1), low)
         high = jnp.where(field == f, pltpu.roll(s, CELLS - TY + HALO + HALO * f, 1), high)
+        top_ref[f * HALO : (f + 1) * HALO, :] = pltpu.roll(s[:8], HALO, 1)[:HALO]
+        bottom_ref[f * HALO : (f + 1) * HALO, :] = pltpu.roll(s[TX - 8 :], HALO, 1)[HALO:]
     low_ref[...] = low
     high_ref[...] = high
 
@@ -183,23 +225,8 @@
     return jnp.where(lane < HALO, before, jnp.where(lane < TY + 2 * HALO, wide, 0.0))
 
 
-def rows_kernel(s_any, left_ref, right_ref, low_ref, high_ref, s_ref, wide_ref, sems):
-    ends = ((0, 0), (8, TX - 8))
-    for copy in fetch([(s_any.at[:, pl.ds(src, 8), :], s_ref.at[:, pl.ds(dst, 8), :]) for dst, src in ends], sems):
-        copy.wait()
-    left = jnp.concatenate([left_ref[:8, :], left_ref[TX - 8 :, :]], axis=0)
-    right = jnp.concatenate([right_ref[:8, :], right_ref[TX - 8 :, :]], axis=0)
-    wide_ref[...] = jnp.zeros_like(wide_ref)
-    for f in range(F):
-        wide_ref[:, :TY] = s_ref[f]
-        wide = widened(wide_ref[...], left, right, f)
-        low_ref[f * HALO : (f + 1) * HALO, :] = wide[:HALO]
-        high_ref[f * HALO : (f + 1) * HALO, :] = wide[16 - HALO :]
-
-
-def ready_kernel(
-    holder_ref, corner_ref, owner_ref, s_ref, left_ref, right_ref, before_ref, after_ref,
-    wx_ref, wlast_ref, mask_ref, wy_ref, wyc_ref, send_ref, back_ref, state_ref, wide_ref,
+def tables_kernel(
+    holder_ref, corner_ref, owner_ref, wx_ref, wlast_ref, mask_ref, wy_ref, wyc_ref, send_ref, back_ref
 ):
     ix, iy = lax.axis_index("gx"), lax.axis_index("gy")
     cx, cy = corner_ref[0], corner_ref[1]
@@ -217,39 +244,65 @@
     wy_ref[...] = jnp.where((at >= 0) & (at < WQ), hat(iota((CELLS, GROUP), 0) + y0, cy, at + qy), 0.0).astype(bf16)
     lane = iota((CELLS, CELLS), 1)
     wyc_ref[...] = hat(iota((CELLS, CELLS), 0) + y0, cy, qy + ((lane - qy) & (WP - 1))).astype(bf16)
-    wide_ref[...] = jnp.zeros_like(wide_ref)
     column = column_of(owner_ref[...])
     number, owner = by_thirds(column)
     rank = rank_of(column, owner, number)
     send_ref[...] = (iota((CAP * DEV, NB), 0) == rank * DEV + owner).astype(f32).astype(bf16)
     back_ref[...] = (column_of(owner * CAP + rank) == iota((NB, CAP * DEV), 1)).astype(f32).astype(bf16)
-    left, right = left_ref[...], right_ref[...]
-    for f in range(F):
-        wide_ref[:, :TY] = s_ref[f]
-        state_ref[f, :HALO, :] = before_ref[f * HALO : (f + 1) * HALO, :]
-        state_ref[f, HALO : HALO + TX, :] = widened(wide_ref[...], left, right, f)
-        state_ref[f, HALO + TX :, :] = after_ref[f * HALO : (f + 1) * HALO, :]
+
+
+def corner_of(got_ref, step):
+    other, there = neighbour(step)
+    rows = got_ref[pl.ds(pl.multiple_of((other >> 2) * GROUP, 16), GROUP), :].astype(f32)
+    mine = jnp.where(there, (other & 3) * ROWS + ROWS - 1, -1)
+    row = jnp.sum(jnp.where(iota((GROUP, CELLS), 0) == mine, rows, 0.0), axis=0, keepdims=True)
+    row = jnp.broadcast_to(row, (8, CELLS))
+    return row + pltpu.roll(row, CELLS - CORNER, 1) + pltpu.roll(row, CELLS - 2 * CORNER, 1)
 
 
 def nest_kernel(
-    holder_ref, got_ref, wx_ref, wlast_ref, mask_ref, wy_ref, wyc_ref, send_ref, begin_ref, skin_ref, next_any, out_any,
-    next_ref, out_ref, state_ref, force_ref, flux_ref, z_ref, sems,
+    wait, holder_ref, got_ref, wx_ref, wlast_ref, mask_ref, wy_ref, wyc_ref, send_ref, s_ref, left_ref, right_ref,
+    before_ref, after_ref, skin_ref, next_any, out_any,
+    wide_ref, next_ref, out_ref, state_ref, force_ref, flux_ref, z_ref, sems,
 ):
+    wide_ref[...] = jnp.zeros_like(wide_ref)
+    corners = [corner_of(got_ref, step) for step in CORNERS]
     group = pl.multiple_of((holder_ref[0] >> 2) * GROUP, 16)
     got = got_ref[pl.ds(group, GROUP), :]
+    wait(5)
     partial = dot(wy_ref[...], got).astype(bf16)
     last = jnp.sum(
         jnp.where(iota((GROUP, CELLS), 0) == (holder_ref[0] & 3) * ROWS + WQ, got.astype(f32), 0.0), axis=0, keepdims=True
     )
     last = jnp.where(iota((8, CELLS), 1) >> 5 == iota((8, CELLS), 0), last, 0.0).astype(bf16)
+    wait(6)
     partial_last = dot_nt(last, wyc_ref[...]).astype(bf16).astype(f32)
+    wait(2)
     force_ref[...] = dot_nt(wx_ref[...], partial)
     flux_ref[...] = jnp.zeros_like(flux_ref)
+    for k in (3, 4, 8):
+        wait(k)
     mask = mask_ref[...]
+    left, right = left_ref[...], right_ref[...]
+    lane, sub = iota((8, CELLS), 1), iota((8, CELLS), 0)
     written = []
     for f in range(F):
         force = relax_coef * force_ref[f * ROWS_X : (f + 1) * ROWS_X, :] + wlast_ref[...] * partial_last[f : f + 1, :]
-        s = begin_ref[f]
+        wide_ref[:, :TY] = s_ref[f]
+        state_ref[:HALO, :] = before_ref[f * HALO : (f + 1) * HALO, :]
+        state_ref[HALO : HALO + TX, :] = widened(wide_ref[...], left, right, f)
+        state_ref[HALO + TX :, :] = after_ref[f * HALO : (f + 1) * HALO, :]
+        for side, base in ((-1, 0), (1, ROWS_X - 8)):
+            tile = state_ref[base : base + 8, :]
+            for k, (dx, dy) in enumerate(CORNERS):
+                for r in range(EDGE if dx == side else 0):
+                    row = HALO - EDGE + r if dx < 0 else 8 - HALO + r
+                    column = HALO - EDGE if dy < 0 else HALO + TY
+                    at = FREE + (f * EDGE + r) * EDGE
+                    moved = pltpu.roll(corners[k], (column - at) % CELLS, 1)
+                    tile = jnp.where((sub == row) & (lane >= column) & (lane < column + EDGE), moved, tile)
+            state_ref[base : base + 8, :] = tile
+        s = state_ref[...]
         for _ in range(STEPS):
             beside = (
                 pltpu.roll(s, 1, 0) + pltpu.roll(s, ROWS_X - 1, 0) + pltpu.roll(s, 1, 1) + pltpu.roll(s, CELLS - 1, 1)
@@ -261,6 +314,7 @@
         written[f].start()
     u, v, ta, qa = next_ref[0], next_ref[1], next_ref[2], next_ref[3]
     half = drag_coefficient * jnp.sqrt(1.0 + u * u + v * v)
+    wait(13)
     skin = skin_ref[...]
     flux = (half * (ta - skin), half * (qa - 0.5 * skin), half * u, half * v)
     rows = NB // CAP
@@ -275,6 +329,7 @@
                 [jnp.where(lane < 96, m[0], r1), jnp.where(lane < 64, r1, r2), jnp.where(lane < 32, r2, r3)], axis=0
             ).astype(bf16)
         )
+    wait(7)
     sent = dot(send_ref[...], jnp.concatenate(blocks, axis=1))
     for slot in range(CAP):
         for f in range(F):
@@ -364,7 +419,7 @@
 SPACES = {"h": pltpu.HBM, "v": pltpu.VMEM, "H": pltpu.HBM, "S": pltpu.HBM, "p": pltpu.VMEM, "s": pltpu.SMEM}
 
 
-def call(kernel, ins, outs, args, shapes, scratch=(), copies=0):
+def call(kernel, ins, outs, args, shapes, scratch=(), copies=0, lazy=False):
     args = [pltpu.with_memory_space_constraint(a, MEMORY[c]) if c in MEMORY else a for c, a in zip(ins, args)]
     letters = ins + outs
     kinds = [(a.shape, a.dtype) for a in args] + list(shapes)
@@ -377,14 +432,15 @@
         far = [arrays[k] for k in moved]
         for n, k in enumerate(moved):
             arrays[k] = rest[own + n]
-        pending = [
-            pltpu.make_async_copy(far[n], arrays[k], sems.at[n]) for n, k in enumerate(moved) if k < len(ins)
-        ]
-        for copy in pending:
+        pending = {k: pltpu.make_async_copy(far[n], arrays[k], sems.at[n]) for n, k in enumerate(moved) if k < len(ins)}
+        for copy in pending.values():
             copy.start()
-        for copy in pending:
-            copy.wait()
-        kernel(*arrays, *rest[:own])
+        if lazy:
+            kernel(lambda k: pending[k].wait(), *arrays, *rest[:own])
+        else:
+            for copy in pending.values():
+                copy.wait()
+            kernel(*arrays, *rest[:own])
         done = [pltpu.make_async_copy(arrays[k], far[n], sems.at[n]) for n, k in enumerate(moved) if k >= len(ins)]
         for copy in done:
             copy.start()
@@ -433,34 +489,31 @@
     owner = exchange_patch_holder.reshape(1, NB)
     place = holder_patch_position.reshape(1, NB)
     names, message, tile, strip = ((1, NB), i32), ((DEV * ROWS, CELLS), bf16), ((F, TX, TY), f32), ((TX, CELLS), f32)
-    windows, low, high = call(
-        pack_kernel, "SHHHH", "hvv",
-        (corner_offset, owner, place, coarse_lowest_values, fine_atmospheric_values), (message, strip, strip),
-        (strip, ((DEV * ROWS, CELLS), f32), message), 4,
-    )
+    (windows,) = call(
+        pack_kernel, "SHHHh", "h", (corner_offset, owner, place, coarse_lowest_values, fine_atmospheric_values), (message,),
+        (((F, 16, TY), f32), ((16, CELLS), f32), ((DEV * ROWS, CELLS), f32), message), 4,
+    )
+    got = exchange(windows, (DEV, ROWS // 4, 4, CELLS))
+    present, _ = lax.optimization_barrier((fine_atmospheric_values, windows))
+    ends = ((F * HALO, CELLS), f32)
+    low, high, top, bottom = call(strips_kernel, "H", "vvvv", (present,), (strip, strip, ends, ends), (strip,))
     left, right = shift(high, "gy", 1), shift(low, "gy", -1)
-    got = exchange(windows, (DEV, ROWS // 4, 4, CELLS))
-    ends = ((F * HALO, CELLS), f32)
-    low, high = call(
-        rows_kernel, "hvv", "vv", (fine_atmospheric_values, left, right), (ends, ends),
-        (((F, 16, TY), f32), ((16, CELLS), f32)), 2,
-    )
-    before, after = shift(high, "gx", 1), shift(low, "gx", -1)
-    holder, _ = lax.optimization_barrier((holder_flat, low))
+    before, after = shift(bottom, "gx", 1), shift(top, "gx", -1)
+    holder, corner, _ = lax.optimization_barrier((holder_flat, corner_offset, windows))
     holder = jnp.minimum(holder, DEV - 1)
     wide = (ROWS_X, CELLS)
-    *weights, send, back, state = call(
-        ready_kernel, "sSHHvvvv", "HHHHHHHH",
-        (holder, corner_offset, owner, fine_atmospheric_values, left, right, before, after),
+    *weights, send, back = call(
+        tables_kernel, "sSH", "HHHHHHH", (holder, corner, owner),
         (
             ((F * ROWS_X, CELLS), bf16), (wide, f32), (wide, f32), ((CELLS, GROUP), bf16), ((CELLS, CELLS), bf16),
-            ((CAP * DEV, NB), bf16), ((NB, CAP * DEV), bf16), ((F,) + wide, f32),
-        ), (strip,),
+            ((CAP * DEV, NB), bf16), ((NB, CAP * DEV), bf16),
+        ),
     )
     sent = ((DEV * CAP * F, CELLS), bf16)
     nest_next, flux = call(
-        nest_kernel, "svHHHHHHHH", "hh", (holder, got, *weights, send, state, fine_skin_heat), (tile, sent),
-        (tile, sent, (wide, f32), ((F * ROWS_X, CELLS), f32), strip, ((DEV * CAP * F, CELLS), f32)), F,
+        nest_kernel, "svHHHHHHHvvvvH", "hh",
+        (holder, got, *weights, send, fine_atmospheric_values, left, right, before, after, fine_skin_heat), (tile, sent),
+        (strip, tile, sent, (wide, f32), ((F * ROWS_X, CELLS), f32), strip, ((DEV * CAP * F, CELLS), f32)), F, True,
     )
     got_flux = exchange(flux, (DEV, CAP, F, CELLS))
     layers = marine_stratum_values.shape[1]
@@ -472,10 +525,10 @@
         hot_kernel, "vH", "HHHH", (got_late, by_block(coarse_interface_exchange)), (hot, give, block, block),
         (((DEV * CAP * F, OCEAN * F), f32), ((DEV * ROWS, CELLS), f32), ((DEV * CAP, OCEAN * F), f32)),
     )
-    (top,) = call(top_kernel, "Sp", "H", (diffusion_solver_operator, marine_late), (((OCEAN * F + 8, CELLS), f32),))
+    (layer0,) = call(top_kernel, "Sp", "H", (diffusion_solver_operator, marine_late), (((OCEAN * F + 8, CELLS), f32),))
     returned = ((DEV * CAP, CELLS), f32)
     forcing, skins = call(
-        ocean_kernel, "HHHHHH", "HH", (got_flux, hot, inverse, cover, top, give), (block, returned)
+        ocean_kernel, "HHHHHH", "HH", (got_flux, hot, inverse, cover, layer0, give), (block, returned)
     )
     arrived = exchange(skins, (DEV, 1, CAP * CELLS))
     part = 32

time: 85.8 us -> 79.1 us (0.922)
  waiting for transfers between devices: 23.6 us -> 15.2 us
  starting transfers between devices: 34.7 us -> 35.7 us
    ppermute x4, waiting for transfers between devices: 9.82 us -> 0.79 us  [shift(): lax.ppermute(value, axis, [(i, i + by) for i in range(n) if 0 <= i + by <...]
    ppermute x4, starting transfers between devices: 9.01 us -> 10.1 us  [shift(): lax.ppermute(value, axis, [(i, i + by) for i in range(n) if 0 <= i + by <...]
  transfers between devices with their start and end apart: 7 -> 7, of which waited for: 5 -> 4; matrix products, arithmetic and copies ran while one was open for 0% -> 0% of each run, Pallas kernels for 14% -> 15%
where the time goes in v4:
time: 79.1 us; the launch traced here: 78.4 us
  starting transfers between devices  35.7 us (45%)
  Pallas kernels  25.3 us (32%)
  waiting for transfers between devices  15.2 us (19%)
  between operations  1.44 us (2%)
  local copies, waits for them, and re-layouts  0.85 us (1%)
    all_to_all x3, starting transfers between devices, exchange(): lax.all_to_all(split, ('gx', 'gy'), split_axis=0, concat_axis=0, tiled=True)  25.6 us
    pallas_call x8, Pallas kernels, call(): pl.pallas_call(body, out_shape=tuple((MEMORY[c](s, d) if c in MEMORY else...  20.7 us
    all_to_all x3, waiting for transfers between devices, exchange(): lax.all_to_all(split, ('gx', 'gy'), split_axis=0, concat_axis=0, tiled=True)  14.4 us
    ppermute x4, starting transfers between devices, shift(): lax.ppermute(value, axis, [(i, i + by) for i in range(n) if 0 <= i + by <...  10.1 us
    pallas_call x1, Pallas kernels, on_device(): pl.pallas_call(mix_kernel, out_shape=jax.ShapeDtypeStruct((layers, OCEAN...  4.54 us
  transfers between devices with their start and end apart: 7, of which 4 were waited for; matrix products, arithmetic and copies ran while one was open for 0% of the time, Pallas kernels for 15%

profile of v4, /device:TPU:1, one launch (start us, length us, event | category | flops | bytes accessed | tf_op | source)
XLA Modules:
  0.0 78.4 jit_solution(3394021409277572168)
XLA Ops:
  0.6 4.0 %shard_map.121 = bf16[2560,128]{1,0:T(8,128)(2,1)} custom-call(s32[2]{0:T(128)} %refs_1_, s32[1,144]{1,0:T(1,128)} %bitcast.33, s32[1,144]{1,0:T(1,128)} %bitcast.35, bf16[4,384,384]{2,1,0:T(8,128)(2,1)} %refs_3_.1, f32[4,192,96]{2,1,0:T(8,128)} %refs_8_.1), custom_call_target="tpu_custom_call" | custom-call | tf_op jit(solution)/shard_map/pallas_call | solution.py:450
  4.6 0.0 copy-start
  4.6 11.5 %all-to-all-start = ((bf16[128,5,4,128]{3,2,1,0:T(4,128)(2,1)}), bf16[128,5,4,128]{3,2,1,0:T(4,128)(2,1)S(1)}, u32[]{:S(2)}, u32[]{:S(2)}) async-start(bf16[128,5,4,128]{3,2,1,0:T(4,128)(2,1)} %bitcast.29), calls=%async_computation | async-start | bytes 1310720 | tf_op jit(solution)/shard_map/all_to_all | solution.py:470
  16.1 1.3 %shard_map.123 = (f32[192,128]{1,0:T(8,128)S(1)}, f32[192,128]{1,0:T(8,128)S(1)}, f32[16,128]{1,0:T(8,128)S(1)}, f32[16,128]{1,0:T(8,128)S(1)}) custom-call(f32[4,192,96]{2,1,0:T(8,128)} %refs_8_.1), custom_call_target="tpu_custom_call" | custom-call | tf_op jit(solution)/shard_map/pallas_call | solution.py:450
  17.4 3.3 %collective-permute-start = (f32[192,128]{1,0:T(8,128)S(1)}, f32[192,128]{1,0:T(8,128)S(1)}, u32[]{:S(2)}, u32[]{:S(2)}) collective-permute-start(f32[192,128]{1,0:T(8,128)S(1)} %get-tuple-element.36), channel_id=1, source_target_pairs={{0,1},{1,2},{2,3},{3,4},{4,5},{5,6},{6,7},{7,8},{8,9},{9,10},{10,1... | collective-permute-start | bytes 294920 | tf_op jit(solution)/shard_map/ppermute | solution.py:465
  20.7 1.3 %collective-permute-start.1 = (f32[192,128]{1,0:T(8,128)S(1)}, f32[192,128]{1,0:T(8,128)S(1)}, u32[]{:S(2)}, u32[]{:S(2)}) collective-permute-start(f32[192,128]{1,0:T(8,128)S(1)} %get-tuple-element.37), channel_id=1, source_target_pairs={{1,0},{2,1},{3,2},{4,3},{5,4},{6,5},{7,6},{8,7},{9,8},{10,9},{11,1... | collective-permute-start | bytes 294920 | tf_op jit(solution)/shard_map/ppermute | solution.py:465
  22.0 3.6 %collective-permute-start.2 = (f32[16,128]{1,0:T(8,128)S(1)}, f32[16,128]{1,0:T(8,128)S(1)}, u32[]{:S(2)}, u32[]{:S(2)}) collective-permute-start(f32[16,128]{1,0:T(8,128)S(1)} %get-tuple-element.38), channel_id=1, source_target_pairs={{0,16},{16,32},{32,48},{48,64},{64,80},{80,96},{96,112},{1,17},{17... | collective-permute-start | bytes 24584 | tf_op jit(solution)/shard_map/ppermute | solution.py:465
  25.7 1.9 %collective-permute-start.3 = (f32[16,128]{1,0:T(8,128)S(1)}, f32[16,128]{1,0:T(8,128)S(1)}, u32[]{:S(2)}, u32[]{:S(2)}) collective-permute-start(f32[16,128]{1,0:T(8,128)S(1)} %get-tuple-element.39), channel_id=1, source_target_pairs={{16,0},{32,16},{48,32},{64,48},{80,64},{96,80},{112,96},{17,1},{33... | collective-permute-start | bytes 24584 | tf_op jit(solution)/shard_map/ppermute | solution.py:465
  28.2 1.9 %shard_map.122 = (bf16[800,128]{1,0:T(8,128)(2,1)}, f32[200,128]{1,0:T(8,128)}, f32[200,128]{1,0:T(8,128)}, bf16[128,80]{1,0:T(8,128)(2,1)}, bf16[128,128]{1,0:T...) custom-call(s32[1]{0:T(128)S(6)} %min.3.refs_0_, s32[2]{0:T(128)} %refs_1_, s32[1,144]{1,0:T(1,128)} %bitcast.34), custom_call_target="tpu_custom_call" | custom-call | tf_op jit(solution)/shard_map/pallas_call | solution.py:450
  30.1 0.8 collective-permute-done.3.refs_12_
  30.9 0.6 all-to-all-done
  31.5 5.1 %shard_map.124 = (f32[4,192,96]{2,1,0:T(8,128)}, bf16[1536,128]{1,0:T(8,128)(2,1)}) custom-call(s32[1]{0:T(128)S(6)} %min.3.refs_0_, bf16[2560,128]{1,0:T(8,128)(2,1)S(1)} %bitcast.25, bf16[800,128]{1,0:T(8,128)(2,1)} %get-tuple-element.29.refs_2_, f32[200,128]{1,0:T(8,128)} %get-tuple-element.30.refs_3_, f32[200,128]{1,0:T(8,128)} %get-tuple-element.31.refs_4_, ...), custom_call_target="tpu_custom_call" | custom-call | tf_op jit(solution)/shard_map/pallas_call | solution.py:450
  36.7 10.1 %all-to-all-start.1 = ((bf16[128,3,4,128]{3,2,1,0:T(4,128)(2,1)}), bf16[128,3,4,128]{3,2,1,0:T(4,128)(2,1)}, u32[]{:S(2)}, u32[]{:S(2)}) async-start(bf16[128,3,4,128]{3,2,1,0:T(4,128)(2,1)} %bitcast.30), calls=%async_computation.1 | async-start | bytes 786432 | tf_op jit(solution)/shard_map/all_to_all | solution.py:470
  46.8 0.0 copy-start.1
  46.8 2.3 %shard_map.125 = (bf16[128,1536]{1,0:T(8,128)(2,1)}, bf16[384,128]{1,0:T(8,128)(2,1)}, f32[128,128]{1,0:T(8,128)}, f32[128,128]{1,0:T(8,128)}) custom-call(bf16[2560,128]{1,0:T(8,128)(2,1)S(1)} %bitcast.26, f32[128,128]{1,0:T(8,128)} %bitcast.32), custom_call_target="tpu_custom_call" | custom-call | tf_op jit(solution)/shard_map/pallas_call | solution.py:450
  49.1 1.9 %shard_map.126.refs_4_ = f32[136,128]{1,0:T(8,128)} custom-call(f32[41,41]{1,0:T(8,128)} %scale_ref.1, f32[41,128,128]{2,1,0:T(8,128)S(1)} %bitcast.23), custom_call_target="tpu_custom_call" | custom-call | tf_op jit(solution)/shard_map/pallas_call | solution.py:450
  51.0 8.3 %all-to-all-done.1 = bf16[128,3,4,128]{3,2,1,0:T(4,128)(2,1)} async-done(((bf16[128,3,4,128]{3,2,1,0:T(4,128)(2,1)}), bf16[128,3,4,128]{3,2,1,0:T(4,128)(2,1)}, u32[]{:S(2)}, u32[]{:S(2)}) %all-to-all-start.1) | async-done | bytes 393248 | tf_op jit(solution)/shard_map/all_to_all | solution.py:470
  59.3 2.4 %shard_map.127 = (f32[128,128]{1,0:T(8,128)}, f32[384,128]{1,0:T(8,128)}) custom-call(bf16[1536,128]{1,0:T(8,128)(2,1)} %bitcast.5.refs_0_, bf16[128,1536]{1,0:T(8,128)(2,1)} %get-tuple-element.43.refs_1_, f32[128,128]{1,0:T(8,128)} %get-tuple-element.44.refs_2_, f32[128,128]{1,0:T(8,128)} %get-tuple-element.45.refs_3_, f32[136,128]{1,0:T(8,128)} %shard_map.126.refs_4_, ...), custom_call_target="tpu_custom_call" | custom-call | tf_op jit(solution)/shard_map/pallas_call | solution.py:450
  61.7 4.0 %all-to-all-start.2 = ((f32[128,1,384]{2,1,0:T(1,128)}), f32[128,1,384]{2,1,0:T(1,128)S(1)}, u32[]{:S(2)}, u32[]{:S(2)}) async-start(f32[128,1,384]{2,1,0:T(1,128)} %bitcast.31), calls=%async_computation.2 | async-start | bytes 393216 | tf_op jit(solution)/shard_map/all_to_all | solution.py:470
  65.7 0.0 copy-start.2
  65.7 0.8 %copy-done.2 = f32[128,128]{1,0:T(8,128)S(1)} copy-done((f32[128,128]{1,0:T(8,128)S(1)}, f32[128,128]{1,0:T(8,128)}, u32[]{:S(2)}) %copy-start.2) | copy-done | bytes 65560
  66.5 4.5 %shard_map.128 = f32[41,128,128]{2,1,0:T(8,128)} custom-call(f32[41,41]{1,0:T(8,128)S(1)} %copy-done.1, f32[128,128]{1,0:T(8,128)S(1)} %copy-done.2, f32[41,128,128]{2,1,0:T(8,128)S(1)} %bitcast.24), custom_call_target="tpu_custom_call" | custom-call | tf_op jit(solution)/shard_map/pallas_call | solution.py:535
  71.1 5.5 %all-to-all-done.2 = f32[128,1,384]{2,1,0:T(1,128)S(1)} async-done(((f32[128,1,384]{2,1,0:T(1,128)}), f32[128,1,384]{2,1,0:T(1,128)S(1)}, u32[]{:S(2)}, u32[]{:S(2)}) %all-to-all-start.2) | async-done | bytes 196640 | tf_op jit(solution)/shard_map/all_to_all | solution.py:470
  76.6 1.9 %shard_map.129 = f32[192,96]{1,0:T(8,128)} custom-call(f32[384,128]{1,0:T(8,128)S(1)} %bitcast.27, bf16[144,384]{1,0:T(8,128)(2,1)} %get-tuple-element.50.refs_1_), custom_call_target="tpu_custom_call" | custom-call | tf_op jit(solution)/shard_map/pallas_call | solution.py:450
  (5 shorter events, 0.0 us)
Async XLA Ops:
  4.6 44.5 %copy-start = (f32[4,41,4096]{2,0,1:T(4,128)S(1)}, f32[4,41,4096]{2,0,1:T(4,128)}, u32[]{:S(2)}) copy-start(f32[4,41,4096]{2,0,1:T(4,128)} %param.18) | copy-start | bytes 8060932
  4.6 26.9 %all-to-all-start = ((bf16[128,5,4,128]{3,2,1,0:T(4,128)(2,1)}), bf16[128,5,4,128]{3,2,1,0:T(4,128)(2,1)S(1)}, u32[]{:S(2)}, u32[]{:S(2)}) async-start(bf16[128,5,4,128]{3,2,1,0:T(4,128)(2,1)} %bitcast.29), calls=%async_computation | async-start | bytes 1310720 | tf_op jit(solution)/shard_map/all_to_all | solution.py:470
  17.4 13.5 %collective-permute-start = (f32[192,128]{1,0:T(8,128)S(1)}, f32[192,128]{1,0:T(8,128)S(1)}, u32[]{:S(2)}, u32[]{:S(2)}) collective-permute-start(f32[192,128]{1,0:T(8,128)S(1)} %get-tuple-element.36), channel_id=1, source_target_pairs={{0,1},{1,2},{2,3},{3,4},{4,5},{5,6},{6,7},{7,8},{8,9},{9,10},{10,1... | collective-permute-start | bytes 294920 | tf_op jit(solution)/shard_map/ppermute | solution.py:465
  20.7 10.2 %collective-permute-start.1 = (f32[192,128]{1,0:T(8,128)S(1)}, f32[192,128]{1,0:T(8,128)S(1)}, u32[]{:S(2)}, u32[]{:S(2)}) collective-permute-start(f32[192,128]{1,0:T(8,128)S(1)} %get-tuple-element.37), channel_id=1, source_target_pairs={{1,0},{2,1},{3,2},{4,3},{5,4},{6,5},{7,6},{8,7},{9,8},{10,9},{11,1... | collective-permute-start | bytes 294920 | tf_op jit(solution)/shard_map/ppermute | solution.py:465
  22.0 8.1 %collective-permute-start.2 = (f32[16,128]{1,0:T(8,128)S(1)}, f32[16,128]{1,0:T(8,128)S(1)}, u32[]{:S(2)}, u32[]{:S(2)}) collective-permute-start(f32[16,128]{1,0:T(8,128)S(1)} %get-tuple-element.38), channel_id=1, source_target_pairs={{0,16},{16,32},{32,48},{48,64},{64,80},{80,96},{96,112},{1,17},{17... | collective-permute-start | bytes 24584 | tf_op jit(solution)/shard_map/ppermute | solution.py:465
  25.7 5.3 %collective-permute-start.3 = (f32[16,128]{1,0:T(8,128)S(1)}, f32[16,128]{1,0:T(8,128)S(1)}, u32[]{:S(2)}, u32[]{:S(2)}) collective-permute-start(f32[16,128]{1,0:T(8,128)S(1)} %get-tuple-element.39), channel_id=1, source_target_pairs={{16,0},{32,16},{48,32},{64,48},{80,64},{96,80},{112,96},{17,1},{33... | collective-permute-start | bytes 24584 | tf_op jit(solution)/shard_map/ppermute | solution.py:465
  36.7 22.6 %all-to-all-start.1 = ((bf16[128,3,4,128]{3,2,1,0:T(4,128)(2,1)}), bf16[128,3,4,128]{3,2,1,0:T(4,128)(2,1)}, u32[]{:S(2)}, u32[]{:S(2)}) async-start(bf16[128,3,4,128]{3,2,1,0:T(4,128)(2,1)} %bitcast.30), calls=%async_computation.1 | async-start | bytes 786432 | tf_op jit(solution)/shard_map/all_to_all | solution.py:470
  46.8 18.9 %copy-start.1 = (f32[41,41]{1,0:T(8,128)S(1)}, f32[41,41]{1,0:T(8,128)}, u32[]{:S(2)}) copy-start(f32[41,41]{1,0:T(8,128)} %scale_ref.1) | copy-start | bytes 20176
  61.7 14.9 %all-to-all-start.2 = ((f32[128,1,384]{2,1,0:T(1,128)}), f32[128,1,384]{2,1,0:T(1,128)S(1)}, u32[]{:S(2)}, u32[]{:S(2)}) async-start(f32[128,1,384]{2,1,0:T(1,128)} %bitcast.31), calls=%async_computation.2 | async-start | bytes 393216 | tf_op jit(solution)/shard_map/all_to_all | solution.py:470
  65.7 0.8 %copy-start.2 = (f32[128,128]{1,0:T(8,128)S(1)}, f32[128,128]{1,0:T(8,128)}, u32[]{:S(2)}) copy-start(f32[128,128]{1,0:T(8,128)} %get-tuple-element.48.forcing_ref) | copy-start | bytes 196612

commit v5 on v4

--- a/solution.py
+++ b/solution.py
@@ -17,6 +17,7 @@
 NB = 144
 HALO = 4
 ROWS_X = TX + 2 * HALO
+PAD = 8
 WP = 32
 WQ = 18
 ROWS = 20
@@ -121,11 +122,24 @@
 
 
 def pack_kernel(
-    corner_ref, owner_ref, place_ref, parent_ref, s_any, out_any, s_ref, wide_ref, z_ref, out_ref, sems,
+    wait, corner_ref, owner_ref, place_ref, parent_ref, s_any, out_any, s_ref, wide_ref, pick_ref, z_ref, out_ref, sems,
 ):
     ends = fetch([(s_any.at[:, pl.ds(src, 8), :], s_ref.at[:, pl.ds(dst, 8), :]) for dst, src in ((0, 0), (8, TX - 8))], sems)
+    wait(0)
     cx, cy = corner_ref[0], corner_ref[1]
     base = pl.multiple_of(jnp.minimum(jnp.maximum(cx - 1, 0) // 16 * 16, PC - PROW), 16)
+    row = iota((GY * ROWS, 1), 0)
+    j = row * 3277 >> 16
+    r = row - j * ROWS
+    wanted = jnp.where(r < WQ, cy + first_y_of(j) + r, -1)
+    pick_y = (wanted == iota((GY * ROWS, PC), 1)).astype(f32).astype(bf16)
+    lane = iota((1, 2 * CELLS), 1)
+    for f in range(F):
+        i = (lane >> 7) * F + (((lane >> 5) - f) & 3)
+        p = cx - base + first_x_of(i) + (lane & (WP - 1))
+        pick_ref[f] = (iota((PROW, 2 * CELLS), 0) == p).astype(f32).astype(bf16)
+    wait(1)
+    wait(2)
     owner = owner_ref[...]
     rank = rank_of(column_of(owner), owner, iota((NB, NB), 1))
     named = iota((DEV, NB), 0) == owner
@@ -133,23 +147,15 @@
     for s in range(CAP):
         value = jnp.sum(jnp.where(named & (rank == s), place_ref[...] + 1, 0).astype(f32), axis=1, keepdims=True) - 1.0
         slots = jnp.where(iota((DEV, CELLS), 1) == s, value, slots)
-    row = iota((GY * ROWS, 1), 0)
-    j = row * 3277 >> 16
-    r = row - j * ROWS
-    wanted = jnp.where(r < WQ, cy + first_y_of(j) + r, -1)
-    pick_y = (wanted == iota((GY * ROWS, PC), 1)).astype(f32).astype(bf16)
+    for copy in ends:
+        copy.wait()
+    corners = corner_rows(s_ref, wide_ref)
+    for k, step in enumerate(CORNERS):
+        other, there = neighbour(step)
+        slots = slots + jnp.where(iota((DEV, CELLS), 0) == jnp.where(there, other, -1), corners[k : k + 1, :], 0.0)
+    wait(3)
     parts = [parent_ref[f, pl.ds(base, PROW), :] for f in range(F)]
-    across = jnp.concatenate([dot_nt(pick_y, parts[f]).astype(bf16) for f in range(F)], axis=1)
-    lane = iota((1, 2 * CELLS), 1)
-    for pair in range(GX // 2):
-        first = jnp.where(lane < CELLS, first_x(2 * pair), first_x(2 * pair + 1))
-        p = cx - base + first + (lane & (WP - 1))
-        target = jnp.where((p >= 0) & (p < PROW), (lane >> 5 & 3) * PROW + p, -1)
-        pick_x = (iota((F * PROW, 2 * CELLS), 0) == target).astype(f32).astype(bf16)
-        window = dot(across, pick_x)
-        for k in range(2):
-            i = 2 * pair + k
-            z_ref[pl.ds(i * GY * ROWS, GY * ROWS), :] = window[:, k * CELLS : (k + 1) * CELLS]
+    windows = [dot(dot_nt(pick_y, parts[f]).astype(bf16), pick_ref[f]) for f in range(F)]
     j16 = iota((GY, PC), 0)
     q = iota((GY, PC), 1) - (cy + first_y_of(j16))
     inside = (q >= 0) & (q < WQ)
@@ -168,38 +174,37 @@
             folded = folded + pltpu.roll(folded, 64, 1)
             folded = folded + pltpu.roll(folded, 32, 1)
             left[k] = jnp.where(lanes == f, folded, left[k])
-    for k, i in enumerate(LEFT):
-        z_ref[pl.ds(i * GY * ROWS + WQ, GY, stride=ROWS), :] = left[k]
-    z_ref[pl.ds(ROWS - 1, DEV, stride=ROWS), :] = slots
-    for copy in ends:
-        copy.wait()
-    corners = corner_rows(s_ref, wide_ref)
-    for k, step in enumerate(CORNERS):
-        other, there = neighbour(step)
-        at = pl.ds(other * ROWS + ROWS - 1, 1)
-
-        @pl.when(there)
-        def _():
-            z_ref[at, :] = z_ref[at, :] + corners[k : k + 1, :]
-
-    write(z_ref, out_ref, out_any, sems, 4)
-
-
-def write(z_ref, out_ref, out_any, sems, parts):
-    rows = z_ref.shape[0] // parts
     copies = []
-    for k in range(parts):
-        at = pl.ds(k * rows, rows)
-        out_ref[at, :] = z_ref[at, :].astype(bf16)
-        copies.append(pltpu.make_async_copy(out_ref.at[at, :], out_any.at[at, :], sems.at[k]))
-        copies[k].start()
+    size = 2 * GY * ROWS
+    quarter = iota((GY * ROWS, CELLS), 1) >> 5
+    for pair in range(GX // 2):
+        for i in (2 * pair, 2 * pair + 1):
+            tile = slice(i // F * CELLS, i // F * CELLS + CELLS)
+            message = windows[0][:, tile]
+            for f in range(1, F):
+                message = jnp.where(quarter == (f + i) % F, windows[f][:, tile], message)
+            z_ref[pl.ds(i * GY * ROWS, GY * ROWS), :] = message
+            if i in LEFT:
+                z_ref[pl.ds(i * GY * ROWS + WQ, GY, stride=ROWS), :] = left[LEFT.index(i)]
+        z_ref[pl.ds(pair * size + ROWS - 1, 2 * GY, stride=ROWS), :] = slots[2 * GY * pair : 2 * GY * (pair + 1)]
+        copies.append(write(z_ref, out_ref, out_any, sems.at[pair], pl.ds(pair * size, size)))
     for copy in copies:
         copy.wait()
+
+
+def write(z_ref, out_ref, out_any, sem, at):
+    out_ref[at, :] = z_ref[at, :].astype(bf16)
+    copy = pltpu.make_async_copy(out_ref.at[at, :], out_any.at[at, :], sem)
+    copy.start()
+    return copy
 
 
 def hat(fine, anchor, coarse):
     centre = (fine.astype(f32) + 0.5) * (2.0 / 13.0) - 0.5 + anchor.astype(f32)
     return jnp.maximum(0.0, 1.0 - jnp.abs(centre - coarse.astype(f32)))
+
+
+FOLD = TX // (CELLS // (F * HALO))
 
 
 def strips_kernel(s_ref, low_ref, high_ref, top_ref, bottom_ref, wide_ref):
@@ -213,8 +218,16 @@
         high = jnp.where(field == f, pltpu.roll(s, CELLS - TY + HALO + HALO * f, 1), high)
         top_ref[f * HALO : (f + 1) * HALO, :] = pltpu.roll(s[:8], HALO, 1)[:HALO]
         bottom_ref[f * HALO : (f + 1) * HALO, :] = pltpu.roll(s[TX - 8 :], HALO, 1)[HALO:]
-    low_ref[...] = low
-    high_ref[...] = high
+    for strip, ref in ((low, low_ref), (high, high_ref)):
+        packed = strip[:FOLD]
+        for g in range(1, TX // FOLD):
+            packed = packed + pltpu.roll(strip[g * FOLD : (g + 1) * FOLD], g * F * HALO, 1)
+        ref[...] = packed
+
+
+def unfolded(packed):
+    n = F * HALO
+    return jnp.concatenate([packed] + [pltpu.roll(packed, CELLS - g * n, 1) for g in range(1, TX // FOLD)], axis=0)
 
 
 def widened(s, left, right, f):
@@ -225,9 +238,25 @@
     return jnp.where(lane < HALO, before, jnp.where(lane < TY + 2 * HALO, wide, 0.0))
 
 
-def tables_kernel(
-    holder_ref, corner_ref, owner_ref, wx_ref, wlast_ref, mask_ref, wy_ref, wyc_ref, send_ref, back_ref
+def corner_of(got_ref, step):
+    other, there = neighbour(step)
+    rows = got_ref[pl.ds(pl.multiple_of((other >> 2) * GROUP, 16), GROUP), :].astype(f32)
+    mine = jnp.where(there, (other & 3) * ROWS + ROWS - 1, -1)
+    row = jnp.sum(jnp.where(iota((GROUP, CELLS), 0) == mine, rows, 0.0), axis=0, keepdims=True)
+    row = jnp.broadcast_to(row, (8, CELLS))
+    return row + pltpu.roll(row, CELLS - CORNER, 1) + pltpu.roll(row, CELLS - 2 * CORNER, 1)
+
+
+def nest_kernel(
+    wait, holder_ref, corner_ref, owner_ref, got_ref, s_ref, left_ref, right_ref, before_ref, after_ref, skin_ref,
+    next_any, out_any, wx_ref, wide_ref, next_ref, out_ref, state_ref, force_ref, flux_ref, z_ref, sems,
 ):
+    wide_ref[...] = jnp.zeros_like(wide_ref)
+    flux_ref[...] = jnp.zeros_like(flux_ref)
+    corners = [corner_of(got_ref, step) for step in CORNERS]
+    group = pl.multiple_of((holder_ref[0] >> 2) * GROUP, 16)
+    got = got_ref[pl.ds(group, GROUP), :]
+    wait(1)
     ix, iy = lax.axis_index("gx"), lax.axis_index("gy")
     cx, cy = corner_ref[0], corner_ref[1]
     x0, y0 = ix * TX - HALO, iy * TY - HALO
@@ -236,64 +265,40 @@
     row = iota((ROWS_X, CELLS), 0)
     weight = hat(row + x0, cx, (lane & (WP - 1)) + px)
     for f in range(F):
-        wx_ref[f * ROWS_X : (f + 1) * ROWS_X, :] = jnp.where(lane >> 5 == f, weight, 0.0).astype(bf16)
-    wlast_ref[...] = relax_coef * hat(row + x0, cx, jnp.full_like(row, WP) + px).astype(bf16).astype(f32)
+        wx_ref[f * ROWS_X : (f + 1) * ROWS_X, :] = jnp.where(lane >> 5 == ((f + ix) & 3), weight, 0.0).astype(bf16)
+    weight_last = relax_coef / diffuse_coef * hat(row + x0, cx, jnp.full_like(row, WP) + px).astype(bf16).astype(f32)
     inside = (row + x0 >= 0) & (row + x0 < GX * TX) & (lane + y0 >= 0) & (lane + y0 < GY * TY)
-    mask_ref[...] = jnp.where(inside, 1.0, 0.0)
+    mask = jnp.where(inside, diffuse_coef, 0.0)
+    for now in range(2):
+        state_ref[:, now, :PAD, :] = jnp.zeros((F, PAD, CELLS), f32)
+        state_ref[:, now, PAD + ROWS_X :, :] = jnp.zeros((F, PAD, CELLS), f32)
     at = iota((CELLS, GROUP), 1) - (holder_ref[0] & 3) * ROWS
-    wy_ref[...] = jnp.where((at >= 0) & (at < WQ), hat(iota((CELLS, GROUP), 0) + y0, cy, at + qy), 0.0).astype(bf16)
+    weight_y = jnp.where((at >= 0) & (at < WQ), hat(iota((CELLS, GROUP), 0) + y0, cy, at + qy), 0.0).astype(bf16)
     lane = iota((CELLS, CELLS), 1)
-    wyc_ref[...] = hat(iota((CELLS, CELLS), 0) + y0, cy, qy + ((lane - qy) & (WP - 1))).astype(bf16)
+    weight_c = hat(iota((CELLS, CELLS), 0) + y0, cy, qy + ((lane - qy) & (WP - 1))).astype(bf16)
+    partial = dot(weight_y, got).astype(bf16)
+    last = jnp.sum(
+        jnp.where(iota((GROUP, CELLS), 0) == (holder_ref[0] & 3) * ROWS + WQ, got.astype(f32), 0.0), axis=0, keepdims=True
+    )
+    last = jnp.where(iota((8, CELLS), 1) >> 5 == iota((8, CELLS), 0), last, 0.0).astype(bf16)
+    partial_last = dot_nt(last, weight_c).astype(bf16).astype(f32)
+    force_ref[...] = dot_nt(wx_ref[...], partial)
+    wait(2)
     column = column_of(owner_ref[...])
     number, owner = by_thirds(column)
-    rank = rank_of(column, owner, number)
-    send_ref[...] = (iota((CAP * DEV, NB), 0) == rank * DEV + owner).astype(f32).astype(bf16)
-    back_ref[...] = (column_of(owner * CAP + rank) == iota((NB, CAP * DEV), 1)).astype(f32).astype(bf16)
-
-
-def corner_of(got_ref, step):
-    other, there = neighbour(step)
-    rows = got_ref[pl.ds(pl.multiple_of((other >> 2) * GROUP, 16), GROUP), :].astype(f32)
-    mine = jnp.where(there, (other & 3) * ROWS + ROWS - 1, -1)
-    row = jnp.sum(jnp.where(iota((GROUP, CELLS), 0) == mine, rows, 0.0), axis=0, keepdims=True)
-    row = jnp.broadcast_to(row, (8, CELLS))
-    return row + pltpu.roll(row, CELLS - CORNER, 1) + pltpu.roll(row, CELLS - 2 * CORNER, 1)
-
-
-def nest_kernel(
-    wait, holder_ref, got_ref, wx_ref, wlast_ref, mask_ref, wy_ref, wyc_ref, send_ref, s_ref, left_ref, right_ref,
-    before_ref, after_ref, skin_ref, next_any, out_any,
-    wide_ref, next_ref, out_ref, state_ref, force_ref, flux_ref, z_ref, sems,
-):
-    wide_ref[...] = jnp.zeros_like(wide_ref)
-    corners = [corner_of(got_ref, step) for step in CORNERS]
-    group = pl.multiple_of((holder_ref[0] >> 2) * GROUP, 16)
-    got = got_ref[pl.ds(group, GROUP), :]
-    wait(5)
-    partial = dot(wy_ref[...], got).astype(bf16)
-    last = jnp.sum(
-        jnp.where(iota((GROUP, CELLS), 0) == (holder_ref[0] & 3) * ROWS + WQ, got.astype(f32), 0.0), axis=0, keepdims=True
-    )
-    last = jnp.where(iota((8, CELLS), 1) >> 5 == iota((8, CELLS), 0), last, 0.0).astype(bf16)
-    wait(6)
-    partial_last = dot_nt(last, wyc_ref[...]).astype(bf16).astype(f32)
-    wait(2)
-    force_ref[...] = dot_nt(wx_ref[...], partial)
-    flux_ref[...] = jnp.zeros_like(flux_ref)
-    for k in (3, 4, 8):
-        wait(k)
-    mask = mask_ref[...]
-    left, right = left_ref[...], right_ref[...]
+    send = (iota((CAP * DEV, NB), 0) == rank_of(column, owner, number) * DEV + owner).astype(f32).astype(bf16)
+    wait(4)
+    left, right = unfolded(left_ref[...]), unfolded(right_ref[...])
     lane, sub = iota((8, CELLS), 1), iota((8, CELLS), 0)
     written = []
     for f in range(F):
-        force = relax_coef * force_ref[f * ROWS_X : (f + 1) * ROWS_X, :] + wlast_ref[...] * partial_last[f : f + 1, :]
-        wide_ref[:, :TY] = s_ref[f]
-        state_ref[:HALO, :] = before_ref[f * HALO : (f + 1) * HALO, :]
-        state_ref[HALO : HALO + TX, :] = widened(wide_ref[...], left, right, f)
-        state_ref[HALO + TX :, :] = after_ref[f * HALO : (f + 1) * HALO, :]
-        for side, base in ((-1, 0), (1, ROWS_X - 8)):
-            tile = state_ref[base : base + 8, :]
+        force = relax_coef / diffuse_coef * force_ref[f * ROWS_X : (f + 1) * ROWS_X, :] + weight_last * partial_last[f : f + 1, :]
+        wide_ref[f, :, :TY] = s_ref[f]
+        state_ref[f, 0, PAD : PAD + HALO, :] = before_ref[f * HALO : (f + 1) * HALO, :]
+        state_ref[f, 0, PAD + HALO : PAD + HALO + TX, :] = widened(wide_ref[f], left, right, f)
+        state_ref[f, 0, PAD + HALO + TX : PAD + ROWS_X, :] = after_ref[f * HALO : (f + 1) * HALO, :]
+        for side, base in ((-1, PAD), (1, PAD + ROWS_X - 8)):
+            tile = state_ref[f, 0, base : base + 8, :]
             for k, (dx, dy) in enumerate(CORNERS):
                 for r in range(EDGE if dx == side else 0):
                     row = HALO - EDGE + r if dx < 0 else 8 - HALO + r
@@ -301,47 +306,55 @@
                     at = FREE + (f * EDGE + r) * EDGE
                     moved = pltpu.roll(corners[k], (column - at) % CELLS, 1)
                     tile = jnp.where((sub == row) & (lane >= column) & (lane < column + EDGE), moved, tile)
-            state_ref[base : base + 8, :] = tile
-        s = state_ref[...]
-        for _ in range(STEPS):
-            beside = (
-                pltpu.roll(s, 1, 0) + pltpu.roll(s, ROWS_X - 1, 0) + pltpu.roll(s, 1, 1) + pltpu.roll(s, CELLS - 1, 1)
-            )
-            s = mask * ((1.0 - 4.0 * diffuse_coef - relax_coef) * s + diffuse_coef * beside + force)
-        state_ref[...] = pltpu.roll(s, CELLS - HALO, 1)
-        next_ref[f] = state_ref[HALO : HALO + TX, :TY]
-        written.append(pltpu.make_async_copy(next_ref.at[f], next_any.at[f], sems.at[f]))
-        written[f].start()
+            state_ref[f, 0, base : base + 8, :] = tile
+        s = state_ref[f, 0, PAD : PAD + ROWS_X, :]
+        for step in range(STEPS):
+            now = step % 2
+            beside = state_ref[f, now, PAD - 1 : PAD - 1 + ROWS_X, :] + state_ref[f, now, PAD + 1 : PAD + 1 + ROWS_X, :]
+            beside = beside + (pltpu.roll(s, 1, 1) + pltpu.roll(s, CELLS - 1, 1))
+            s = mask * ((1.0 - 4.0 * diffuse_coef - relax_coef) / diffuse_coef * s + beside + force)
+            state_ref[f, 1 - now, PAD : PAD + ROWS_X, :] = s if step < STEPS - 1 else pltpu.roll(s, CELLS - HALO, 1)
+        last_state = state_ref.at[f, STEPS % 2]
+        next_ref[f] = last_state[PAD + HALO : PAD + HALO + TX, :TY]
     u, v, ta, qa = next_ref[0], next_ref[1], next_ref[2], next_ref[3]
     half = drag_coefficient * jnp.sqrt(1.0 + u * u + v * v)
-    wait(13)
+    written.append(pltpu.make_async_copy(next_ref, next_any, sems.at[4]))
+    written[0].start()
+    wait(9)
     skin = skin_ref[...]
     flux = (half * (ta - skin), half * (qa - 0.5 * skin), half * u, half * v)
     rows = NB // CAP
     lane = iota((rows, CELLS), 1)
     blocks = []
     for f in range(F):
-        flux_ref[:, :TY] = flux[f]
-        m = [flux_ref[pl.ds(k, rows, stride=4), :] for k in range(4)]
+        flux_ref[f, :, :TY] = flux[f]
+        m = [flux_ref[f, pl.ds(k, rows, stride=4), :] for k in range(4)]
         r1, r2, r3 = pltpu.roll(m[1], 96, 1), pltpu.roll(m[2], 64, 1), pltpu.roll(m[3], 32, 1)
         blocks.append(
             jnp.concatenate(
                 [jnp.where(lane < 96, m[0], r1), jnp.where(lane < 64, r1, r2), jnp.where(lane < 32, r2, r3)], axis=0
             ).astype(bf16)
         )
-    wait(7)
-    sent = dot(send_ref[...], jnp.concatenate(blocks, axis=1))
-    for slot in range(CAP):
-        for f in range(F):
-            z_ref[pl.ds(slot * F + f, DEV, stride=CAP * F), :] = sent[
-                slot * DEV : (slot + 1) * DEV, f * CELLS : (f + 1) * CELLS
-            ]
+    sent = dot(send, jnp.concatenate(blocks, axis=1))
+    part = DEV // 4
+    for c in range(4):
+        for slot in range(CAP):
+            for f in range(F):
+                z_ref[pl.ds(c * part * CAP * F + slot * F + f, part, stride=CAP * F), :] = sent[
+                    slot * DEV + c * part : slot * DEV + (c + 1) * part, f * CELLS : (f + 1) * CELLS
+                ]
+        written.append(write(z_ref, out_ref, out_any, sems.at[c], pl.ds(c * part * CAP * F, part * CAP * F)))
     for copy in written:
         copy.wait()
-    write(z_ref, out_ref, out_any, sems, 4)
-
-
-def hot_kernel(got_ref, kept_ref, hot_ref, give_ref, inverse_ref, cover_ref, z_ref, slot_ref, row_ref):
+
+
+def hot_kernel(
+    got_ref, kept_ref, owner_ref, hot_ref, give_ref, inverse_ref, cover_ref, back_ref, z_ref, slot_ref, row_ref
+):
+    column = column_of(owner_ref[...])
+    number, owner = by_thirds(column)
+    source = column_of(owner * CAP + rank_of(column, owner, number))
+    back_ref[...] = (source == iota((NB, CAP * DEV), 1)).astype(f32).astype(bf16)
     slot_ref[...] = got_ref[...].astype(f32)
     slots = slot_ref[pl.ds(ROWS - 1, DEV, stride=ROWS), :].astype(i32)
     lane = iota((DEV, OCEAN * F), 1)
@@ -366,8 +379,13 @@
     out_ref[OCEAN * F :, :] = jnp.full((8, CELLS), scale_ref[0, 0], f32)
 
 
-def ocean_kernel(got_ref, hot_ref, inverse_ref, cover_ref, top_ref, give_ref, forcing_ref, out_ref):
-    forcing = dot(hot_ref[...], got_ref[...]) * inverse_ref[...] + cover_ref[...]
+def ocean_kernel(wait, got_ref, hot_ref, inverse_ref, cover_ref, top_ref, give_ref, forcing_ref, out_ref):
+    wait(1)
+    wait(0)
+    sums = dot(hot_ref[...], got_ref[...])
+    for k in (2, 3, 4, 5):
+        wait(k)
+    forcing = sums * inverse_ref[...] + cover_ref[...]
     forcing_ref[...] = forcing
     top = top_ref[: OCEAN * F, :] + top_ref[OCEAN * F : OCEAN * F + 1, :] * forcing
     back = dot(give_ref[...], jnp.concatenate(split3(top), axis=1))
@@ -491,29 +509,27 @@
     names, message, tile, strip = ((1, NB), i32), ((DEV * ROWS, CELLS), bf16), ((F, TX, TY), f32), ((TX, CELLS), f32)
     (windows,) = call(
         pack_kernel, "SHHHh", "h", (corner_offset, owner, place, coarse_lowest_values, fine_atmospheric_values), (message,),
-        (((F, 16, TY), f32), ((16, CELLS), f32), ((DEV * ROWS, CELLS), f32), message), 4,
+        (
+            ((F, 16, TY), f32), ((16, CELLS), f32), ((F, PROW, 2 * CELLS), bf16), ((DEV * ROWS, CELLS), f32),
+            message,
+        ), 4, True,
     )
     got = exchange(windows, (DEV, ROWS // 4, 4, CELLS))
     present, _ = lax.optimization_barrier((fine_atmospheric_values, windows))
-    ends = ((F * HALO, CELLS), f32)
-    low, high, top, bottom = call(strips_kernel, "H", "vvvv", (present,), (strip, strip, ends, ends), (strip,))
+    ends, fold = ((F * HALO, CELLS), f32), ((FOLD, CELLS), f32)
+    low, high, top, bottom = call(strips_kernel, "H", "vvvv", (present,), (fold, fold, ends, ends), (strip,))
     left, right = shift(high, "gy", 1), shift(low, "gy", -1)
     before, after = shift(bottom, "gx", 1), shift(top, "gx", -1)
-    holder, corner, _ = lax.optimization_barrier((holder_flat, corner_offset, windows))
+    holder, _ = lax.optimization_barrier((holder_flat, windows))
     holder = jnp.minimum(holder, DEV - 1)
-    wide = (ROWS_X, CELLS)
-    *weights, send, back = call(
-        tables_kernel, "sSH", "HHHHHHH", (holder, corner, owner),
+    sent, strips = ((DEV * CAP * F, CELLS), bf16), ((F, TX, CELLS), f32)
+    nest_next, flux = call(
+        nest_kernel, "sSHvHvvvvH", "hh",
+        (holder, corner_offset, owner, got, fine_atmospheric_values, left, right, before, after, fine_skin_heat), (tile, sent),
         (
-            ((F * ROWS_X, CELLS), bf16), (wide, f32), (wide, f32), ((CELLS, GROUP), bf16), ((CELLS, CELLS), bf16),
-            ((CAP * DEV, NB), bf16), ((NB, CAP * DEV), bf16),
-        ),
-    )
-    sent = ((DEV * CAP * F, CELLS), bf16)
-    nest_next, flux = call(
-        nest_kernel, "svHHHHHHHvvvvH", "hh",
-        (holder, got, *weights, send, fine_atmospheric_values, left, right, before, after, fine_skin_heat), (tile, sent),
-        (strip, tile, sent, (wide, f32), ((F * ROWS_X, CELLS), f32), strip, ((DEV * CAP * F, CELLS), f32)), F, True,
+            ((F * ROWS_X, CELLS), bf16), strips, tile, sent, ((F, 2, ROWS_X + 2 * PAD, CELLS), f32),
+            ((F * ROWS_X, CELLS), f32), strips, ((DEV * CAP * F, CELLS), f32),
+        ), 5, True,
     )
     got_flux = exchange(flux, (DEV, CAP, F, CELLS))
     layers = marine_stratum_values.shape[1]
@@ -521,14 +537,16 @@
     marine_late, got_late, flux = lax.optimization_barrier((marine, got, flux))
     block = ((OCEAN * F, CELLS), f32)
     hot, give = ((OCEAN * F, DEV * CAP * F), bf16), ((DEV * CAP, OCEAN * F), bf16)
-    hot, give, inverse, cover = call(
-        hot_kernel, "vH", "HHHH", (got_late, by_block(coarse_interface_exchange)), (hot, give, block, block),
+    hot, give, inverse, cover, back = call(
+        hot_kernel, "vHH", "HHHHv", (got_late, by_block(coarse_interface_exchange), owner),
+        (hot, give, block, block, ((NB, CAP * DEV), bf16)),
         (((DEV * CAP * F, OCEAN * F), f32), ((DEV * ROWS, CELLS), f32), ((DEV * CAP, OCEAN * F), f32)),
     )
     (layer0,) = call(top_kernel, "Sp", "H", (diffusion_solver_operator, marine_late), (((OCEAN * F + 8, CELLS), f32),))
     returned = ((DEV * CAP, CELLS), f32)
     forcing, skins = call(
-        ocean_kernel, "HHHHHH", "HH", (got_flux, hot, inverse, cover, layer0, give), (block, returned)
+        ocean_kernel, "HHHHHH", "HH", (got_flux, hot, inverse, cover, layer0, give), (block, returned),
+        lazy=True,
     )
     arrived = exchange(skins, (DEV, 1, CAP * CELLS))
     part = 32
@@ -546,7 +564,7 @@
         compiler_params=pltpu.CompilerParams(vmem_limit_bytes=40 << 20),
     )(diffusion_solver_operator, forcing, marine)
     refreshed = refreshed.reshape(layers, OCEAN, F, CELLS).transpose(2, 0, 1, 3).reshape(marine_stratum_values.shape)
-    (skin,) = call(skin_kernel, "vH", "p", (arrived, back), (((TX, TY), f32),), (((TX, CELLS), f32),))
+    (skin,) = call(skin_kernel, "vv", "p", (arrived, back), (((TX, TY), f32),), (((TX, CELLS), f32),))
     return (nest_next, refreshed, skin)
 
 

time: 79.1 us -> 77.7 us (0.982)
  Pallas kernels: 25.3 us -> 22.5 us
  waiting for transfers between devices: 15.2 us -> 16.9 us
    pallas_call x8 -> x7, Pallas kernels: 20.7 us -> 18 us  [call(): pl.pallas_call(body, out_shape=tuple((MEMORY[c](s, d) if c in MEMORY else...]
    ppermute x4, waiting for transfers between devices: 0.79 us -> 2.69 us  [shift(): lax.ppermute(value, axis, [(i, i + by) for i in range(n) if 0 <= i + by <...]
  transfers between devices with their start and end apart: 7 -> 7, of which waited for: 4 -> 4; matrix products, arithmetic and copies ran while one was open for 0% -> 0% of each run, Pallas kernels for 15% -> 13%
where the time goes in v5:
time: 77.7 us; the launch traced here: 77.1 us
  starting transfers between devices  35.4 us (46%)
  Pallas kernels  22.5 us (29%)
  waiting for transfers between devices  16.9 us (22%)
  between operations  1.43 us (2%)
  local copies, waits for them, and re-layouts  0.85 us (1%)
    all_to_all x3, starting transfers between devices, exchange(): lax.all_to_all(split, ('gx', 'gy'), split_axis=0, concat_axis=0, tiled=True)  25.3 us
    pallas_call x7, Pallas kernels, call(): pl.pallas_call(body, out_shape=tuple((MEMORY[c](s, d) if c in MEMORY else...  18 us
    all_to_all x3, waiting for transfers between devices, exchange(): lax.all_to_all(split, ('gx', 'gy'), split_axis=0, concat_axis=0, tiled=True)  14.2 us
    ppermute x4, starting transfers between devices, shift(): lax.ppermute(value, axis, [(i, i + by) for i in range(n) if 0 <= i + by <...  10.1 us
    pallas_call x1, Pallas kernels, on_device(): pl.pallas_call(mix_kernel, out_shape=jax.ShapeDtypeStruct((layers, OCEAN...  4.54 us
    ppermute x4, waiting for transfers between devices, shift(): lax.ppermute(value, axis, [(i, i + by) for i in range(n) if 0 <= i + by <...  2.69 us
  transfers between devices with their start and end apart: 7, of which 4 were waited for; matrix products, arithmetic and copies ran while one was open for 0% of the time, Pallas kernels for 13%

profile of v5, /device:TPU:1, one launch (start us, length us, event | category | flops | bytes accessed | tf_op | source)
XLA Modules:
  0.0 77.1 jit_solution(13825134855067465923)
XLA Ops:
  0.6 4.0 %shard_map.121 = bf16[2560,128]{1,0:T(8,128)(2,1)} custom-call(s32[2]{0:T(128)} %refs_1_.1, s32[1,144]{1,0:T(1,128)} %bitcast.33, s32[1,144]{1,0:T(1,128)} %bitcast.36, bf16[4,384,384]{2,1,0:T(8,128)(2,1)} %refs_3_.1, f32[4,192,96]{2,1,0:T(8,128)} %refs_4_.3), custom_call_target="tpu_custom_call" | custom-call | tf_op jit(solution)/shard_map/pallas_call | solution.py:468
  4.7 11.5 %all-to-all-start = ((bf16[128,5,4,128]{3,2,1,0:T(4,128)(2,1)}), bf16[128,5,4,128]{3,2,1,0:T(4,128)(2,1)S(1)}, u32[]{:S(2)}, u32[]{:S(2)}) async-start(bf16[128,5,4,128]{3,2,1,0:T(4,128)(2,1)} %bitcast.29), calls=%async_computation | async-start | bytes 1310720 | tf_op jit(solution)/shard_map/all_to_all | solution.py:488
  16.2 1.4 %shard_map.122 = (f32[24,128]{1,0:T(8,128)S(1)}, f32[24,128]{1,0:T(8,128)S(1)}, f32[16,128]{1,0:T(8,128)S(1)}, f32[16,128]{1,0:T(8,128)S(1)}) custom-call(f32[4,192,96]{2,1,0:T(8,128)} %refs_4_.3), custom_call_target="tpu_custom_call" | custom-call | tf_op jit(solution)/shard_map/pallas_call | solution.py:468
  17.6 3.3 %collective-permute-start = (f32[24,128]{1,0:T(8,128)S(1)}, f32[24,128]{1,0:T(8,128)S(1)}, u32[]{:S(2)}, u32[]{:S(2)}) collective-permute-start(f32[24,128]{1,0:T(8,128)S(1)} %get-tuple-element.22), channel_id=1, source_target_pairs={{0,1},{1,2},{2,3},{3,4},{4,5},{5,6},{6,7},{7,8},{8,9},{9,10},{10,1... | collective-permute-start | bytes 36872 | tf_op jit(solution)/shard_map/ppermute | solution.py:483
  20.9 1.3 %collective-permute-start.1 = (f32[24,128]{1,0:T(8,128)S(1)}, f32[24,128]{1,0:T(8,128)S(1)}, u32[]{:S(2)}, u32[]{:S(2)}) collective-permute-start(f32[24,128]{1,0:T(8,128)S(1)} %get-tuple-element.23), channel_id=1, source_target_pairs={{1,0},{2,1},{3,2},{4,3},{5,4},{6,5},{7,6},{8,7},{9,8},{10,9},{11,1... | collective-permute-start | bytes 36872 | tf_op jit(solution)/shard_map/ppermute | solution.py:483
  22.2 3.6 %collective-permute-start.2 = (f32[16,128]{1,0:T(8,128)S(1)}, f32[16,128]{1,0:T(8,128)S(1)}, u32[]{:S(2)}, u32[]{:S(2)}) collective-permute-start(f32[16,128]{1,0:T(8,128)S(1)} %get-tuple-element.24), channel_id=1, source_target_pairs={{0,16},{16,32},{32,48},{48,64},{64,80},{80,96},{96,112},{1,17},{17... | collective-permute-start | bytes 24584 | tf_op jit(solution)/shard_map/ppermute | solution.py:483
  25.8 1.9 %collective-permute-start.3 = (f32[16,128]{1,0:T(8,128)S(1)}, f32[16,128]{1,0:T(8,128)S(1)}, u32[]{:S(2)}, u32[]{:S(2)}) collective-permute-start(f32[16,128]{1,0:T(8,128)S(1)} %get-tuple-element.25), channel_id=1, source_target_pairs={{16,0},{32,16},{48,32},{64,48},{80,64},{96,80},{112,96},{17,1},{33... | collective-permute-start | bytes 24584 | tf_op jit(solution)/shard_map/ppermute | solution.py:483
  28.4 0.0 collective-permute-done.2.refs_7_
  28.4 2.7 %collective-permute-done.3.refs_8_ = f32[16,128]{1,0:T(8,128)S(1)} collective-permute-done((f32[16,128]{1,0:T(8,128)S(1)}, f32[16,128]{1,0:T(8,128)S(1)}, u32[]{:S(2)}, u32[]{:S(2)}) %collective-permute-start.3) | collective-permute-done | bytes 8224 | tf_op jit(solution)/shard_map/ppermute | solution.py:483
  31.1 0.0 collective-permute-done.refs_5_
  31.1 0.5 all-to-all-done
  31.6 4.9 %shard_map.123 = (f32[4,192,96]{2,1,0:T(8,128)}, bf16[1536,128]{1,0:T(8,128)(2,1)}) custom-call(s32[1]{0:T(128)S(6)} %min.3.refs_0_, s32[2]{0:T(128)} %refs_1_.1, s32[1,144]{1,0:T(1,128)} %bitcast.34, bf16[2560,128]{1,0:T(8,128)(2,1)S(1)} %bitcast.25, f32[4,192,96]{2,1,0:T(8,128)} %refs_4_.3, f32[24,128]{1,0:T(8,128)S(1)} %collective-permute-done.refs_5_, ...), custom_call_target="tpu_custom_call" | custom-call | tf_op jit(solution)/shard_map/pallas_call | solution.py:468
  36.5 9.8 %all-to-all-start.1 = ((bf16[128,3,4,128]{3,2,1,0:T(4,128)(2,1)}), bf16[128,3,4,128]{3,2,1,0:T(4,128)(2,1)}, u32[]{:S(2)}, u32[]{:S(2)}) async-start(bf16[128,3,4,128]{3,2,1,0:T(4,128)(2,1)} %bitcast.30), calls=%async_computation.1 | async-start | bytes 786432 | tf_op jit(solution)/shard_map/all_to_all | solution.py:488
  46.4 0.0 copy-start.1
  46.4 1.9 %shard_map.125.refs_4_ = f32[136,128]{1,0:T(8,128)} custom-call(f32[41,41]{1,0:T(8,128)} %scale_ref.1, f32[41,128,128]{2,1,0:T(8,128)S(1)} %bitcast.23), custom_call_target="tpu_custom_call" | custom-call | tf_op jit(solution)/shard_map/pallas_call | solution.py:468
  48.2 2.5 %shard_map.124 = (bf16[128,1536]{1,0:T(8,128)(2,1)}, bf16[384,128]{1,0:T(8,128)(2,1)}, f32[128,128]{1,0:T(8,128)}, f32[128,128]{1,0:T(8,128)}, bf16[144,384]{1,0:T(8,128)(2,1)S(1)}) custom-call(bf16[2560,128]{1,0:T(8,128)(2,1)S(1)} %bitcast.26, f32[128,128]{1,0:T(8,128)} %bitcast.32, s32[1,144]{1,0:T(1,128)} %bitcast.35), custom_call_target="tpu_custom_call" | custom-call | tf_op jit(solution)/shard_map/pallas_call | solution.py:468
  50.7 8.1 %all-to-all-done.1 = bf16[128,3,4,128]{3,2,1,0:T(4,128)(2,1)} async-done(((bf16[128,3,4,128]{3,2,1,0:T(4,128)(2,1)}), bf16[128,3,4,128]{3,2,1,0:T(4,128)(2,1)}, u32[]{:S(2)}, u32[]{:S(2)}) %all-to-all-start.1) | async-done | bytes 393248 | tf_op jit(solution)/shard_map/all_to_all | solution.py:488
  58.8 2.4 %shard_map.126 = (f32[128,128]{1,0:T(8,128)}, f32[384,128]{1,0:T(8,128)}) custom-call(bf16[1536,128]{1,0:T(8,128)(2,1)} %bitcast.5.refs_0_, bf16[128,1536]{1,0:T(8,128)(2,1)} %get-tuple-element.29.refs_1_, f32[128,128]{1,0:T(8,128)} %get-tuple-element.30.refs_2_, f32[128,128]{1,0:T(8,128)} %get-tuple-element.31.refs_3_, f32[136,128]{1,0:T(8,128)} %shard_map.125.refs_4_, ...), custom_call_target="tpu_custom_call" | custom-call | tf_op jit(solution)/shard_map/pallas_call | solution.py:468
  61.2 4.0 %all-to-all-start.2 = ((f32[128,1,384]{2,1,0:T(1,128)}), f32[128,1,384]{2,1,0:T(1,128)S(1)}, u32[]{:S(2)}, u32[]{:S(2)}) async-start(f32[128,1,384]{2,1,0:T(1,128)} %bitcast.31), calls=%async_computation.2 | async-start | bytes 393216 | tf_op jit(solution)/shard_map/all_to_all | solution.py:488
  65.2 0.0 copy-start.2
  65.2 0.8 %copy-done.2 = f32[128,128]{1,0:T(8,128)S(1)} copy-done((f32[128,128]{1,0:T(8,128)S(1)}, f32[128,128]{1,0:T(8,128)}, u32[]{:S(2)}) %copy-start.2) | copy-done | bytes 65560
  66.0 4.5 %shard_map.127 = f32[41,128,128]{2,1,0:T(8,128)} custom-call(f32[41,41]{1,0:T(8,128)S(1)} %copy-done.1, f32[128,128]{1,0:T(8,128)S(1)} %copy-done.2, f32[41,128,128]{2,1,0:T(8,128)S(1)} %bitcast.24), custom_call_target="tpu_custom_call" | custom-call | tf_op jit(solution)/shard_map/pallas_call | solution.py:553
  70.6 5.5 %all-to-all-done.2 = f32[128,1,384]{2,1,0:T(1,128)S(1)} async-done(((f32[128,1,384]{2,1,0:T(1,128)}), f32[128,1,384]{2,1,0:T(1,128)S(1)}, u32[]{:S(2)}, u32[]{:S(2)}) %all-to-all-start.2) | async-done | bytes 196640 | tf_op jit(solution)/shard_map/all_to_all | solution.py:488
  76.1 1.0 %shard_map.128 = f32[192,96]{1,0:T(8,128)} custom-call(f32[384,128]{1,0:T(8,128)S(1)} %bitcast.27, bf16[144,384]{1,0:T(8,128)(2,1)S(1)} %get-tuple-element.36.refs_1_), custom_call_target="tpu_custom_call" | custom-call | tf_op jit(solution)/shard_map/pallas_call | solution.py:468
  (4 shorter events, 0.0 us)
Async XLA Ops:
  0.6 45.7 %copy-start = (f32[4,41,4096]{2,0,1:T(4,128)S(1)}, f32[4,41,4096]{2,0,1:T(4,128)}, u32[]{:S(2)}) copy-start(f32[4,41,4096]{2,0,1:T(4,128)} %param.18) | copy-start | bytes 8060932
  4.7 26.9 %all-to-all-start = ((bf16[128,5,4,128]{3,2,1,0:T(4,128)(2,1)}), bf16[128,5,4,128]{3,2,1,0:T(4,128)(2,1)S(1)}, u32[]{:S(2)}, u32[]{:S(2)}) async-start(bf16[128,5,4,128]{3,2,1,0:T(4,128)(2,1)} %bitcast.29), calls=%async_computation | async-start | bytes 1310720 | tf_op jit(solution)/shard_map/all_to_all | solution.py:488
  17.6 13.5 %collective-permute-start = (f32[24,128]{1,0:T(8,128)S(1)}, f32[24,128]{1,0:T(8,128)S(1)}, u32[]{:S(2)}, u32[]{:S(2)}) collective-permute-start(f32[24,128]{1,0:T(8,128)S(1)} %get-tuple-element.22), channel_id=1, source_target_pairs={{0,1},{1,2},{2,3},{3,4},{4,5},{5,6},{6,7},{7,8},{8,9},{9,10},{10,1... | collective-permute-start | bytes 36872 | tf_op jit(solution)/shard_map/ppermute | solution.py:483
  20.9 10.2 %collective-permute-start.1 = (f32[24,128]{1,0:T(8,128)S(1)}, f32[24,128]{1,0:T(8,128)S(1)}, u32[]{:S(2)}, u32[]{:S(2)}) collective-permute-start(f32[24,128]{1,0:T(8,128)S(1)} %get-tuple-element.23), channel_id=1, source_target_pairs={{1,0},{2,1},{3,2},{4,3},{5,4},{6,5},{7,6},{8,7},{9,8},{10,9},{11,1... | collective-permute-start | bytes 36872 | tf_op jit(solution)/shard_map/ppermute | solution.py:483
  22.2 6.2 %collective-permute-start.2 = (f32[16,128]{1,0:T(8,128)S(1)}, f32[16,128]{1,0:T(8,128)S(1)}, u32[]{:S(2)}, u32[]{:S(2)}) collective-permute-start(f32[16,128]{1,0:T(8,128)S(1)} %get-tuple-element.24), channel_id=1, source_target_pairs={{0,16},{16,32},{32,48},{48,64},{64,80},{80,96},{96,112},{1,17},{17... | collective-permute-start | bytes 24584 | tf_op jit(solution)/shard_map/ppermute | solution.py:483
  25.8 5.3 %collective-permute-start.3 = (f32[16,128]{1,0:T(8,128)S(1)}, f32[16,128]{1,0:T(8,128)S(1)}, u32[]{:S(2)}, u32[]{:S(2)}) collective-permute-start(f32[16,128]{1,0:T(8,128)S(1)} %get-tuple-element.25), channel_id=1, source_target_pairs={{16,0},{32,16},{48,32},{64,48},{80,64},{96,80},{112,96},{17,1},{33... | collective-permute-start | bytes 24584 | tf_op jit(solution)/shard_map/ppermute | solution.py:483
  36.5 22.3 %all-to-all-start.1 = ((bf16[128,3,4,128]{3,2,1,0:T(4,128)(2,1)}), bf16[128,3,4,128]{3,2,1,0:T(4,128)(2,1)}, u32[]{:S(2)}, u32[]{:S(2)}) async-start(bf16[128,3,4,128]{3,2,1,0:T(4,128)(2,1)} %bitcast.30), calls=%async_computation.1 | async-start | bytes 786432 | tf_op jit(solution)/shard_map/all_to_all | solution.py:488
  46.4 18.8 %copy-start.1 = (f32[41,41]{1,0:T(8,128)S(1)}, f32[41,41]{1,0:T(8,128)}, u32[]{:S(2)}) copy-start(f32[41,41]{1,0:T(8,128)} %scale_ref.1) | copy-start | bytes 20176
  61.2 14.9 %all-to-all-start.2 = ((f32[128,1,384]{2,1,0:T(1,128)}), f32[128,1,384]{2,1,0:T(1,128)S(1)}, u32[]{:S(2)}, u32[]{:S(2)}) async-start(f32[128,1,384]{2,1,0:T(1,128)} %bitcast.31), calls=%async_computation.2 | async-start | bytes 393216 | tf_op jit(solution)/shard_map/all_to_all | solution.py:488
  65.2 0.8 %copy-start.2 = (f32[128,128]{1,0:T(8,128)S(1)}, f32[128,128]{1,0:T(8,128)}, u32[]{:S(2)}) copy-start(f32[128,128]{1,0:T(8,128)} %get-tuple-element.34.forcing_ref) | copy-start | bytes 196612

commit v6 on v5

--- a/solution.py
+++ b/solution.py
@@ -104,27 +104,25 @@
     return jnp.where(there, x * GY + y, 0), there
 
 
-def corner_rows(s_ref, wide_ref):
+def corner_rows(wide_ref):
     lane, sub = iota((8, CELLS), 1), iota((8, CELLS), 0)
-    wide_ref[...] = jnp.zeros_like(wide_ref)
     out = jnp.zeros((8, CELLS), f32)
     for f in range(F):
-        wide_ref[:, :TY] = s_ref[f]
         for k, (dx, dy) in enumerate(CORNERS):
             for r in range(EDGE):
-                row = r if dx < 0 else 16 - EDGE + r
+                row = r if dx < 0 else TX - EDGE + r
                 column = 0 if dy < 0 else TY - EDGE
                 at = FREE + (f * EDGE + r) * EDGE
-                moved = pltpu.roll(jnp.broadcast_to(wide_ref[row : row + 1, :], (8, CELLS)), (at - column) % CELLS, 1)
+                moved = pltpu.roll(jnp.broadcast_to(wide_ref[f, row : row + 1, :], (8, CELLS)), (at - column) % CELLS, 1)
                 out = jnp.where((sub == k) & (lane >= at) & (lane < at + EDGE), moved, out)
     high, mid, low = (x.astype(f32) for x in split3(out))
     return high + pltpu.roll(mid, CORNER, 1) + pltpu.roll(low, 2 * CORNER, 1)
 
 
 def pack_kernel(
-    wait, corner_ref, owner_ref, place_ref, parent_ref, s_any, out_any, s_ref, wide_ref, pick_ref, z_ref, out_ref, sems,
+    wait, corner_ref, owner_ref, place_ref, parent_ref, s_ref, out_any, low_ref, high_ref, top_ref, bottom_ref,
+    wide_ref, pick_ref, z_ref, out_ref, sems,
 ):
-    ends = fetch([(s_any.at[:, pl.ds(src, 8), :], s_ref.at[:, pl.ds(dst, 8), :]) for dst, src in ((0, 0), (8, TX - 8))], sems)
     wait(0)
     cx, cy = corner_ref[0], corner_ref[1]
     base = pl.multiple_of(jnp.minimum(jnp.maximum(cx - 1, 0) // 16 * 16, PC - PROW), 16)
@@ -147,9 +145,12 @@
     for s in range(CAP):
         value = jnp.sum(jnp.where(named & (rank == s), place_ref[...] + 1, 0).astype(f32), axis=1, keepdims=True) - 1.0
         slots = jnp.where(iota((DEV, CELLS), 1) == s, value, slots)
-    for copy in ends:
-        copy.wait()
-    corners = corner_rows(s_ref, wide_ref)
+    wait(4)
+    wide_ref[...] = jnp.zeros_like(wide_ref)
+    for f in range(F):
+        wide_ref[f, :, :TY] = s_ref[f]
+    strips(wide_ref, low_ref, high_ref, top_ref, bottom_ref)
+    corners = corner_rows(wide_ref)
     for k, step in enumerate(CORNERS):
         other, there = neighbour(step)
         slots = slots + jnp.where(iota((DEV, CELLS), 0) == jnp.where(there, other, -1), corners[k : k + 1, :], 0.0)
@@ -207,13 +208,11 @@
 FOLD = TX // (CELLS // (F * HALO))
 
 
-def strips_kernel(s_ref, low_ref, high_ref, top_ref, bottom_ref, wide_ref):
+def strips(wide_ref, low_ref, high_ref, top_ref, bottom_ref):
     field = iota((TX, CELLS), 1) >> 2
-    wide_ref[...] = jnp.zeros_like(wide_ref)
     low, high = jnp.zeros((TX, CELLS), f32), jnp.zeros((TX, CELLS), f32)
     for f in range(F):
-        wide_ref[:, :TY] = s_ref[f]
-        s = wide_ref[...]
+        s = wide_ref[f]
         low = jnp.where(field == f, s if f == 0 else pltpu.roll(s, HALO * f, 1), low)
         high = jnp.where(field == f, pltpu.roll(s, CELLS - TY + HALO + HALO * f, 1), high)
         top_ref[f * HALO : (f + 1) * HALO, :] = pltpu.roll(s[:8], HALO, 1)[:HALO]
@@ -507,17 +506,13 @@
     owner = exchange_patch_holder.reshape(1, NB)
     place = holder_patch_position.reshape(1, NB)
     names, message, tile, strip = ((1, NB), i32), ((DEV * ROWS, CELLS), bf16), ((F, TX, TY), f32), ((TX, CELLS), f32)
-    (windows,) = call(
-        pack_kernel, "SHHHh", "h", (corner_offset, owner, place, coarse_lowest_values, fine_atmospheric_values), (message,),
-        (
-            ((F, 16, TY), f32), ((16, CELLS), f32), ((F, PROW, 2 * CELLS), bf16), ((DEV * ROWS, CELLS), f32),
-            message,
-        ), 4, True,
+    ends, fold, whole = ((F * HALO, CELLS), f32), ((FOLD, CELLS), f32), ((F, TX, CELLS), f32)
+    windows, low, high, top, bottom = call(
+        pack_kernel, "SHHHH", "hvvvv", (corner_offset, owner, place, coarse_lowest_values, fine_atmospheric_values),
+        (message, fold, fold, ends, ends),
+        (whole, ((F, PROW, 2 * CELLS), bf16), ((DEV * ROWS, CELLS), f32), message), 4, True,
     )
     got = exchange(windows, (DEV, ROWS // 4, 4, CELLS))
-    present, _ = lax.optimization_barrier((fine_atmospheric_values, windows))
-    ends, fold = ((F * HALO, CELLS), f32), ((FOLD, CELLS), f32)
-    low, high, top, bottom = call(strips_kernel, "H", "vvvv", (present,), (fold, fold, ends, ends), (strip,))
     left, right = shift(high, "gy", 1), shift(low, "gy", -1)
     before, after = shift(bottom, "gx", 1), shift(top, "gx", -1)
     holder, _ = lax.optimization_barrier((holder_flat, windows))

time: 77.7 us -> 76.6 us (0.986)
  waiting for transfers between devices: 16.9 us -> 18.2 us
  starting transfers between devices: 35.4 us -> 34.1 us
  Pallas kernels: 22.5 us -> 21.5 us
    all_to_all x3, waiting for transfers between devices: 14.2 us -> 15.5 us  [exchange(): lax.all_to_all(split, ('gx', 'gy'), split_axis=0, concat_axis=0, tiled=True)]
    all_to_all x3, starting transfers between devices: 25.3 us -> 23.9 us  [exchange(): lax.all_to_all(split, ('gx', 'gy'), split_axis=0, concat_axis=0, tiled=True)]
    pallas_call x7 -> x6, Pallas kernels: 18 us -> 17 us  [call(): pl.pallas_call(body, out_shape=tuple((MEMORY[c](s, d) if c in MEMORY else...]
  transfers between devices with their start and end apart: 7 -> 7, of which waited for: 4 -> 4; matrix products, arithmetic and copies ran while one was open for 0% -> 0% of each run, Pallas kernels for 13% -> 12%
where the time goes in v6:
time: 76.6 us; the launch traced here: 76.1 us
  starting transfers between devices  34.1 us (45%)
  Pallas kernels  21.5 us (28%)
  waiting for transfers between devices  18.2 us (24%)
  between operations  1.43 us (2%)
  local copies, waits for them, and re-layouts  0.85 us (1%)
    all_to_all x3, starting transfers between devices, exchange(): lax.all_to_all(split, ('gx', 'gy'), split_axis=0, concat_axis=0, tiled=True)  23.9 us
    pallas_call x6, Pallas kernels, call(): pl.pallas_call(body, out_shape=tuple((MEMORY[c](s, d) if c in MEMORY else...  17 us
    all_to_all x3, waiting for transfers between devices, exchange(): lax.all_to_all(split, ('gx', 'gy'), split_axis=0, concat_axis=0, tiled=True)  15.5 us
    ppermute x4, starting transfers between devices, shift(): lax.ppermute(value, axis, [(i, i + by) for i in range(n) if 0 <= i + by <...  10.1 us
    pallas_call x1, Pallas kernels, on_device(): pl.pallas_call(mix_kernel, out_shape=jax.ShapeDtypeStruct((layers, OCEAN...  4.54 us
    ppermute x4, waiting for transfers between devices, shift(): lax.ppermute(value, axis, [(i, i + by) for i in range(n) if 0 <= i + by <...  2.69 us
  transfers between devices with their start and end apart: 7, of which 4 were waited for; matrix products, arithmetic and copies ran while one was open for 0% of the time, Pallas kernels for 12%

profile of v6, /device:TPU:1, one launch (start us, length us, event | category | flops | bytes accessed | tf_op | source)
XLA Modules:
  0.0 76.1 jit_solution(2726071520460955937)
XLA Ops:
  0.6 4.4 %shard_map.121 = (bf16[2560,128]{1,0:T(8,128)(2,1)}, f32[24,128]{1,0:T(8,128)S(1)}, f32[24,128]{1,0:T(8,128)S(1)}, f32[16,128]{1,0:T(8,128)S(1)}, f32[16,128]{1,0:T(8,128)S(1)}) custom-call(s32[2]{0:T(128)} %refs_1_.1, s32[1,144]{1,0:T(1,128)} %bitcast.33, s32[1,144]{1,0:T(1,128)} %bitcast.36, bf16[4,384,384]{2,1,0:T(8,128)(2,1)} %refs_3_.1, ...), custom_call_target="tpu_custom_call" | custom-call | tf_op jit(solution)/shard_map/pallas_call | solution.py:467
  5.1 11.5 %all-to-all-start = ((bf16[128,5,4,128]{3,2,1,0:T(4,128)(2,1)}), bf16[128,5,4,128]{3,2,1,0:T(4,128)(2,1)S(1)}, u32[]{:S(2)}, u32[]{:S(2)}) async-start(bf16[128,5,4,128]{3,2,1,0:T(4,128)(2,1)} %bitcast.29), calls=%async_computation | async-start | bytes 1310720 | tf_op jit(solution)/shard_map/all_to_all | solution.py:487
  16.6 3.3 %collective-permute-start = (f32[24,128]{1,0:T(8,128)S(1)}, f32[24,128]{1,0:T(8,128)S(1)}, u32[]{:S(2)}, u32[]{:S(2)}) collective-permute-start(f32[24,128]{1,0:T(8,128)S(1)} %get-tuple-element.22), channel_id=1, source_target_pairs={{0,1},{1,2},{2,3},{3,4},{4,5},{5,6},{6,7},{7,8},{8,9},{9,10},{10,1... | collective-permute-start | bytes 36872 | tf_op jit(solution)/shard_map/ppermute | solution.py:482
  19.9 1.3 %collective-permute-start.1 = (f32[24,128]{1,0:T(8,128)S(1)}, f32[24,128]{1,0:T(8,128)S(1)}, u32[]{:S(2)}, u32[]{:S(2)}) collective-permute-start(f32[24,128]{1,0:T(8,128)S(1)} %get-tuple-element.23), channel_id=1, source_target_pairs={{1,0},{2,1},{3,2},{4,3},{5,4},{6,5},{7,6},{8,7},{9,8},{10,9},{11,1... | collective-permute-start | bytes 36872 | tf_op jit(solution)/shard_map/ppermute | solution.py:482
  21.2 3.6 %collective-permute-start.2 = (f32[16,128]{1,0:T(8,128)S(1)}, f32[16,128]{1,0:T(8,128)S(1)}, u32[]{:S(2)}, u32[]{:S(2)}) collective-permute-start(f32[16,128]{1,0:T(8,128)S(1)} %get-tuple-element.24), channel_id=1, source_target_pairs={{0,16},{16,32},{32,48},{48,64},{64,80},{80,96},{96,112},{1,17},{17... | collective-permute-start | bytes 24584 | tf_op jit(solution)/shard_map/ppermute | solution.py:482
  24.8 1.9 %collective-permute-start.3 = (f32[16,128]{1,0:T(8,128)S(1)}, f32[16,128]{1,0:T(8,128)S(1)}, u32[]{:S(2)}, u32[]{:S(2)}) collective-permute-start(f32[16,128]{1,0:T(8,128)S(1)} %get-tuple-element.25), channel_id=1, source_target_pairs={{16,0},{32,16},{48,32},{64,48},{80,64},{96,80},{112,96},{17,1},{33... | collective-permute-start | bytes 24584 | tf_op jit(solution)/shard_map/ppermute | solution.py:482
  27.4 0.0 collective-permute-done.2.refs_7_
  27.4 2.7 %collective-permute-done.3.refs_8_ = f32[16,128]{1,0:T(8,128)S(1)} collective-permute-done((f32[16,128]{1,0:T(8,128)S(1)}, f32[16,128]{1,0:T(8,128)S(1)}, u32[]{:S(2)}, u32[]{:S(2)}) %collective-permute-start.3) | collective-permute-done | bytes 8224 | tf_op jit(solution)/shard_map/ppermute | solution.py:482
  30.1 0.0 collective-permute-done.refs_5_
  30.1 0.0 collective-permute-done.1.refs_6_
  30.1 1.9 %all-to-all-done = bf16[128,5,4,128]{3,2,1,0:T(4,128)(2,1)S(1)} async-done(((bf16[128,5,4,128]{3,2,1,0:T(4,128)(2,1)}), bf16[128,5,4,128]{3,2,1,0:T(4,128)(2,1)S(1)}, u32[]{:S(2)}, u32[]{:S(2)}) %all-to-all-start) | async-done | bytes 655392 | tf_op jit(solution)/shard_map/all_to_all | solution.py:487
  32.0 4.9 %shard_map.122 = (f32[4,192,96]{2,1,0:T(8,128)}, bf16[1536,128]{1,0:T(8,128)(2,1)}) custom-call(s32[1]{0:T(128)S(6)} %min.3.refs_0_, s32[2]{0:T(128)} %refs_1_.1, s32[1,144]{1,0:T(1,128)} %bitcast.34, bf16[2560,128]{1,0:T(8,128)(2,1)S(1)} %bitcast.25, f32[4,192,96]{2,1,0:T(8,128)} %refs_4_.3, f32[24,128]{1,0:T(8,128)S(1)} %collective-permute-done.refs_5_, ...), custom_call_target="tpu_custom_call" | custom-call | tf_op jit(solution)/shard_map/pallas_call | solution.py:467
  36.9 8.5 %all-to-all-start.1 = ((bf16[128,3,4,128]{3,2,1,0:T(4,128)(2,1)}), bf16[128,3,4,128]{3,2,1,0:T(4,128)(2,1)}, u32[]{:S(2)}, u32[]{:S(2)}) async-start(bf16[128,3,4,128]{3,2,1,0:T(4,128)(2,1)} %bitcast.30), calls=%async_computation.1 | async-start | bytes 786432 | tf_op jit(solution)/shard_map/all_to_all | solution.py:487
  45.4 0.0 copy-start.1
  45.4 1.9 %shard_map.124.refs_4_ = f32[136,128]{1,0:T(8,128)} custom-call(f32[41,41]{1,0:T(8,128)} %scale_ref.1, f32[41,128,128]{2,1,0:T(8,128)S(1)} %bitcast.23), custom_call_target="tpu_custom_call" | custom-call | tf_op jit(solution)/shard_map/pallas_call | solution.py:467
  47.2 2.5 %shard_map.123 = (bf16[128,1536]{1,0:T(8,128)(2,1)}, bf16[384,128]{1,0:T(8,128)(2,1)}, f32[128,128]{1,0:T(8,128)}, f32[128,128]{1,0:T(8,128)}, bf16[144,384]{1,0:T(8,128)(2,1)S(1)}) custom-call(bf16[2560,128]{1,0:T(8,128)(2,1)S(1)} %bitcast.26, f32[128,128]{1,0:T(8,128)} %bitcast.32, s32[1,144]{1,0:T(1,128)} %bitcast.35), custom_call_target="tpu_custom_call" | custom-call | tf_op jit(solution)/shard_map/pallas_call | solution.py:467
  49.7 8.1 %all-to-all-done.1 = bf16[128,3,4,128]{3,2,1,0:T(4,128)(2,1)} async-done(((bf16[128,3,4,128]{3,2,1,0:T(4,128)(2,1)}), bf16[128,3,4,128]{3,2,1,0:T(4,128)(2,1)}, u32[]{:S(2)}, u32[]{:S(2)}) %all-to-all-start.1) | async-done | bytes 393248 | tf_op jit(solution)/shard_map/all_to_all | solution.py:487
  57.8 2.4 %shard_map.125 = (f32[128,128]{1,0:T(8,128)}, f32[384,128]{1,0:T(8,128)}) custom-call(bf16[1536,128]{1,0:T(8,128)(2,1)} %bitcast.5.refs_0_, bf16[128,1536]{1,0:T(8,128)(2,1)} %get-tuple-element.29.refs_1_, f32[128,128]{1,0:T(8,128)} %get-tuple-element.30.refs_2_, f32[128,128]{1,0:T(8,128)} %get-tuple-element.31.refs_3_, f32[136,128]{1,0:T(8,128)} %shard_map.124.refs_4_, ...), custom_call_target="tpu_custom_call" | custom-call | tf_op jit(solution)/shard_map/pallas_call | solution.py:467
  60.2 4.0 %all-to-all-start.2 = ((f32[128,1,384]{2,1,0:T(1,128)}), f32[128,1,384]{2,1,0:T(1,128)S(1)}, u32[]{:S(2)}, u32[]{:S(2)}) async-start(f32[128,1,384]{2,1,0:T(1,128)} %bitcast.31), calls=%async_computation.2 | async-start | bytes 393216 | tf_op jit(solution)/shard_map/all_to_all | solution.py:487
  64.2 0.0 copy-start.2
  64.2 0.8 %copy-done.2 = f32[128,128]{1,0:T(8,128)S(1)} copy-done((f32[128,128]{1,0:T(8,128)S(1)}, f32[128,128]{1,0:T(8,128)}, u32[]{:S(2)}) %copy-start.2) | copy-done | bytes 65560
  65.1 4.5 %shard_map.126 = f32[41,128,128]{2,1,0:T(8,128)} custom-call(f32[41,41]{1,0:T(8,128)S(1)} %copy-done.1, f32[128,128]{1,0:T(8,128)S(1)} %copy-done.2, f32[41,128,128]{2,1,0:T(8,128)S(1)} %bitcast.24), custom_call_target="tpu_custom_call" | custom-call | tf_op jit(solution)/shard_map/pallas_call | solution.py:548
  69.6 5.5 %all-to-all-done.2 = f32[128,1,384]{2,1,0:T(1,128)S(1)} async-done(((f32[128,1,384]{2,1,0:T(1,128)}), f32[128,1,384]{2,1,0:T(1,128)S(1)}, u32[]{:S(2)}, u32[]{:S(2)}) %all-to-all-start.2) | async-done | bytes 196640 | tf_op jit(solution)/shard_map/all_to_all | solution.py:487
  75.1 1.0 %shard_map.127 = f32[192,96]{1,0:T(8,128)} custom-call(f32[384,128]{1,0:T(8,128)S(1)} %bitcast.27, bf16[144,384]{1,0:T(8,128)(2,1)S(1)} %get-tuple-element.36.refs_1_), custom_call_target="tpu_custom_call" | custom-call | tf_op jit(solution)/shard_map/pallas_call | solution.py:467
  (3 shorter events, 0.0 us)
Async XLA Ops:
  0.6 44.7 %copy-start = (f32[4,41,4096]{2,0,1:T(4,128)S(1)}, f32[4,41,4096]{2,0,1:T(4,128)}, u32[]{:S(2)}) copy-start(f32[4,41,4096]{2,0,1:T(4,128)} %param.18) | copy-start | bytes 8060932
  5.1 26.9 %all-to-all-start = ((bf16[128,5,4,128]{3,2,1,0:T(4,128)(2,1)}), bf16[128,5,4,128]{3,2,1,0:T(4,128)(2,1)S(1)}, u32[]{:S(2)}, u32[]{:S(2)}) async-start(bf16[128,5,4,128]{3,2,1,0:T(4,128)(2,1)} %bitcast.29), calls=%async_computation | async-start | bytes 1310720 | tf_op jit(solution)/shard_map/all_to_all | solution.py:487
  16.6 13.5 %collective-permute-start = (f32[24,128]{1,0:T(8,128)S(1)}, f32[24,128]{1,0:T(8,128)S(1)}, u32[]{:S(2)}, u32[]{:S(2)}) collective-permute-start(f32[24,128]{1,0:T(8,128)S(1)} %get-tuple-element.22), channel_id=1, source_target_pairs={{0,1},{1,2},{2,3},{3,4},{4,5},{5,6},{6,7},{7,8},{8,9},{9,10},{10,1... | collective-permute-start | bytes 36872 | tf_op jit(solution)/shard_map/ppermute | solution.py:482
  19.9 10.2 %collective-permute-start.1 = (f32[24,128]{1,0:T(8,128)S(1)}, f32[24,128]{1,0:T(8,128)S(1)}, u32[]{:S(2)}, u32[]{:S(2)}) collective-permute-start(f32[24,128]{1,0:T(8,128)S(1)} %get-tuple-element.23), channel_id=1, source_target_pairs={{1,0},{2,1},{3,2},{4,3},{5,4},{6,5},{7,6},{8,7},{9,8},{10,9},{11,1... | collective-permute-start | bytes 36872 | tf_op jit(solution)/shard_map/ppermute | solution.py:482
  21.2 6.2 %collective-permute-start.2 = (f32[16,128]{1,0:T(8,128)S(1)}, f32[16,128]{1,0:T(8,128)S(1)}, u32[]{:S(2)}, u32[]{:S(2)}) collective-permute-start(f32[16,128]{1,0:T(8,128)S(1)} %get-tuple-element.24), channel_id=1, source_target_pairs={{0,16},{16,32},{32,48},{48,64},{64,80},{80,96},{96,112},{1,17},{17... | collective-permute-start | bytes 24584 | tf_op jit(solution)/shard_map/ppermute | solution.py:482
  24.8 5.3 %collective-permute-start.3 = (f32[16,128]{1,0:T(8,128)S(1)}, f32[16,128]{1,0:T(8,128)S(1)}, u32[]{:S(2)}, u32[]{:S(2)}) collective-permute-start(f32[16,128]{1,0:T(8,128)S(1)} %get-tuple-element.25), channel_id=1, source_target_pairs={{16,0},{32,16},{48,32},{64,48},{80,64},{96,80},{112,96},{17,1},{33... | collective-permute-start | bytes 24584 | tf_op jit(solution)/shard_map/ppermute | solution.py:482
  36.9 20.9 %all-to-all-start.1 = ((bf16[128,3,4,128]{3,2,1,0:T(4,128)(2,1)}), bf16[128,3,4,128]{3,2,1,0:T(4,128)(2,1)}, u32[]{:S(2)}, u32[]{:S(2)}) async-start(bf16[128,3,4,128]{3,2,1,0:T(4,128)(2,1)} %bitcast.30), calls=%async_computation.1 | async-start | bytes 786432 | tf_op jit(solution)/shard_map/all_to_all | solution.py:487
  45.4 18.8 %copy-start.1 = (f32[41,41]{1,0:T(8,128)S(1)}, f32[41,41]{1,0:T(8,128)}, u32[]{:S(2)}) copy-start(f32[41,41]{1,0:T(8,128)} %scale_ref.1) | copy-start | bytes 20176
  60.2 14.9 %all-to-all-start.2 = ((f32[128,1,384]{2,1,0:T(1,128)}), f32[128,1,384]{2,1,0:T(1,128)S(1)}, u32[]{:S(2)}, u32[]{:S(2)}) async-start(f32[128,1,384]{2,1,0:T(1,128)} %bitcast.31), calls=%async_computation.2 | async-start | bytes 393216 | tf_op jit(solution)/shard_map/all_to_all | solution.py:487
  64.2 0.8 %copy-start.2 = (f32[128,128]{1,0:T(8,128)S(1)}, f32[128,128]{1,0:T(8,128)}, u32[]{:S(2)}) copy-start(f32[128,128]{1,0:T(8,128)} %get-tuple-element.34.forcing_ref) | copy-start | bytes 196612

commit v7 on v6

--- a/solution.py
+++ b/solution.py
@@ -14,6 +14,7 @@
 DEV = GX * GY
 PC = 384
 CAP = 3
+BACK = 4
 NB = 144
 HALO = 4
 ROWS_X = TX + 2 * HALO
@@ -149,7 +150,6 @@
     wide_ref[...] = jnp.zeros_like(wide_ref)
     for f in range(F):
         wide_ref[f, :, :TY] = s_ref[f]
-    strips(wide_ref, low_ref, high_ref, top_ref, bottom_ref)
     corners = corner_rows(wide_ref)
     for k, step in enumerate(CORNERS):
         other, there = neighbour(step)
@@ -189,6 +189,7 @@
                 z_ref[pl.ds(i * GY * ROWS + WQ, GY, stride=ROWS), :] = left[LEFT.index(i)]
         z_ref[pl.ds(pair * size + ROWS - 1, 2 * GY, stride=ROWS), :] = slots[2 * GY * pair : 2 * GY * (pair + 1)]
         copies.append(write(z_ref, out_ref, out_any, sems.at[pair], pl.ds(pair * size, size)))
+    strips(wide_ref, low_ref, high_ref, top_ref, bottom_ref)
     for copy in copies:
         copy.wait()
 
@@ -352,16 +353,17 @@
 ):
     column = column_of(owner_ref[...])
     number, owner = by_thirds(column)
-    source = column_of(owner * CAP + rank_of(column, owner, number))
-    back_ref[...] = (source == iota((NB, CAP * DEV), 1)).astype(f32).astype(bf16)
+    source = column_of(owner * BACK + rank_of(column, owner, number))
+    back_ref[...] = (source == iota((NB, BACK * DEV), 1)).astype(f32).astype(bf16)
     slot_ref[...] = got_ref[...].astype(f32)
     slots = slot_ref[pl.ds(ROWS - 1, DEV, stride=ROWS), :].astype(i32)
     lane = iota((DEV, OCEAN * F), 1)
+    row_ref[...] = jnp.zeros_like(row_ref)
     for s in range(CAP):
         target = slots[:, s : s + 1] * F
         for f in range(F):
             z_ref[pl.ds(s * F + f, DEV, stride=CAP * F), :] = (lane == jnp.where(target < 0, -1, target + f)).astype(f32)
-        row_ref[pl.ds(s, DEV, stride=CAP), :] = (lane == target).astype(f32)
+        row_ref[pl.ds(s, DEV, stride=BACK), :] = (lane == target).astype(f32)
     give_ref[...] = row_ref[...].astype(bf16)
     hot = jnp.swapaxes(z_ref[...], 0, 1)
     hot_ref[...] = hot.astype(bf16)
@@ -387,8 +389,7 @@
     forcing = sums * inverse_ref[...] + cover_ref[...]
     forcing_ref[...] = forcing
     top = top_ref[: OCEAN * F, :] + top_ref[OCEAN * F : OCEAN * F + 1, :] * forcing
-    back = dot(give_ref[...], jnp.concatenate(split3(top), axis=1))
-    out_ref[...] = back[:, :CELLS] + back[:, CELLS : 2 * CELLS] + back[:, 2 * CELLS :]
+    out_ref[...] = dot(give_ref[...], top.astype(bf16)).astype(bf16)
 
 def mix_kernel(scale_ref, forcing_ref, marine_ref, out_ref, high_ref, low_ref):
     layers = marine_ref.shape[0]
@@ -420,8 +421,7 @@
 
 
 def skin_kernel(got_ref, back_ref, out_ref, tile_ref):
-    x = dot(back_ref[...], jnp.concatenate(split3(got_ref[...]), axis=1))
-    x = x[:, :CELLS] + x[:, CELLS : 2 * CELLS] + x[:, 2 * CELLS :]
+    x = dot(back_ref[...], got_ref[...])
     rows = NB // CAP
     t0, t1, t2 = x[:rows], x[rows : 2 * rows], x[2 * rows :]
     lane = iota((rows, CELLS), 1)
@@ -531,19 +531,19 @@
     marine = marine_stratum_values.reshape(F, layers, OCEAN, CELLS).transpose(1, 2, 0, 3).reshape(layers, OCEAN * F, CELLS)
     marine_late, got_late, flux = lax.optimization_barrier((marine, got, flux))
     block = ((OCEAN * F, CELLS), f32)
-    hot, give = ((OCEAN * F, DEV * CAP * F), bf16), ((DEV * CAP, OCEAN * F), bf16)
+    hot, give = ((OCEAN * F, DEV * CAP * F), bf16), ((DEV * BACK, OCEAN * F), bf16)
     hot, give, inverse, cover, back = call(
         hot_kernel, "vHH", "HHHHv", (got_late, by_block(coarse_interface_exchange), owner),
-        (hot, give, block, block, ((NB, CAP * DEV), bf16)),
-        (((DEV * CAP * F, OCEAN * F), f32), ((DEV * ROWS, CELLS), f32), ((DEV * CAP, OCEAN * F), f32)),
+        (hot, give, block, block, ((NB, BACK * DEV), bf16)),
+        (((DEV * CAP * F, OCEAN * F), f32), ((DEV * ROWS, CELLS), f32), ((DEV * BACK, OCEAN * F), f32)),
     )
     (layer0,) = call(top_kernel, "Sp", "H", (diffusion_solver_operator, marine_late), (((OCEAN * F + 8, CELLS), f32),))
-    returned = ((DEV * CAP, CELLS), f32)
+    returned = ((DEV * BACK, CELLS), bf16)
     forcing, skins = call(
         ocean_kernel, "HHHHHH", "HH", (got_flux, hot, inverse, cover, layer0, give), (block, returned),
         lazy=True,
     )
-    arrived = exchange(skins, (DEV, 1, CAP * CELLS))
+    arrived = exchange(skins, (DEV, BACK, CELLS))
     part = 32
     refreshed = pl.pallas_call(
         mix_kernel,

time: 76.6 us -> 75.9 us (level)
  no operation moved by 1% of the time
where the time goes in v7:
time: 75.9 us; the launch traced here: 75.3 us
  starting transfers between devices  34.1 us (45%)
  Pallas kernels  21.4 us (28%)
  waiting for transfers between devices  17.6 us (23%)
  between operations  1.43 us (2%)
  local copies, waits for them, and re-layouts  0.85 us (1%)
    all_to_all x3, starting transfers between devices, exchange(): lax.all_to_all(split, ('gx', 'gy'), split_axis=0, concat_axis=0, tiled=True)  23.9 us
    pallas_call x6, Pallas kernels, call(): pl.pallas_call(body, out_shape=tuple((MEMORY[c](s, d) if c in MEMORY else...  16.9 us
    all_to_all x3, waiting for transfers between devices, exchange(): lax.all_to_all(split, ('gx', 'gy'), split_axis=0, concat_axis=0, tiled=True)  14.9 us
    ppermute x4, starting transfers between devices, shift(): lax.ppermute(value, axis, [(i, i + by) for i in range(n) if 0 <= i + by <...  10.1 us
    pallas_call x1, Pallas kernels, on_device(): pl.pallas_call(mix_kernel, out_shape=jax.ShapeDtypeStruct((layers, OCEAN...  4.54 us
    ppermute x4, waiting for transfers between devices, shift(): lax.ppermute(value, axis, [(i, i + by) for i in range(n) if 0 <= i + by <...  2.69 us
  transfers between devices with their start and end apart: 7, of which 4 were waited for; matrix products, arithmetic and copies ran while one was open for 0% of the time, Pallas kernels for 12%

profile of v7, /device:TPU:1, one launch (start us, length us, event | category | flops | bytes accessed | tf_op | source)
XLA Modules:
  0.0 75.3 jit_solution(14614976983345642052)
XLA Ops:
  0.6 4.3 %shard_map.121 = (bf16[2560,128]{1,0:T(8,128)(2,1)}, f32[24,128]{1,0:T(8,128)S(1)}, f32[24,128]{1,0:T(8,128)S(1)}, f32[16,128]{1,0:T(8,128)S(1)}, f32[16,128]{1,0:T(8,128)S(1)}) custom-call(s32[2]{0:T(128)} %refs_1_.1, s32[1,144]{1,0:T(1,128)} %bitcast.33, s32[1,144]{1,0:T(1,128)} %bitcast.36, bf16[4,384,384]{2,1,0:T(8,128)(2,1)} %refs_3_.1, ...), custom_call_target="tpu_custom_call" | custom-call | tf_op jit(solution)/shard_map/pallas_call | solution.py:467
  4.9 11.5 %all-to-all-start = ((bf16[128,5,4,128]{3,2,1,0:T(4,128)(2,1)}), bf16[128,5,4,128]{3,2,1,0:T(4,128)(2,1)S(1)}, u32[]{:S(2)}, u32[]{:S(2)}) async-start(bf16[128,5,4,128]{3,2,1,0:T(4,128)(2,1)} %bitcast.29), calls=%async_computation | async-start | bytes 1310720 | tf_op jit(solution)/shard_map/all_to_all | solution.py:487
  16.5 3.3 %collective-permute-start = (f32[24,128]{1,0:T(8,128)S(1)}, f32[24,128]{1,0:T(8,128)S(1)}, u32[]{:S(2)}, u32[]{:S(2)}) collective-permute-start(f32[24,128]{1,0:T(8,128)S(1)} %get-tuple-element.22), channel_id=1, source_target_pairs={{0,1},{1,2},{2,3},{3,4},{4,5},{5,6},{6,7},{7,8},{8,9},{9,10},{10,1... | collective-permute-start | bytes 36872 | tf_op jit(solution)/shard_map/ppermute | solution.py:482
  19.8 1.3 %collective-permute-start.1 = (f32[24,128]{1,0:T(8,128)S(1)}, f32[24,128]{1,0:T(8,128)S(1)}, u32[]{:S(2)}, u32[]{:S(2)}) collective-permute-start(f32[24,128]{1,0:T(8,128)S(1)} %get-tuple-element.23), channel_id=1, source_target_pairs={{1,0},{2,1},{3,2},{4,3},{5,4},{6,5},{7,6},{8,7},{9,8},{10,9},{11,1... | collective-permute-start | bytes 36872 | tf_op jit(solution)/shard_map/ppermute | solution.py:482
  21.1 3.6 %collective-permute-start.2 = (f32[16,128]{1,0:T(8,128)S(1)}, f32[16,128]{1,0:T(8,128)S(1)}, u32[]{:S(2)}, u32[]{:S(2)}) collective-permute-start(f32[16,128]{1,0:T(8,128)S(1)} %get-tuple-element.24), channel_id=1, source_target_pairs={{0,16},{16,32},{32,48},{48,64},{64,80},{80,96},{96,112},{1,17},{17... | collective-permute-start | bytes 24584 | tf_op jit(solution)/shard_map/ppermute | solution.py:482
  24.7 1.9 %collective-permute-start.3 = (f32[16,128]{1,0:T(8,128)S(1)}, f32[16,128]{1,0:T(8,128)S(1)}, u32[]{:S(2)}, u32[]{:S(2)}) collective-permute-start(f32[16,128]{1,0:T(8,128)S(1)} %get-tuple-element.25), channel_id=1, source_target_pairs={{16,0},{32,16},{48,32},{64,48},{80,64},{96,80},{112,96},{17,1},{33... | collective-permute-start | bytes 24584 | tf_op jit(solution)/shard_map/ppermute | solution.py:482
  27.3 0.0 collective-permute-done.2.refs_7_
  27.3 2.7 %collective-permute-done.3.refs_8_ = f32[16,128]{1,0:T(8,128)S(1)} collective-permute-done((f32[16,128]{1,0:T(8,128)S(1)}, f32[16,128]{1,0:T(8,128)S(1)}, u32[]{:S(2)}, u32[]{:S(2)}) %collective-permute-start.3) | collective-permute-done | bytes 8224 | tf_op jit(solution)/shard_map/ppermute | solution.py:482
  29.9 0.0 collective-permute-done.refs_5_
  29.9 0.0 collective-permute-done.1.refs_6_
  30.0 1.9 %all-to-all-done = bf16[128,5,4,128]{3,2,1,0:T(4,128)(2,1)S(1)} async-done(((bf16[128,5,4,128]{3,2,1,0:T(4,128)(2,1)}), bf16[128,5,4,128]{3,2,1,0:T(4,128)(2,1)S(1)}, u32[]{:S(2)}, u32[]{:S(2)}) %all-to-all-start) | async-done | bytes 655392 | tf_op jit(solution)/shard_map/all_to_all | solution.py:487
  31.9 4.9 %shard_map.122 = (f32[4,192,96]{2,1,0:T(8,128)}, bf16[1536,128]{1,0:T(8,128)(2,1)}) custom-call(s32[1]{0:T(128)S(6)} %min.3.refs_0_, s32[2]{0:T(128)} %refs_1_.1, s32[1,144]{1,0:T(1,128)} %bitcast.34, bf16[2560,128]{1,0:T(8,128)(2,1)S(1)} %bitcast.25, f32[4,192,96]{2,1,0:T(8,128)} %refs_4_.3, f32[24,128]{1,0:T(8,128)S(1)} %collective-permute-done.refs_5_, ...), custom_call_target="tpu_custom_call" | custom-call | tf_op jit(solution)/shard_map/pallas_call | solution.py:467
  36.8 0.0 copy-start.1
  36.8 8.5 %all-to-all-start.1 = ((bf16[128,3,4,128]{3,2,1,0:T(4,128)(2,1)}), bf16[128,3,4,128]{3,2,1,0:T(4,128)(2,1)}, u32[]{:S(2)}, u32[]{:S(2)}) async-start(bf16[128,3,4,128]{3,2,1,0:T(4,128)(2,1)} %bitcast.30), calls=%async_computation.1 | async-start | bytes 786432 | tf_op jit(solution)/shard_map/all_to_all | solution.py:487
  45.3 1.9 %shard_map.124.refs_4_ = f32[136,128]{1,0:T(8,128)} custom-call(f32[41,41]{1,0:T(8,128)} %scale_ref.1, f32[41,128,128]{2,1,0:T(8,128)S(1)} %bitcast.23), custom_call_target="tpu_custom_call" | custom-call | tf_op jit(solution)/shard_map/pallas_call | solution.py:467
  47.1 2.5 %shard_map.123 = (bf16[128,1536]{1,0:T(8,128)(2,1)}, bf16[512,128]{1,0:T(8,128)(2,1)}, f32[128,128]{1,0:T(8,128)}, f32[128,128]{1,0:T(8,128)}, bf16[144,512]{1,0:T(8,128)(2,1)S(1)}) custom-call(bf16[2560,128]{1,0:T(8,128)(2,1)S(1)} %bitcast.26, f32[128,128]{1,0:T(8,128)} %bitcast.32, s32[1,144]{1,0:T(1,128)} %bitcast.35), custom_call_target="tpu_custom_call" | custom-call | tf_op jit(solution)/shard_map/pallas_call | solution.py:467
  49.7 8.1 %all-to-all-done.1 = bf16[128,3,4,128]{3,2,1,0:T(4,128)(2,1)} async-done(((bf16[128,3,4,128]{3,2,1,0:T(4,128)(2,1)}), bf16[128,3,4,128]{3,2,1,0:T(4,128)(2,1)}, u32[]{:S(2)}, u32[]{:S(2)}) %all-to-all-start.1) | async-done | bytes 393248 | tf_op jit(solution)/shard_map/all_to_all | solution.py:487
  57.7 2.3 %shard_map.125 = (f32[128,128]{1,0:T(8,128)}, bf16[512,128]{1,0:T(8,128)(2,1)}) custom-call(bf16[1536,128]{1,0:T(8,128)(2,1)} %bitcast.5.refs_0_, bf16[128,1536]{1,0:T(8,128)(2,1)} %get-tuple-element.29.refs_1_, f32[128,128]{1,0:T(8,128)} %get-tuple-element.30.refs_2_, f32[128,128]{1,0:T(8,128)} %get-tuple-element.31.refs_3_, ...), custom_call_target="tpu_custom_call" | custom-call | tf_op jit(solution)/shard_map/pallas_call | solution.py:467
  60.1 4.0 %all-to-all-start.2 = ((bf16[128,4,128]{2,1,0:T(4,128)(2,1)}), bf16[128,4,128]{2,1,0:T(4,128)(2,1)S(1)}, u32[]{:S(2)}, u32[]{:S(2)}) async-start(bf16[128,4,128]{2,1,0:T(4,128)(2,1)} %bitcast.31), calls=%async_computation.2 | async-start | bytes 262144 | tf_op jit(solution)/shard_map/all_to_all | solution.py:487
  64.1 0.0 copy-start.2
  64.1 0.8 %copy-done.2 = f32[128,128]{1,0:T(8,128)S(1)} copy-done((f32[128,128]{1,0:T(8,128)S(1)}, f32[128,128]{1,0:T(8,128)}, u32[]{:S(2)}) %copy-start.2) | copy-done | bytes 65560
  64.9 4.5 %shard_map.126 = f32[41,128,128]{2,1,0:T(8,128)} custom-call(f32[41,41]{1,0:T(8,128)S(1)} %copy-done.1, f32[128,128]{1,0:T(8,128)S(1)} %copy-done.2, f32[41,128,128]{2,1,0:T(8,128)S(1)} %bitcast.24), custom_call_target="tpu_custom_call" | custom-call | tf_op jit(solution)/shard_map/pallas_call | solution.py:548
  69.5 4.9 %all-to-all-done.2 = bf16[128,4,128]{2,1,0:T(4,128)(2,1)S(1)} async-done(((bf16[128,4,128]{2,1,0:T(4,128)(2,1)}), bf16[128,4,128]{2,1,0:T(4,128)(2,1)S(1)}, u32[]{:S(2)}, u32[]{:S(2)}) %all-to-all-start.2) | async-done | bytes 131104 | tf_op jit(solution)/shard_map/all_to_all | solution.py:487
  74.4 0.9 %shard_map.127 = f32[192,96]{1,0:T(8,128)} custom-call(bf16[512,128]{1,0:T(8,128)(2,1)S(1)} %bitcast.27, bf16[144,512]{1,0:T(8,128)(2,1)S(1)} %get-tuple-element.36.refs_1_), custom_call_target="tpu_custom_call" | custom-call | tf_op jit(solution)/shard_map/pallas_call | solution.py:467
  (3 shorter events, 0.0 us)
Async XLA Ops:
  0.6 44.6 %copy-start = (f32[4,41,4096]{2,0,1:T(4,128)S(1)}, f32[4,41,4096]{2,0,1:T(4,128)}, u32[]{:S(2)}) copy-start(f32[4,41,4096]{2,0,1:T(4,128)} %param.18) | copy-start | bytes 8060932
  4.9 26.9 %all-to-all-start = ((bf16[128,5,4,128]{3,2,1,0:T(4,128)(2,1)}), bf16[128,5,4,128]{3,2,1,0:T(4,128)(2,1)S(1)}, u32[]{:S(2)}, u32[]{:S(2)}) async-start(bf16[128,5,4,128]{3,2,1,0:T(4,128)(2,1)} %bitcast.29), calls=%async_computation | async-start | bytes 1310720 | tf_op jit(solution)/shard_map/all_to_all | solution.py:487
  16.5 13.5 %collective-permute-start = (f32[24,128]{1,0:T(8,128)S(1)}, f32[24,128]{1,0:T(8,128)S(1)}, u32[]{:S(2)}, u32[]{:S(2)}) collective-permute-start(f32[24,128]{1,0:T(8,128)S(1)} %get-tuple-element.22), channel_id=1, source_target_pairs={{0,1},{1,2},{2,3},{3,4},{4,5},{5,6},{6,7},{7,8},{8,9},{9,10},{10,1... | collective-permute-start | bytes 36872 | tf_op jit(solution)/shard_map/ppermute | solution.py:482
  19.8 10.2 %collective-permute-start.1 = (f32[24,128]{1,0:T(8,128)S(1)}, f32[24,128]{1,0:T(8,128)S(1)}, u32[]{:S(2)}, u32[]{:S(2)}) collective-permute-start(f32[24,128]{1,0:T(8,128)S(1)} %get-tuple-element.23), channel_id=1, source_target_pairs={{1,0},{2,1},{3,2},{4,3},{5,4},{6,5},{7,6},{8,7},{9,8},{10,9},{11,1... | collective-permute-start | bytes 36872 | tf_op jit(solution)/shard_map/ppermute | solution.py:482
  21.1 6.2 %collective-permute-start.2 = (f32[16,128]{1,0:T(8,128)S(1)}, f32[16,128]{1,0:T(8,128)S(1)}, u32[]{:S(2)}, u32[]{:S(2)}) collective-permute-start(f32[16,128]{1,0:T(8,128)S(1)} %get-tuple-element.24), channel_id=1, source_target_pairs={{0,16},{16,32},{32,48},{48,64},{64,80},{80,96},{96,112},{1,17},{17... | collective-permute-start | bytes 24584 | tf_op jit(solution)/shard_map/ppermute | solution.py:482
  24.7 5.3 %collective-permute-start.3 = (f32[16,128]{1,0:T(8,128)S(1)}, f32[16,128]{1,0:T(8,128)S(1)}, u32[]{:S(2)}, u32[]{:S(2)}) collective-permute-start(f32[16,128]{1,0:T(8,128)S(1)} %get-tuple-element.25), channel_id=1, source_target_pairs={{16,0},{32,16},{48,32},{64,48},{80,64},{96,80},{112,96},{17,1},{33... | collective-permute-start | bytes 24584 | tf_op jit(solution)/shard_map/ppermute | solution.py:482
  36.8 27.3 %copy-start.1 = (f32[41,41]{1,0:T(8,128)S(1)}, f32[41,41]{1,0:T(8,128)}, u32[]{:S(2)}) copy-start(f32[41,41]{1,0:T(8,128)} %scale_ref.1) | copy-start | bytes 20176
  36.8 20.9 %all-to-all-start.1 = ((bf16[128,3,4,128]{3,2,1,0:T(4,128)(2,1)}), bf16[128,3,4,128]{3,2,1,0:T(4,128)(2,1)}, u32[]{:S(2)}, u32[]{:S(2)}) async-start(bf16[128,3,4,128]{3,2,1,0:T(4,128)(2,1)} %bitcast.30), calls=%async_computation.1 | async-start | bytes 786432 | tf_op jit(solution)/shard_map/all_to_all | solution.py:487
  60.1 14.3 %all-to-all-start.2 = ((bf16[128,4,128]{2,1,0:T(4,128)(2,1)}), bf16[128,4,128]{2,1,0:T(4,128)(2,1)S(1)}, u32[]{:S(2)}, u32[]{:S(2)}) async-start(bf16[128,4,128]{2,1,0:T(4,128)(2,1)} %bitcast.31), calls=%async_computation.2 | async-start | bytes 262144 | tf_op jit(solution)/shard_map/all_to_all | solution.py:487
  64.1 0.8 %copy-start.2 = (f32[128,128]{1,0:T(8,128)S(1)}, f32[128,128]{1,0:T(8,128)}, u32[]{:S(2)}) copy-start(f32[128,128]{1,0:T(8,128)} %get-tuple-element.34.forcing_ref) | copy-start | bytes 196612

commit v8 on v6

--- a/solution.py
+++ b/solution.py
@@ -149,7 +149,6 @@
     wide_ref[...] = jnp.zeros_like(wide_ref)
     for f in range(F):
         wide_ref[f, :, :TY] = s_ref[f]
-    strips(wide_ref, low_ref, high_ref, top_ref, bottom_ref)
     corners = corner_rows(wide_ref)
     for k, step in enumerate(CORNERS):
         other, there = neighbour(step)
@@ -189,6 +188,7 @@
                 z_ref[pl.ds(i * GY * ROWS + WQ, GY, stride=ROWS), :] = left[LEFT.index(i)]
         z_ref[pl.ds(pair * size + ROWS - 1, 2 * GY, stride=ROWS), :] = slots[2 * GY * pair : 2 * GY * (pair + 1)]
         copies.append(write(z_ref, out_ref, out_any, sems.at[pair], pl.ds(pair * size, size)))
+    strips(wide_ref, low_ref, high_ref, top_ref, bottom_ref)
     for copy in copies:
         copy.wait()
 
@@ -515,8 +515,7 @@
     got = exchange(windows, (DEV, ROWS // 4, 4, CELLS))
     left, right = shift(high, "gy", 1), shift(low, "gy", -1)
     before, after = shift(bottom, "gx", 1), shift(top, "gx", -1)
-    holder, _ = lax.optimization_barrier((holder_flat, windows))
-    holder = jnp.minimum(holder, DEV - 1)
+    holder = holder_flat
     sent, strips = ((DEV * CAP * F, CELLS), bf16), ((F, TX, CELLS), f32)
     nest_next, flux = call(
         nest_kernel, "sSHvHvvvvH", "hh",

time: 76.6 us -> 76.5 us (level)
  no operation moved by 1% of the time
where the time goes in v8:
time: 76.5 us; the launch traced here: 76 us
  starting transfers between devices  34.1 us (45%)
  Pallas kernels  21.4 us (28%)
  waiting for transfers between devices  18.2 us (24%)
  between operations  1.42 us (2%)
  local copies, waits for them, and re-layouts  0.85 us (1%)
    all_to_all x3, starting transfers between devices, exchange(): lax.all_to_all(split, ('gx', 'gy'), split_axis=0, concat_axis=0, tiled=True)  23.9 us
    pallas_call x6, Pallas kernels, call(): pl.pallas_call(body, out_shape=tuple((MEMORY[c](s, d) if c in MEMORY else...  16.9 us
    all_to_all x3, waiting for transfers between devices, exchange(): lax.all_to_all(split, ('gx', 'gy'), split_axis=0, concat_axis=0, tiled=True)  15.5 us
    ppermute x4, starting transfers between devices, shift(): lax.ppermute(value, axis, [(i, i + by) for i in range(n) if 0 <= i + by <...  10.1 us
    pallas_call x1, Pallas kernels, on_device(): pl.pallas_call(mix_kernel, out_shape=jax.ShapeDtypeStruct((layers, OCEAN...  4.54 us
    ppermute x4, waiting for transfers between devices, shift(): lax.ppermute(value, axis, [(i, i + by) for i in range(n) if 0 <= i + by <...  2.69 us
  transfers between devices with their start and end apart: 7, of which 4 were waited for; matrix products, arithmetic and copies ran while one was open for 0% of the time, Pallas kernels for 12%

profile of v8, /device:TPU:1, one launch (start us, length us, event | category | flops | bytes accessed | tf_op | source)
XLA Modules:
  0.0 76.0 jit_solution(10144509273603705060)
XLA Ops:
  0.6 4.3 %shard_map.121 = (bf16[2560,128]{1,0:T(8,128)(2,1)}, f32[24,128]{1,0:T(8,128)S(1)}, f32[24,128]{1,0:T(8,128)S(1)}, f32[16,128]{1,0:T(8,128)S(1)}, f32[16,128]{1,0:T(8,128)S(1)}) custom-call(s32[2]{0:T(128)} %refs_1_.1, s32[1,144]{1,0:T(1,128)} %bitcast.33, s32[1,144]{1,0:T(1,128)} %bitcast.36, bf16[4,384,384]{2,1,0:T(8,128)(2,1)} %refs_3_.1, ...), custom_call_target="tpu_custom_call" | custom-call | tf_op jit(solution)/shard_map/pallas_call | solution.py:467
  4.9 11.5 %all-to-all-start = ((bf16[128,5,4,128]{3,2,1,0:T(4,128)(2,1)}), bf16[128,5,4,128]{3,2,1,0:T(4,128)(2,1)S(1)}, u32[]{:S(2)}, u32[]{:S(2)}) async-start(bf16[128,5,4,128]{3,2,1,0:T(4,128)(2,1)} %bitcast.29), calls=%async_computation | async-start | bytes 1310720 | tf_op jit(solution)/shard_map/all_to_all | solution.py:487
  16.5 3.3 %collective-permute-start = (f32[24,128]{1,0:T(8,128)S(1)}, f32[24,128]{1,0:T(8,128)S(1)}, u32[]{:S(2)}, u32[]{:S(2)}) collective-permute-start(f32[24,128]{1,0:T(8,128)S(1)} %get-tuple-element.20), channel_id=1, source_target_pairs={{0,1},{1,2},{2,3},{3,4},{4,5},{5,6},{6,7},{7,8},{8,9},{9,10},{10,1... | collective-permute-start | bytes 36872 | tf_op jit(solution)/shard_map/ppermute | solution.py:482
  19.8 1.3 %collective-permute-start.1 = (f32[24,128]{1,0:T(8,128)S(1)}, f32[24,128]{1,0:T(8,128)S(1)}, u32[]{:S(2)}, u32[]{:S(2)}) collective-permute-start(f32[24,128]{1,0:T(8,128)S(1)} %get-tuple-element.21), channel_id=1, source_target_pairs={{1,0},{2,1},{3,2},{4,3},{5,4},{6,5},{7,6},{8,7},{9,8},{10,9},{11,1... | collective-permute-start | bytes 36872 | tf_op jit(solution)/shard_map/ppermute | solution.py:482
  21.1 3.6 %collective-permute-start.2 = (f32[16,128]{1,0:T(8,128)S(1)}, f32[16,128]{1,0:T(8,128)S(1)}, u32[]{:S(2)}, u32[]{:S(2)}) collective-permute-start(f32[16,128]{1,0:T(8,128)S(1)} %get-tuple-element.22), channel_id=1, source_target_pairs={{0,16},{16,32},{32,48},{48,64},{64,80},{80,96},{96,112},{1,17},{17... | collective-permute-start | bytes 24584 | tf_op jit(solution)/shard_map/ppermute | solution.py:482
  24.7 1.9 %collective-permute-start.3 = (f32[16,128]{1,0:T(8,128)S(1)}, f32[16,128]{1,0:T(8,128)S(1)}, u32[]{:S(2)}, u32[]{:S(2)}) collective-permute-start(f32[16,128]{1,0:T(8,128)S(1)} %get-tuple-element.23), channel_id=1, source_target_pairs={{16,0},{32,16},{48,32},{64,48},{80,64},{96,80},{112,96},{17,1},{33... | collective-permute-start | bytes 24584 | tf_op jit(solution)/shard_map/ppermute | solution.py:482
  27.3 0.0 collective-permute-done.2.refs_7_
  27.3 2.7 %collective-permute-done.3.refs_8_ = f32[16,128]{1,0:T(8,128)S(1)} collective-permute-done((f32[16,128]{1,0:T(8,128)S(1)}, f32[16,128]{1,0:T(8,128)S(1)}, u32[]{:S(2)}, u32[]{:S(2)}) %collective-permute-start.3) | collective-permute-done | bytes 8224 | tf_op jit(solution)/shard_map/ppermute | solution.py:482
  29.9 0.0 collective-permute-done.refs_5_
  29.9 0.0 collective-permute-done.1.refs_6_
  30.0 1.9 %all-to-all-done = bf16[128,5,4,128]{3,2,1,0:T(4,128)(2,1)S(1)} async-done(((bf16[128,5,4,128]{3,2,1,0:T(4,128)(2,1)}), bf16[128,5,4,128]{3,2,1,0:T(4,128)(2,1)S(1)}, u32[]{:S(2)}, u32[]{:S(2)}) %all-to-all-start) | async-done | bytes 655392 | tf_op jit(solution)/shard_map/all_to_all | solution.py:487
  31.9 4.9 %shard_map.122 = (f32[4,192,96]{2,1,0:T(8,128)}, bf16[1536,128]{1,0:T(8,128)(2,1)}) custom-call(s32[1]{0:T(128)S(6)} %copy.20.refs_0_, s32[2]{0:T(128)} %refs_1_.1, s32[1,144]{1,0:T(1,128)} %bitcast.34, bf16[2560,128]{1,0:T(8,128)(2,1)S(1)} %bitcast.25, f32[4,192,96]{2,1,0:T(8,128)} %refs_4_.3, f32[24,128]{1,0:T(8,128)S(1)} %collective-permute-done.refs_5_, ...), custom_call_target="tpu_custom_call" | custom-call | tf_op jit(solution)/shard_map/pallas_call | solution.py:467
  36.8 8.5 %all-to-all-start.1 = ((bf16[128,3,4,128]{3,2,1,0:T(4,128)(2,1)}), bf16[128,3,4,128]{3,2,1,0:T(4,128)(2,1)}, u32[]{:S(2)}, u32[]{:S(2)}) async-start(bf16[128,3,4,128]{3,2,1,0:T(4,128)(2,1)} %bitcast.30), calls=%async_computation.1 | async-start | bytes 786432 | tf_op jit(solution)/shard_map/all_to_all | solution.py:487
  45.3 0.0 copy-start.1
  45.3 1.9 %shard_map.124.refs_4_ = f32[136,128]{1,0:T(8,128)} custom-call(f32[41,41]{1,0:T(8,128)} %scale_ref.1, f32[41,128,128]{2,1,0:T(8,128)S(1)} %bitcast.23), custom_call_target="tpu_custom_call" | custom-call | tf_op jit(solution)/shard_map/pallas_call | solution.py:467
  47.1 2.5 %shard_map.123 = (bf16[128,1536]{1,0:T(8,128)(2,1)}, bf16[384,128]{1,0:T(8,128)(2,1)}, f32[128,128]{1,0:T(8,128)}, f32[128,128]{1,0:T(8,128)}, bf16[144,384]{1,0:T(8,128)(2,1)S(1)}) custom-call(bf16[2560,128]{1,0:T(8,128)(2,1)S(1)} %bitcast.26, f32[128,128]{1,0:T(8,128)} %bitcast.32, s32[1,144]{1,0:T(1,128)} %bitcast.35), custom_call_target="tpu_custom_call" | custom-call | tf_op jit(solution)/shard_map/pallas_call | solution.py:467
  49.6 8.1 %all-to-all-done.1 = bf16[128,3,4,128]{3,2,1,0:T(4,128)(2,1)} async-done(((bf16[128,3,4,128]{3,2,1,0:T(4,128)(2,1)}), bf16[128,3,4,128]{3,2,1,0:T(4,128)(2,1)}, u32[]{:S(2)}, u32[]{:S(2)}) %all-to-all-start.1) | async-done | bytes 393248 | tf_op jit(solution)/shard_map/all_to_all | solution.py:487
  57.7 2.4 %shard_map.125 = (f32[128,128]{1,0:T(8,128)}, f32[384,128]{1,0:T(8,128)}) custom-call(bf16[1536,128]{1,0:T(8,128)(2,1)} %bitcast.5.refs_0_, bf16[128,1536]{1,0:T(8,128)(2,1)} %get-tuple-element.27.refs_1_, f32[128,128]{1,0:T(8,128)} %get-tuple-element.28.refs_2_, f32[128,128]{1,0:T(8,128)} %get-tuple-element.29.refs_3_, f32[136,128]{1,0:T(8,128)} %shard_map.124.refs_4_, ...), custom_call_target="tpu_custom_call" | custom-call | tf_op jit(solution)/shard_map/pallas_call | solution.py:467
  60.1 4.0 %all-to-all-start.2 = ((f32[128,1,384]{2,1,0:T(1,128)}), f32[128,1,384]{2,1,0:T(1,128)S(1)}, u32[]{:S(2)}, u32[]{:S(2)}) async-start(f32[128,1,384]{2,1,0:T(1,128)} %bitcast.31), calls=%async_computation.2 | async-start | bytes 393216 | tf_op jit(solution)/shard_map/all_to_all | solution.py:487
  64.1 0.0 copy-start.2
  64.1 0.8 %copy-done.2 = f32[128,128]{1,0:T(8,128)S(1)} copy-done((f32[128,128]{1,0:T(8,128)S(1)}, f32[128,128]{1,0:T(8,128)}, u32[]{:S(2)}) %copy-start.2) | copy-done | bytes 65560
  64.9 4.5 %shard_map.126 = f32[41,128,128]{2,1,0:T(8,128)} custom-call(f32[41,41]{1,0:T(8,128)S(1)} %copy-done.1, f32[128,128]{1,0:T(8,128)S(1)} %copy-done.2, f32[41,128,128]{2,1,0:T(8,128)S(1)} %bitcast.24), custom_call_target="tpu_custom_call" | custom-call | tf_op jit(solution)/shard_map/pallas_call | solution.py:547
  69.5 5.5 %all-to-all-done.2 = f32[128,1,384]{2,1,0:T(1,128)S(1)} async-done(((f32[128,1,384]{2,1,0:T(1,128)}), f32[128,1,384]{2,1,0:T(1,128)S(1)}, u32[]{:S(2)}, u32[]{:S(2)}) %all-to-all-start.2) | async-done | bytes 196640 | tf_op jit(solution)/shard_map/all_to_all | solution.py:487
  75.0 1.0 %shard_map.127 = f32[192,96]{1,0:T(8,128)} custom-call(f32[384,128]{1,0:T(8,128)S(1)} %bitcast.27, bf16[144,384]{1,0:T(8,128)(2,1)S(1)} %get-tuple-element.34.refs_1_), custom_call_target="tpu_custom_call" | custom-call | tf_op jit(solution)/shard_map/pallas_call | solution.py:467
  (3 shorter events, 0.0 us)
Async XLA Ops:
  0.6 44.6 %copy-start = (f32[4,41,4096]{2,0,1:T(4,128)S(1)}, f32[4,41,4096]{2,0,1:T(4,128)}, u32[]{:S(2)}) copy-start(f32[4,41,4096]{2,0,1:T(4,128)} %param.18) | copy-start | bytes 8060932
  4.9 26.9 %all-to-all-start = ((bf16[128,5,4,128]{3,2,1,0:T(4,128)(2,1)}), bf16[128,5,4,128]{3,2,1,0:T(4,128)(2,1)S(1)}, u32[]{:S(2)}, u32[]{:S(2)}) async-start(bf16[128,5,4,128]{3,2,1,0:T(4,128)(2,1)} %bitcast.29), calls=%async_computation | async-start | bytes 1310720 | tf_op jit(solution)/shard_map/all_to_all | solution.py:487
  16.5 13.5 %collective-permute-start = (f32[24,128]{1,0:T(8,128)S(1)}, f32[24,128]{1,0:T(8,128)S(1)}, u32[]{:S(2)}, u32[]{:S(2)}) collective-permute-start(f32[24,128]{1,0:T(8,128)S(1)} %get-tuple-element.20), channel_id=1, source_target_pairs={{0,1},{1,2},{2,3},{3,4},{4,5},{5,6},{6,7},{7,8},{8,9},{9,10},{10,1... | collective-permute-start | bytes 36872 | tf_op jit(solution)/shard_map/ppermute | solution.py:482
  19.8 10.2 %collective-permute-start.1 = (f32[24,128]{1,0:T(8,128)S(1)}, f32[24,128]{1,0:T(8,128)S(1)}, u32[]{:S(2)}, u32[]{:S(2)}) collective-permute-start(f32[24,128]{1,0:T(8,128)S(1)} %get-tuple-element.21), channel_id=1, source_target_pairs={{1,0},{2,1},{3,2},{4,3},{5,4},{6,5},{7,6},{8,7},{9,8},{10,9},{11,1... | collective-permute-start | bytes 36872 | tf_op jit(solution)/shard_map/ppermute | solution.py:482
  21.1 6.2 %collective-permute-start.2 = (f32[16,128]{1,0:T(8,128)S(1)}, f32[16,128]{1,0:T(8,128)S(1)}, u32[]{:S(2)}, u32[]{:S(2)}) collective-permute-start(f32[16,128]{1,0:T(8,128)S(1)} %get-tuple-element.22), channel_id=1, source_target_pairs={{0,16},{16,32},{32,48},{48,64},{64,80},{80,96},{96,112},{1,17},{17... | collective-permute-start | bytes 24584 | tf_op jit(solution)/shard_map/ppermute | solution.py:482
  24.7 5.3 %collective-permute-start.3 = (f32[16,128]{1,0:T(8,128)S(1)}, f32[16,128]{1,0:T(8,128)S(1)}, u32[]{:S(2)}, u32[]{:S(2)}) collective-permute-start(f32[16,128]{1,0:T(8,128)S(1)} %get-tuple-element.23), channel_id=1, source_target_pairs={{16,0},{32,16},{48,32},{64,48},{80,64},{96,80},{112,96},{17,1},{33... | collective-permute-start | bytes 24584 | tf_op jit(solution)/shard_map/ppermute | solution.py:482
  36.8 20.9 %all-to-all-start.1 = ((bf16[128,3,4,128]{3,2,1,0:T(4,128)(2,1)}), bf16[128,3,4,128]{3,2,1,0:T(4,128)(2,1)}, u32[]{:S(2)}, u32[]{:S(2)}) async-start(bf16[128,3,4,128]{3,2,1,0:T(4,128)(2,1)} %bitcast.30), calls=%async_computation.1 | async-start | bytes 786432 | tf_op jit(solution)/shard_map/all_to_all | solution.py:487
  45.3 18.8 %copy-start.1 = (f32[41,41]{1,0:T(8,128)S(1)}, f32[41,41]{1,0:T(8,128)}, u32[]{:S(2)}) copy-start(f32[41,41]{1,0:T(8,128)} %scale_ref.1) | copy-start | bytes 20176
  60.1 14.9 %all-to-all-start.2 = ((f32[128,1,384]{2,1,0:T(1,128)}), f32[128,1,384]{2,1,0:T(1,128)S(1)}, u32[]{:S(2)}, u32[]{:S(2)}) async-start(f32[128,1,384]{2,1,0:T(1,128)} %bitcast.31), calls=%async_computation.2 | async-start | bytes 393216 | tf_op jit(solution)/shard_map/all_to_all | solution.py:487
  64.1 0.8 %copy-start.2 = (f32[128,128]{1,0:T(8,128)S(1)}, f32[128,128]{1,0:T(8,128)}, u32[]{:S(2)}) copy-start(f32[128,128]{1,0:T(8,128)} %get-tuple-element.32.forcing_ref) | copy-start | bytes 196612
